TPU v7x, 32 devices: a whole 2x2x4 slice. The times are simulated.
32 devices in a mesh: dp: 4 (over x, core), row: 2 (over y), col: 4 (over z).
Axes of the slice: x: 2, y: 2, z: 4, core: 2. Of those that a mesh axis runs over, the one named last changes fastest.
Arguments:
- tokens: bfloat16 [8192, 1024], P(('dp', 'col'), 'row'), may hold values from -6 to 6
- segments: int32 [8192], P('dp'), may hold values from 0 to 17, as said below
- triple_weight: bfloat16 [1024, 3, 1024], P('row', None, 'col'), may hold values from -0.25 to 0.25
- pair_bias: bfloat16 [2, 1024], P(None, 'col'), may hold values from -3 to 3
- merge_weight: bfloat16 [1024, 1024], P('col', 'row'), may hold values from -1.5 to 1.5
- merge_bias: bfloat16 [1024], P('row'), may hold values from -2 to 2
- first_gain: bfloat16 [1024], P('row'), may hold values from 0.5 to 1.5
- first_shift: bfloat16 [1024], P('row'), may hold values from -3 to 3
- expand_weight: bfloat16 [1024, 4096], P('row', 'col'), may hold values from -0.1875 to 0.1875
- expand_bias: bfloat16 [4096], P('col'), may hold values from -3 to 3
- shrink_weight: bfloat16 [4096, 1024], P('col', 'row'), may hold values from -0.09375 to 0.09375
- shrink_bias: bfloat16 [1024], P('row'), may hold values from -2 to 2
- second_gain: bfloat16 [1024], P('row'), may hold values from 0.5 to 1.5
- second_shift: bfloat16 [1024], P('row'), may hold values from -3 to 3
- cotangent: bfloat16 [8192, 1024], P(('dp', 'col'), 'row'), may hold values from -6 to 6
Outputs:
- layer_out: bfloat16 [8192, 1024], P(('dp', 'col'), 'row')
- grad_tokens: float32 [8192, 1024], P(('dp', 'col'), 'row')
- grad_triple: float32 [1024, 3, 1024], P('row', None, 'col')
- grad_pair: float32 [2, 1024], P(None, 'col')
- grad_merge: float32 [1024, 1024], P('col', 'row')
- grad_merge_bias: float32 [1024], P('row')
- grad_first_gain: float32 [1024], P('row')
- grad_first_shift: float32 [1024], P('row')
- grad_expand: float32 [1024, 4096], P('row', 'col')
- grad_expand_bias: float32 [4096], P('col')
- grad_shrink: float32 [4096, 1024], P('col', 'row')
- grad_shrink_bias: float32 [1024], P('row')
- grad_second_gain: float32 [1024], P('row')
- grad_second_shift: float32 [1024], P('row')
Inputs may be any that keep to these rules, and one draw needn't show every extreme that they name: `segments`: within each sequence of 1024 consecutive tokens the numbers are 1, 2, 3, ... over whole documents of 60 to 800 tokens, followed by 0 on a trailing pad of fewer than 800 tokens; some document holds exactly 800 tokens.
All inputs are finite; a program needn't handle non-finite values.
Results may differ from a plain program's by a relative error of at most 0.017.
The roundings to bfloat16 on the way count: a program that leaves them out, or rounds other values in their place, can miss the bound.
Values may be sent and summed in bfloat16 or wider, within the bound.
No kernel may reach another device: no remote copies, remote signals or barrier semaphores. Data moves between devices by JAX's collectives and lax.ppermute only.
A program may use at most 192 MiB of HBM per device.

v0:
```python
import jax
import jax.numpy as jnp
from jax import lax
from jax.sharding import PartitionSpec as P

D = 1024
HEAD = 64
LEN = 1024


epsilon = 1e-05
masked_score = -1e30
forward_dims = ((1,), (0,))
backward_dims = ((1,), (1,))


def gather_cols(values):
    return lax.all_gather(values, "col", axis=0, tiled=True)


def gather_rows(values):
    return lax.all_gather(values, "row", axis=0, tiled=True)


def reduce_rows(gathered, matrix, dims):
    share = gathered.shape[0] // lax.axis_size("row")

    def partial_rows(begin, length):
        return lax.dot_general(
            gathered, matrix, (dims, ((), ())), preferred_element_type=jnp.float32
        )

    return lax.psum_scatter(
        partial_rows(jnp.int32(0), lax.axis_size("row") * share),
        "row",
        scatter_dimension=0,
        tiled=True,
    )


def reduce_cols(gathered, matrix, dims):
    share = gathered.shape[0] // lax.axis_size("col")

    def partial_rows(begin, length):
        return lax.dot_general(
            gathered, matrix, (dims, ((), ())), preferred_element_type=jnp.float32
        )

    return lax.psum_scatter(
        partial_rows(jnp.int32(0), lax.axis_size("col") * share),
        "col",
        scatter_dimension=0,
        tiled=True,
    )


def col_then_row(flat, matrix):
    gathered = gather_cols(flat)
    result = reduce_rows(gathered, matrix, forward_dims)
    return (gathered, result)


def row_then_col(flat, matrix):
    gathered = gather_rows(flat)
    result = reduce_cols(gathered, matrix, forward_dims)
    return (gathered, result)


def weight_grad(inputs, grads):
    return lax.dot_general(
        inputs, grads, (((0,), (0,)), ((), ())), preferred_element_type=jnp.float32
    )


def back_through_shrink(grad_local, kept_in, matrix):
    gathered = gather_cols(grad_local)
    backward = reduce_rows(gathered, matrix, backward_dims)
    return (backward, weight_grad(kept_in, gathered), jnp.sum(gathered, axis=0, dtype=jnp.float32))


def back_through_expand(grad_attend, kept_in, matrix):
    gathered = gather_rows(grad_attend)
    backward = reduce_cols(gathered, matrix, backward_dims)
    return (backward, weight_grad(kept_in, gathered), jnp.sum(gathered, axis=0, dtype=jnp.float32))


def row_sums(first, second):
    return lax.psum((first, second), "row")


def norm_forward(values, gain_row, shift_row):
    sums = row_sums(jnp.sum(values, axis=1), jnp.sum(values * values, axis=1))
    center = sums[0] / D
    inverse = lax.rsqrt(sums[1] / D - center * center + epsilon)
    scaled = (values - center[:, None]) * inverse[:, None]
    return (scaled, inverse, scaled * gain_row + shift_row)


def norm_backward(upstream, scaled, inverse, gain_row):
    through = upstream * gain_row
    sums = row_sums(jnp.sum(through, axis=1), jnp.sum(through * scaled, axis=1))
    grad_input = inverse[:, None] * (through - sums[0][:, None] / D - scaled * sums[1][:, None] / D)
    return (grad_input, jnp.sum(upstream * scaled, axis=0), jnp.sum(upstream, axis=0))


def masked_scores(query_seq, key_seq, segment_seq):
    scores = jnp.einsum(
        "qhd,khd->hqk", query_seq, key_seq, preferred_element_type=jnp.float32
    ) * HEAD ** (-0.5)
    same_doc = segment_seq[:, None] == segment_seq[None, :]
    return jnp.where(same_doc[None], scores, masked_score)


def attention_forward(queries, key_rows, value_rows, segment, head_count):
    seq_count = queries.shape[0] // LEN
    head_shape = (seq_count, LEN, head_count, HEAD)

    def one_sequence(inputs):
        query_seq, key_seq, value_seq, segment_seq = inputs
        scores = masked_scores(query_seq, key_seq, segment_seq)
        row_max = jnp.max(scores, axis=-1, keepdims=True)
        weights = jnp.exp(scores - row_max)
        row_total = jnp.sum(weights, axis=-1, keepdims=True)
        weights_low = (weights / row_total).astype(jnp.bfloat16)
        attended = jnp.einsum(
            "hqk,khd->qhd", weights_low, value_seq, preferred_element_type=jnp.float32
        )
        return (attended.astype(jnp.bfloat16), (row_max + jnp.log(row_total))[..., 0])

    attended, log_total = lax.map(
        one_sequence,
        (
            queries.reshape(head_shape),
            key_rows.reshape(head_shape),
            value_rows.reshape(head_shape),
            segment.reshape(seq_count, LEN),
        ),
    )
    return (attended.reshape(queries.shape[0], head_count * HEAD), log_total)


def attention_backward(
    queries, key_rows, value_rows, segment, log_total, grad_attended, head_count
):
    seq_count = queries.shape[0] // LEN
    head_shape = (seq_count, LEN, head_count, HEAD)
    score_scale = HEAD ** (-0.5)

    def one_sequence(inputs):
        query_seq, key_seq, value_seq, segment_seq, total_seq, grad_seq = inputs
        scores = masked_scores(query_seq, key_seq, segment_seq)
        weights = jnp.exp(scores - total_seq[..., None])
        grad_weights = jnp.einsum(
            "qhd,khd->hqk", grad_seq, value_seq, preferred_element_type=jnp.float32
        )
        inner_sum = jnp.sum(weights * grad_weights, axis=-1, keepdims=True)
        grad_scores = (weights * (grad_weights - inner_sum)).astype(jnp.bfloat16)
        grad_query = (
            jnp.einsum("hqk,khd->qhd", grad_scores, key_seq, preferred_element_type=jnp.float32)
            * score_scale
        )
        grad_key = (
            jnp.einsum("hqk,qhd->khd", grad_scores, query_seq, preferred_element_type=jnp.float32)
            * score_scale
        )
        grad_value = jnp.einsum(
            "hqk,qhd->khd",
            weights.astype(jnp.bfloat16),
            grad_seq,
            preferred_element_type=jnp.float32,
        )
        return (
            grad_query.astype(jnp.bfloat16),
            grad_key.astype(jnp.bfloat16),
            grad_value.astype(jnp.bfloat16),
        )

    gradients = lax.map(
        one_sequence,
        (
            queries.reshape(head_shape),
            key_rows.reshape(head_shape),
            value_rows.reshape(head_shape),
            segment.reshape(seq_count, LEN),
            log_total,
            grad_attended.reshape(head_shape),
        ),
    )
    flat_shape = (queries.shape[0], head_count * HEAD)
    return tuple((member.reshape(flat_shape) for member in gradients))


def exact_gelu(values):
    return jax.nn.gelu(values, approximate=False)


def shards(
    tokens,
    segments,
    triple_weight,
    pair_bias,
    merge_weight,
    merge_bias,
    first_gain,
    first_shift,
    expand_weight,
    expand_bias,
    shrink_weight,
    shrink_bias,
    second_gain,
    second_shift,
    cotangent,
):
    local_rows = tokens.shape[0]
    attend_rows = segments.shape[0] // lax.axis_size("row")
    seg_attend = lax.dynamic_slice_in_dim(
        segments, lax.axis_index("row") * attend_rows, attend_rows
    )
    seg_local = lax.dynamic_slice_in_dim(segments, lax.axis_index("col") * local_rows, local_rows)
    width = triple_weight.shape[2]
    head_count = width // HEAD
    triple_flat = triple_weight.reshape(triple_weight.shape[0], 3 * width)

    def run_forward(entry):
        x_gathered, projected = col_then_row(entry, triple_flat)
        projected = projected.reshape(attend_rows, 3, width)
        queries = (projected[:, 0] + pair_bias[0]).astype(jnp.bfloat16)
        key_rows = projected[:, 1].astype(jnp.bfloat16)
        value_rows = (projected[:, 2] + pair_bias[1]).astype(jnp.bfloat16)
        attended, log_total = attention_forward(
            queries, key_rows, value_rows, seg_attend, head_count
        )
        mixed_gathered, branch = row_then_col(attended, merge_weight)
        residual = entry.astype(jnp.float32) + (branch + merge_bias)
        scaled_one, inverse_one, normed_one = norm_forward(residual, first_gain, first_shift)
        y_gathered, pre_gelu = col_then_row(normed_one.astype(jnp.bfloat16), expand_weight)
        pre_gelu = pre_gelu + expand_bias
        hidden = exact_gelu(pre_gelu).astype(jnp.bfloat16)
        hidden_gathered, shrunk = row_then_col(hidden, shrink_weight)
        scaled_two, inverse_two, final = norm_forward(
            normed_one + (shrunk + shrink_bias), second_gain, second_shift
        )
        return (
            x_gathered,
            queries,
            key_rows,
            value_rows,
            log_total,
            mixed_gathered,
            scaled_one,
            inverse_one,
            y_gathered,
            pre_gelu,
            hidden_gathered,
            scaled_two,
            inverse_two,
            final,
        )

    kept = run_forward(tokens)
    layer_out = kept[13].astype(jnp.bfloat16)
    fenced = lax.optimization_barrier((tokens, kept[13]))
    kept = run_forward(fenced[0])
    (
        x_gathered,
        queries,
        key_rows,
        value_rows,
        log_total,
        mixed_gathered,
        scaled_one,
        inverse_one,
        y_gathered,
        pre_gelu,
        hidden_gathered,
        scaled_two,
        inverse_two,
        final,
    ) = kept
    live_mask = (seg_local != 0).astype(jnp.float32)[:, None]
    upstream = cotangent.astype(jnp.float32) * live_mask
    grad_sum_two, grad_gain_two, grad_shift_two = norm_backward(
        upstream, scaled_two, inverse_two, second_gain
    )
    grad_hidden, grad_shrink, grad_shrink_bias = back_through_shrink(
        grad_sum_two.astype(jnp.bfloat16), hidden_gathered, shrink_weight
    )
    gelu_pull = jax.vjp(exact_gelu, pre_gelu)[1]
    grad_pre = gelu_pull(grad_hidden)[0].astype(jnp.bfloat16)
    grad_normed, grad_expand, grad_expand_bias = back_through_expand(
        grad_pre, y_gathered, expand_weight
    )
    grad_res, grad_gain_one, grad_shift_one = norm_backward(
        grad_sum_two + grad_normed, scaled_one, inverse_one, first_gain
    )
    grad_mixed, grad_merge, grad_merge_bias = back_through_shrink(
        grad_res.astype(jnp.bfloat16), mixed_gathered, merge_weight
    )
    grad_query, grad_key, grad_value = attention_backward(
        queries,
        key_rows,
        value_rows,
        seg_attend,
        log_total,
        grad_mixed.astype(jnp.bfloat16),
        head_count,
    )
    grad_wide = jnp.stack((grad_query, grad_key, grad_value), axis=1).reshape(
        attend_rows, 3 * width
    )
    grad_entry, grad_triple, grad_triple_bias = back_through_expand(
        grad_wide, x_gathered, triple_flat
    )
    grad_tokens = grad_res + grad_entry
    bias_rows = grad_triple_bias.reshape(3, width)
    pair_grad = jnp.stack((bias_rows[0], bias_rows[2]))
    norm_totals = lax.psum(
        (grad_gain_one, grad_shift_one, grad_gain_two, grad_shift_two), ("dp", "col")
    )
    totals = (
        lax.psum(
            grad_triple.reshape(grad_triple.shape[0], 3, width).astype(jnp.bfloat16), "dp"
        ).astype(jnp.float32),
        lax.psum(pair_grad.astype(jnp.bfloat16), "dp").astype(jnp.float32),
        lax.psum(grad_merge.astype(jnp.bfloat16), "dp").astype(jnp.float32),
        lax.psum(grad_merge_bias.astype(jnp.bfloat16), "dp").astype(jnp.float32),
        lax.psum(grad_expand.astype(jnp.bfloat16), "dp").astype(jnp.float32),
        lax.psum(grad_expand_bias.astype(jnp.bfloat16), "dp").astype(jnp.float32),
        lax.psum(grad_shrink.astype(jnp.bfloat16), "dp").astype(jnp.float32),
        lax.psum(grad_shrink_bias.astype(jnp.bfloat16), "dp").astype(jnp.float32),
    )
    return (
        layer_out,
        grad_tokens,
        totals[0],
        totals[1],
        totals[2],
        totals[3],
        norm_totals[0],
        norm_totals[1],
        totals[4],
        totals[5],
        totals[6],
        totals[7],
        norm_totals[2],
        norm_totals[3],
    )


def solution(mesh):
    placed = (
        P(("dp", "col"), "row"),
        P("dp"),
        P("row", None, "col"),
        P(None, "col"),
        P("col", "row"),
        P("row"),
        P("row"),
        P("row"),
        P("row", "col"),
        P("col"),
        P("col", "row"),
        P("row"),
        P("row"),
        P("row"),
        P(("dp", "col"), "row"),
    )
    return jax.shard_map(
        shards,
        mesh=mesh,
        in_specs=placed,
        out_specs=(
            P(("dp", "col"), "row"),
            P(("dp", "col"), "row"),
            P("row", None, "col"),
            P(None, "col"),
            P("col", "row"),
            P("row"),
            P("row"),
            P("row"),
            P("row", "col"),
            P("col"),
            P("col", "row"),
            P("row"),
            P("row"),
            P("row"),
        ),
        check_vma=False,
    )
```

profile of v0, /device:TPU:0, one launch (start us, length us, event | category | flops | bytes accessed | tf_op | source)
XLA Modules:
  0.0 1825.4 jit_solution(1170940338350591646)
XLA Ops:
  9.4 48.9 %all-gather.13.cloned.1.call-done = bf16[2048,512]{1,0:T(8,128)(2,1)} async-done(((bf16[512,512]{1,0:T(8,128)(2,1)}), bf16[2048,512]{1,0:T(8,128)(2,1)}) %all-gather.13.cloned.1.call-update) | async-done | bytes 2097168 | tf_op jit(solution)/shard_map/all_gather | solution.py:18
  65.9 74.4 %reduce-scatter.13.cloned.1.call-done = f32[1024,768]{1,0:T(8,128)} async-done(((f32[2048,768]{1,0:T(8,128)}), f32[1024,768]{1,0:T(8,128)}) %reduce-scatter.13.cloned.1.call-update) | async-done | bytes 3145744 | tf_op jit(solution)/shard_map/reduce_scatter | solution.py:33
  148.3 11.0 fusion.58
  159.2 8.6 fusion.36
  167.9 21.4 %all-gather.15.cloned.1.call-done = bf16[2048,256]{0,1:T(8,128)(2,1)} async-done(((bf16[1024,256]{0,1:T(8,128)(2,1)}), bf16[2048,256]{0,1:T(8,128)(2,1)}) %all-gather.15.cloned.1.call-update) | async-done | bytes 1048592 | tf_op jit(solution)/shard_map/all_gather | solution.py:22
  193.9 76.2 %reduce-scatter.15.cloned.1.call-done = f32[512,512]{1,0:T(8,128)} async-done(((f32[2048,512]{1,0:T(8,128)}), f32[512,512]{1,0:T(8,128)}) %reduce-scatter.15.cloned.1.call-update) | async-done | bytes 1048592 | tf_op jit(solution)/shard_map/reduce_scatter | solution.py:49
  279.0 46.6 %all-gather.17.cloned.1.call-done = bf16[2048,512]{1,0:T(8,128)(2,1)} async-done(((bf16[512,512]{1,0:T(8,128)(2,1)}), bf16[2048,512]{1,0:T(8,128)(2,1)}) %all-gather.17.cloned.1.call-update) | async-done | bytes 2097168 | tf_op jit(solution)/shard_map/all_gather | solution.py:18
  333.4 97.5 %reduce-scatter.17.cloned.1.call-done = f32[1024,1024]{1,0:T(8,128)} async-done(((f32[2048,1024]{1,0:T(8,128)}), f32[1024,1024]{1,0:T(8,128)}) %reduce-scatter.17.cloned.1.call-update) | async-done | bytes 4194320 | tf_op jit(solution)/shard_map/reduce_scatter | solution.py:33
  430.9 11.3 fusion.14
  442.3 56.9 %all-gather.19.cloned.1.call-done = bf16[2048,1024]{1,0:T(8,128)(2,1)} async-done(((bf16[1024,1024]{1,0:T(8,128)(2,1)}), bf16[2048,1024]{1,0:T(8,128)(2,1)}) %all-gather.19.cloned.1.call-update) | async-done | bytes 4194320 | tf_op jit(solution)/shard_map/all_gather | solution.py:22
  506.3 76.2 %reduce-scatter.19.cloned.1.call-done = f32[512,512]{1,0:T(8,128)} async-done(((f32[2048,512]{1,0:T(8,128)}), f32[512,512]{1,0:T(8,128)}) %reduce-scatter.19.cloned.1.call-update) | async-done | bytes 1048592 | tf_op jit(solution)/shard_map/reduce_scatter | solution.py:49
  592.4 46.6 %all-gather.21.cloned.1.call-done = bf16[2048,512]{1,0:T(8,128)(2,1)} async-done(((bf16[512,512]{1,0:T(8,128)(2,1)}), bf16[2048,512]{1,0:T(8,128)(2,1)}) %all-gather.21.cloned.1.call-update) | async-done | bytes 2097168 | tf_op jit(solution)/shard_map/all_gather | solution.py:18
  645.6 75.5 %reduce-scatter.21.cloned.1.call-done = f32[1024,768]{1,0:T(8,128)} async-done(((f32[2048,768]{1,0:T(8,128)}), f32[1024,768]{1,0:T(8,128)}) %reduce-scatter.21.cloned.1.call-update) | async-done | bytes 3145744 | tf_op jit(solution)/shard_map/reduce_scatter | solution.py:33
  751.7 21.4 %all-gather.23.cloned.1.call-done = bf16[2048,256]{0,1:T(8,128)(2,1)} async-done(((bf16[1024,256]{0,1:T(8,128)(2,1)}), bf16[2048,256]{0,1:T(8,128)(2,1)}) %all-gather.23.cloned.1.call-update) | async-done | bytes 1048592 | tf_op jit(solution)/shard_map/all_gather | solution.py:22
  777.1 76.9 %reduce-scatter.23.cloned.1.call-done = f32[512,512]{1,0:T(8,128)} async-done(((f32[2048,512]{1,0:T(8,128)}), f32[512,512]{1,0:T(8,128)}) %reduce-scatter.23.cloned.1.call-update) | async-done | bytes 1048592 | tf_op jit(solution)/shard_map/reduce_scatter | solution.py:49
  861.6 46.6 %all-gather.25.cloned.1.call-done = bf16[2048,512]{1,0:T(8,128)(2,1)} async-done(((bf16[512,512]{1,0:T(8,128)(2,1)}), bf16[2048,512]{1,0:T(8,128)(2,1)}) %all-gather.25.cloned.1.call-update) | async-done | bytes 2097168 | tf_op jit(solution)/shard_map/all_gather | solution.py:18
  915.6 97.9 %reduce-scatter.25.cloned.1.call-done = f32[1024,1024]{1,0:T(8,128)} async-done(((f32[2048,1024]{1,0:T(8,128)}), f32[1024,1024]{1,0:T(8,128)}) %reduce-scatter.25.cloned.1.call-update) | async-done | bytes 4194320 | tf_op jit(solution)/shard_map/reduce_scatter | solution.py:33
  1013.5 11.6 multiply_convert_fusion.1
  1025.2 56.9 %all-gather.27.cloned.1.call-done = bf16[2048,1024]{1,0:T(8,128)(2,1)} async-done(((bf16[1024,1024]{1,0:T(8,128)(2,1)}), bf16[2048,1024]{1,0:T(8,128)(2,1)}) %all-gather.27.cloned.1.call-update) | async-done | bytes 4194320 | tf_op jit(solution)/shard_map/all_gather | solution.py:22
  1088.7 76.8 %reduce-scatter.27.cloned.1.call-done = f32[512,512]{1,0:T(8,128)} async-done(((f32[2048,512]{1,0:T(8,128)}), f32[512,512]{1,0:T(8,128)}) %reduce-scatter.27.cloned.1.call-update) | async-done | bytes 1048592 | tf_op jit(solution)/shard_map/reduce_scatter | solution.py:49
  1181.7 46.6 %all-gather.29.cloned.1.call-done = bf16[2048,512]{1,0:T(8,128)(2,1)} async-done(((bf16[512,512]{1,0:T(8,128)(2,1)}), bf16[2048,512]{1,0:T(8,128)(2,1)}) %all-gather.29.cloned.1.call-update) | async-done | bytes 2097168 | tf_op jit(solution)/shard_map/all_gather | solution.py:18
  1235.8 98.1 %reduce-scatter.29.cloned.1.call-done = f32[1024,1024]{1,0:T(8,128)} async-done(((f32[2048,1024]{1,0:T(8,128)}), f32[1024,1024]{1,0:T(8,128)}) %reduce-scatter.29.cloned.1.call-update) | async-done | bytes 4194320 | tf_op jit(solution)/shard_map/reduce_scatter | solution.py:33
  1340.5 56.9 %all-gather.31.cloned.1.call-done = bf16[2048,1024]{1,0:T(8,128)(2,1)} async-done(((bf16[1024,1024]{1,0:T(8,128)(2,1)}), bf16[2048,1024]{1,0:T(8,128)(2,1)}) %all-gather.31.cloned.1.call-update) | async-done | bytes 4194320 | tf_op jit(solution)/shard_map/all_gather | solution.py:22
  1404.2 76.7 %reduce-scatter.31.cloned.1.call-done = f32[512,512]{1,0:T(8,128)} async-done(((f32[2048,512]{1,0:T(8,128)}), f32[512,512]{1,0:T(8,128)}) %reduce-scatter.31.cloned.1.call-update) | async-done | bytes 1048592 | tf_op jit(solution)/shard_map/reduce_scatter | solution.py:49
  1492.1 46.6 %all-gather.33.cloned.1.call-done = bf16[2048,512]{1,0:T(8,128)(2,1)} async-done(((bf16[512,512]{1,0:T(8,128)(2,1)}), bf16[2048,512]{1,0:T(8,128)(2,1)}) %all-gather.33.cloned.1.call-update) | async-done | bytes 2097168 | tf_op jit(solution)/shard_map/all_gather | solution.py:18
  1542.4 30.6 %reduce-scatter.33.cloned.1.call-done = f32[1024,256]{1,0:T(8,128)} async-done(((f32[2048,256]{1,0:T(8,128)}), f32[1024,256]{1,0:T(8,128)}) %reduce-scatter.33.cloned.1.call-update) | async-done | bytes 1048592 | tf_op jit(solution)/shard_map/reduce_scatter | solution.py:33
  1575.3 9.4 fusion.30
  1584.7 15.8 multiply_reduce_fusion
  1625.4 33.9 %all-gather.35.cloned.1.call-done = bf16[2048,768]{0,1:T(8,128)(2,1)} async-done(((bf16[1024,768]{0,1:T(8,128)(2,1)}), bf16[2048,768]{0,1:T(8,128)(2,1)}) %all-gather.35.cloned.1.call-update) | async-done | bytes 3145744 | tf_op jit(solution)/shard_map/all_gather | solution.py:22
  1677.7 35.4 %all-reduce = (f32[512]{0:T(512)}, f32[512]{0:T(512)}, f32[512]{0:T(512)}, f32[512]{0:T(512)}) all-reduce(f32[512]{0:T(512)S(1)} %copy-done.24, f32[512]{0:T(512)S(1)} %copy-done.25, f32[512]{0:T(512)S(1)} %get-tuple-element.101, f32[512]{0:T(512)S(1)} %copy-done.23), channel_id=1, replica_groups=mesh['dp'=4,'row'=2,'col'=4] {'dp','col'}, use_global_device_ids=true, to_apply=%region_48.49 | all-reduce | flops 2048 | bytes 16384 | tf_op jit(solution)/shard_map/psum | solution.py:317
  1724.7 12.1 all-reduce.11.cloned.1.call-done
  1745.8 70.2 %reduce-scatter.35.cloned.1.call-done = f32[512,512]{1,0:T(8,128)} async-done(((f32[2048,512]{1,0:T(8,128)}), f32[512,512]{1,0:T(8,128)}) %reduce-scatter.35.cloned.1.call-update) | async-done | bytes 1048592 | tf_op jit(solution)/shard_map/reduce_scatter | solution.py:49
  (224 shorter events, 239.4 us)
Async XLA Ops:
  7.2 318.4 %copy-start = (bf16[512,1024]{1,0:T(8,128)(2,1)S(1)}, bf16[512,1024]{1,0:T(8,128)(2,1)}, u32[]{:S(2)}) copy-start(bf16[512,1024]{1,0:T(8,128)(2,1)} %param.23) | copy-start | bytes 3145732
  7.2 51.1 %all-gather.13.cloned.1.call-start = ((), (), s32[]{:S(2)}) async-start(), calls=%async_computation.12 | async-start | bytes 2621440 | tf_op jit(solution)/shard_map/all_gather | solution.py:18
  7.9 132.4 %reduce-scatter.13.cloned.1.call-start = ((), (), s32[]{:S(2)}) async-start(), calls=%async_computation.13 | async-start | bytes 9437184 | tf_op jit(solution)/shard_map/reduce_scatter | solution.py:33
  9.4 629.6 %copy-start.7 = (bf16[512,3,256]{0,2,1:T(8,128)(2,1)}, bf16[512,3,256]{0,2,1:T(8,128)(2,1)S(1)}, u32[]{:S(2)}) copy-start(bf16[512,3,256]{0,2,1:T(8,128)(2,1)S(1)} %copy.43) | copy-start | bytes 2359300
  64.4 124.9 %all-gather.15.cloned.1.call-start = ((), (), s32[]{:S(2)}) async-start(), calls=%async_computation.14 | async-start | bytes 1572864 | tf_op jit(solution)/shard_map/all_gather | solution.py:22
  65.9 82.4 %copy-start.12 = (pred[1024,1024]{0,1:T(8,128)(4,1)}, pred[1024,1024]{0,1:T(8,128)(4,1)S(1)}, u32[]{:S(2)}) copy-start(pred[1024,1024]{0,1:T(8,128)(4,1)S(1)} %broadcast_compare_fusion) | copy-start | bytes 3145732
  167.8 102.3 %reduce-scatter.15.cloned.1.call-start = ((), (), s32[]{:S(2)}) async-start(), calls=%async_computation.15 | async-start | bytes 5242880 | tf_op jit(solution)/shard_map/reduce_scatter | solution.py:49
  193.2 76.9 %copy-start.1 = (bf16[512,512]{1,0:T(8,128)(2,1)S(1)}, bf16[512,512]{1,0:T(8,128)(2,1)}, u32[]{:S(2)}) copy-start(bf16[512,512]{1,0:T(8,128)(2,1)} %param.15) | copy-start | bytes 1572868
  193.2 132.4 %all-gather.17.cloned.1.call-start = ((), (), s32[]{:S(2)}) async-start(), calls=%async_computation.16 | async-start | bytes 2621440 | tf_op jit(solution)/shard_map/all_gather | solution.py:18
  279.0 151.9 %reduce-scatter.17.cloned.1.call-start = ((), (), s32[]{:S(2)}) async-start(), calls=%async_computation.17 | async-start | bytes 12582912 | tf_op jit(solution)/shard_map/reduce_scatter | solution.py:33
  332.8 166.4 %all-gather.19.cloned.1.call-start = ((), (), s32[]{:S(2)}) async-start(), calls=%async_computation.18 | async-start | bytes 6291456 | tf_op jit(solution)/shard_map/all_gather | solution.py:22
  333.4 165.7 %copy-start.36 = (bf16[1024,512]{1,0:T(8,128)(2,1)S(1)}, bf16[1024,512]{1,0:T(8,128)(2,1)}, u32[]{:S(2)}) copy-start(bf16[1024,512]{1,0:T(8,128)(2,1)} %param.25) | copy-start | bytes 3145732
  442.2 140.3 %reduce-scatter.19.cloned.1.call-start = ((), (), s32[]{:S(2)}) async-start(), calls=%async_computation.19 | async-start | bytes 5242880 | tf_op jit(solution)/shard_map/reduce_scatter | solution.py:49
  505.7 133.4 %all-gather.21.cloned.1.call-start = ((), (), s32[]{:S(2)}) async-start(), calls=%async_computation.20 | async-start | bytes 2621440 | tf_op jit(solution)/shard_map/all_gather | solution.py:18
  592.4 128.7 %reduce-scatter.21.cloned.1.call-start = ((), (), s32[]{:S(2)}) async-start(), calls=%async_computation.21 | async-start | bytes 9437184 | tf_op jit(solution)/shard_map/reduce_scatter | solution.py:33
  645.1 128.0 %all-gather.23.cloned.1.call-start = ((), (), s32[]{:S(2)}) async-start(), calls=%async_computation.22 | async-start | bytes 1572864 | tf_op jit(solution)/shard_map/all_gather | solution.py:22
  751.7 102.3 %reduce-scatter.23.cloned.1.call-start = ((), (), s32[]{:S(2)}) async-start(), calls=%async_computation.23 | async-start | bytes 5242880 | tf_op jit(solution)/shard_map/reduce_scatter | solution.py:49
  777.1 131.1 %all-gather.25.cloned.1.call-start = ((), (), s32[]{:S(2)}) async-start(), calls=%async_computation.24 | async-start | bytes 2621440 | tf_op jit(solution)/shard_map/all_gather | solution.py:18
  861.5 151.9 %reduce-scatter.25.cloned.1.call-start = ((), (), s32[]{:S(2)}) async-start(), calls=%async_computation.25 | async-start | bytes 12582912 | tf_op jit(solution)/shard_map/reduce_scatter | solution.py:33
  915.3 166.7 %copy-start.37 = (bf16[1024,512]{1,0:T(8,128)(2,1)S(1)}, bf16[1024,512]{1,0:T(8,128)(2,1)}, u32[]{:S(2)}) copy-start(bf16[1024,512]{1,0:T(8,128)(2,1)} %param.25) | copy-start | bytes 3145732
  915.4 166.7 %all-gather.27.cloned.1.call-start = ((), (), s32[]{:S(2)}) async-start(), calls=%async_computation.26 | async-start | bytes 6291456 | tf_op jit(solution)/shard_map/all_gather | solution.py:22
  1025.1 140.4 %reduce-scatter.27.cloned.1.call-start = ((), (), s32[]{:S(2)}) async-start(), calls=%async_computation.27 | async-start | bytes 5242880 | tf_op jit(solution)/shard_map/reduce_scatter | solution.py:49
  1088.6 139.7 %all-gather.29.cloned.1.call-start = ((), (), s32[]{:S(2)}) async-start(), calls=%async_computation.28 | async-start | bytes 2621440 | tf_op jit(solution)/shard_map/all_gather | solution.py:18
  1181.7 152.2 %reduce-scatter.29.cloned.1.call-start = ((), (), s32[]{:S(2)}) async-start(), calls=%async_computation.29 | async-start | bytes 12582912 | tf_op jit(solution)/shard_map/reduce_scatter | solution.py:33
  1235.8 161.6 %all-gather.31.cloned.1.call-start = ((), (), s32[]{:S(2)}) async-start(), calls=%async_computation.30 | async-start | bytes 6291456 | tf_op jit(solution)/shard_map/all_gather | solution.py:22
  1340.5 140.4 %reduce-scatter.31.cloned.1.call-start = ((), (), s32[]{:S(2)}) async-start(), calls=%async_computation.31 | async-start | bytes 5242880 | tf_op jit(solution)/shard_map/reduce_scatter | solution.py:49
  1403.9 134.8 %all-gather.33.cloned.1.call-start = ((), (), s32[]{:S(2)}) async-start(), calls=%async_computation.32 | async-start | bytes 2621440 | tf_op jit(solution)/shard_map/all_gather | solution.py:18
  1492.1 81.0 %reduce-scatter.33.cloned.1.call-start = ((), (), s32[]{:S(2)}) async-start(), calls=%async_computation.33 | async-start | bytes 3145728 | tf_op jit(solution)/shard_map/reduce_scatter | solution.py:33
  1542.4 116.9 %all-gather.35.cloned.1.call-start = ((), (), s32[]{:S(2)}) async-start(), calls=%async_computation.34 | async-start | bytes 4718592 | tf_op jit(solution)/shard_map/all_gather | solution.py:22
  1614.2 122.7 %all-reduce.11.cloned.1.call-start = ((), (), s32[]{:S(2)}) async-start(), calls=%async_computation.36 | async-start | bytes 6291456 | tf_op jit(solution)/shard_map/psum | solution.py:321
  1666.9 149.1 %reduce-scatter.35.cloned.1.call-start = ((), (), s32[]{:S(2)}) async-start(), calls=%async_computation.35 | async-start | bytes 5242880 | tf_op jit(solution)/shard_map/reduce_scatter | solution.py:49
  1738.7 77.3 %copy-start.11 = (f32[512,512]{1,0:T(8,128)S(1)}, f32[512,512]{1,0:T(8,128)}, u32[]{:S(2)}) copy-start(f32[512,512]{1,0:T(8,128)} %get-tuple-element.142) | copy-start | bytes 3145732
  (35 other events, 425.1 us)
Sparse Core Ops, SparseCore 0:
  9.6 48.6 all-gather.12
  64.5 75.7 reduce-scatter.12
  167.9 21.2 all-gather.14
  193.4 76.7 reduce-scatter.14
  279.1 46.4 all-gather.16
  332.9 97.9 reduce-scatter.16
  442.4 56.7 all-gather.18
  505.8 76.7 reduce-scatter.18
  592.5 46.4 all-gather.20
  645.3 75.7 reduce-scatter.20
  751.8 21.2 all-gather.22
  777.2 76.7 reduce-scatter.22
  861.7 46.4 all-gather.24
  915.5 97.9 reduce-scatter.24
  1025.2 56.7 all-gather.26
  1088.7 76.7 reduce-scatter.26
  1181.8 46.4 all-gather.28
  1235.9 97.9 reduce-scatter.28
  1340.6 56.7 all-gather.30
  1404.0 76.7 reduce-scatter.30
  1492.2 46.4 all-gather.32
  1542.5 30.5 reduce-scatter.32
  1614.3 44.9 all-gather.34
  1667.0 69.7 all-reduce.10
  1739.2 76.7 reduce-scatter.34
where the time goes:
time: 1840 us; the launch traced here: 1830 us
  waiting for transfers between devices  1470 us (80%)
  matrix products  151 us (8%)
  other arithmetic  91.3 us (5%)
  blocking collectives  71.4 us (4%)
  local copies, waits for them, and re-layouts  25.1 us (1%)
    reduce_scatter x6, waiting for transfers between devices, reduce_rows(): lax.psum_scatter(partial_rows(jnp.int32(0), lax.axis_size('row') * share)...  474 us
    reduce_scatter x6, waiting for transfers between devices, reduce_cols(): lax.psum_scatter(partial_rows(jnp.int32(0), lax.axis_size('col') * share)...  453 us
    all_gather x6, waiting for transfers between devices, gather_cols(): return lax.all_gather(values, 'col', axis=0, tiled=True)  282 us
    all_gather x6, waiting for transfers between devices, gather_rows(): return lax.all_gather(values, 'row', axis=0, tiled=True)  247 us
    dot_general x12, matrix products, partial_rows(): lax.dot_general(gathered, matrix, (dims, ((), ())), preferred_element_typ...  70.8 us
  transfers between devices with their start and end apart: 25, of which 25 were waited for; matrix products, arithmetic and copies ran while one was open for 2% of the time, Pallas kernels for 0%

commit v1 on v0

v1 whole, which is shorter than its diff:
```python
import jax
import jax.numpy as jnp
from jax import lax
from jax.sharding import Mesh, PartitionSpec as P

D = 1024
HEAD = 64
LEN = 1024
epsilon = 1e-05
masked_score = -1e30
bf16 = jnp.bfloat16
f32 = jnp.float32


def size(axis):
    return lax.axis_size(axis)


def place(axis):
    return lax.axis_index(axis)


def pair(values, axis):
    return lax.ppermute(values, axis, [(0, 1), (1, 0)])


def by_place(bit, own, other, axis):
    return jnp.where(
        bit == 0,
        jnp.concatenate((own, other), axis),
        jnp.concatenate((other, own), axis),
    )


def nt(left, right, kind=f32):
    return lax.dot_general(
        left, right, (((1,), (1,)), ((), ())), preferred_element_type=f32
    ).astype(kind)


def nn(left, right, kind=f32):
    return lax.dot_general(
        left, right, (((1,), (0,)), ((), ())), preferred_element_type=f32
    ).astype(kind)


def tn(left, right, kind=f32):
    return lax.dot_general(
        left, right, (((0,), (0,)), ((), ())), preferred_element_type=f32
    ).astype(kind)


def swap_sequences(values):
    count = size("col")
    perm = []
    for core in range(2):
        for col in range(count):
            half, other = col % 2, col - col % 2
            target = (half, other + core)
            perm.append((core * count + col, target[0] * count + target[1]))
    return lax.ppermute(values, ("core", "col"), perm)


def own_first(values):
    if size("row") != 2:
        return values
    half = values.shape[0] // 2
    return jnp.where(place("row") == 0, values, jnp.roll(values, half, axis=0))


def own_part(values):
    share = values.shape[0] // size("row")
    if size("row") == 2:
        return values[:share]
    return lax.dynamic_slice_in_dim(values, place("row") * share, share)


def gather_features(values):
    if size("row") == 2:
        full = by_place(place("row"), values, pair(values, "row"), 1)
        return own_first(full)
    return lax.all_gather(values, "row", axis=1, tiled=True)


def gather_tokens(values):
    if size("row") == 2:
        return jnp.concatenate((values, pair(values, "row")), 0)
    return lax.all_gather(values, "row", axis=0, tiled=True)


def sum_tokens(partial):
    if size("row") == 2:
        share = partial.shape[0] // 2
        return partial[:share] + pair(partial[share:].astype(bf16), "row").astype(f32)
    return lax.psum_scatter(partial, "row", scatter_dimension=0, tiled=True)


def to_own_tokens(values):
    if size("row") == 2:
        bit = place("row")
        ordered = own_first(values)
        share = values.shape[0] // 2
        return by_place(bit, ordered[:share], pair(ordered[share:], "row"), 1)
    return lax.all_to_all(values, "row", 0, 1, tiled=True)


def to_own_features(values):
    if size("row") == 2:
        bit = place("row")
        half = values.shape[1] // 2
        low, high = values[:, :half], values[:, half:]
        own = jnp.where(bit == 0, low, high)
        other = pair(jnp.where(bit == 0, high, low), "row")
        return by_place(bit, own, other, 0)
    return lax.all_to_all(values, "row", 1, 0, tiled=True)


def three_groups(triple, merge, expand, shrink):
    depth = triple.shape[0]
    heads = triple.transpose(1, 2, 0).reshape(3, 2, 2, 1, HEAD, depth)
    out = merge.reshape(1, 2, 2, 1, HEAD, depth)
    keys_values = jnp.concatenate((heads[1], heads[2]), 3 - 1)
    queries_merge = jnp.concatenate((heads[0], out[0]), 3 - 1)
    attend = jnp.stack((keys_values, queries_merge), 2).reshape(2, 2, 2, 2 * HEAD, depth)
    widen = expand.T.reshape(2, 2, 2, -1, depth)
    narrow = shrink.reshape(2, 2, 2, -1, depth)
    return attend, widen, narrow


def my_quarter(group):
    some = lax.dynamic_index_in_dim(group, place("outer"), 1, keepdims=False)
    return lax.dynamic_index_in_dim(some, place("core"), 1, keepdims=False)


def exchange_rows(quarter):
    bit = place("row")
    mine = jnp.where(bit == 0, quarter[0], quarter[1])
    other = pair(jnp.where(bit == 0, quarter[1], quarter[0]), "row")
    return by_place(bit, mine, other, 1)


def spread(quarter):
    count = size("col")
    parts = [quarter] + [
        lax.ppermute(quarter, "col", [(i, (i + step) % count) for i in range(count)])
        for step in range(1, count)
    ]
    four = jnp.stack(parts)
    eight = jnp.stack((four, pair(four, "outer")))
    return jnp.stack((eight, pair(eight, "core")))


def collect(own, other):
    count = size("col")
    bit = place("row")
    total = own + pair(other.astype(bf16), "core").astype(f32)
    total = total[0] + pair(total[1].astype(bf16), "outer").astype(f32)
    last = total[0]
    for step in range(1, count):
        last = last + lax.ppermute(
            total[step].astype(bf16), "col", [(i, (i - step) % count) for i in range(count)]
        ).astype(f32)
    half = last.shape[1] // 2
    low, high = last[:, :half].astype(bf16), last[:, half:].astype(bf16)
    mine = jnp.where(bit == 0, low, high)
    got = pair(jnp.where(bit == 0, high, low), "row")
    block = jnp.stack((jnp.where(bit == 0, mine, got), jnp.where(bit == 0, got, mine)))
    block = by_place(place("core"), block[:, None], pair(block, "core")[:, None], 1)
    block = by_place(place("outer"), block[:, None], pair(block, "outer")[:, None], 1)
    return block.astype(f32)


def ungroup(attend, widen, narrow):
    depth = attend.shape[-1]
    heads = attend.reshape(4, 2, 2, HEAD, depth)
    keys, values = heads[:, 0, 0], heads[:, 0, 1]
    queries, merge = heads[:, 1, 0], heads[:, 1, 1]
    triple = jnp.stack((queries, keys, values)).reshape(3, 4 * HEAD, depth).transpose(2, 0, 1)
    return (
        triple,
        merge.reshape(4 * HEAD, depth),
        widen.reshape(-1, depth).T,
        narrow.reshape(-1, depth),
    )


def local_order(full, units):
    count = size("col")
    rows = full.reshape(count, 2, 2, 2, units)
    rows = lax.dynamic_index_in_dim(rows, place("row"), 1, keepdims=False)
    rows = jnp.where(place("outer") == 0, rows, rows[:, ::-1])
    rows = jnp.where(place("core") == 0, rows, rows[:, :, ::-1])
    steps = [
        lax.dynamic_index_in_dim(rows, (place("col") - step) % count, 0, keepdims=False)
        for step in range(count)
    ]
    return jnp.stack(steps).transpose(2, 1, 0, 3)


def global_order(local, units):
    count = size("col")
    rows = local.reshape(2, 2, count, units).transpose(2, 1, 0, 3)
    rows = jnp.where(place("core") == 0, rows, rows[:, :, ::-1])
    rows = jnp.where(place("outer") == 0, rows, rows[:, ::-1])
    full = jnp.zeros((count, 2, 2, 2, units), local.dtype)
    for step in range(count):
        full = lax.dynamic_update_slice(
            full,
            rows[step][None, None],
            ((place("col") - step) % count, place("row"), 0, 0, 0),
        )
    return full.reshape(-1)


def masked(scores, query_segment, key_segment):
    same = query_segment[:, None] == key_segment[None, :]
    return jnp.where(same[None], scores, masked_score)


def attention_forward(queries, keys, values, query_segment, key_segment):
    scores = jnp.einsum("qhd,khd->hqk", queries, keys, preferred_element_type=f32)
    scores = masked(scores * HEAD**-0.5, query_segment, key_segment)
    top = jnp.max(scores, axis=-1, keepdims=True)
    weights = jnp.exp(scores - top)
    total = jnp.sum(weights, axis=-1, keepdims=True)
    low = (weights / total).astype(bf16)
    attended = jnp.einsum("hqk,khd->qhd", low, values, preferred_element_type=f32)
    return attended.astype(bf16), top + jnp.log(total)


def attention_backward(queries, keys, values, query_segment, key_segment, lse, grad):
    scores = jnp.einsum("qhd,khd->hqk", queries, keys, preferred_element_type=f32)
    scores = masked(scores * HEAD**-0.5, query_segment, key_segment)
    weights = jnp.exp(scores - lse)
    grad_weights = jnp.einsum("qhd,khd->hqk", grad, values, preferred_element_type=f32)
    inner = jnp.sum(weights * grad_weights, axis=-1, keepdims=True)
    grad_scores = (weights * (grad_weights - inner)).astype(bf16)
    scale = HEAD**-0.5
    grad_queries = jnp.einsum("hqk,khd->qhd", grad_scores, keys, preferred_element_type=f32) * scale
    grad_keys = jnp.einsum("hqk,qhd->khd", grad_scores, queries, preferred_element_type=f32) * scale
    grad_values = jnp.einsum(
        "hqk,qhd->khd", weights.astype(bf16), grad, preferred_element_type=f32
    )
    return grad_queries.astype(bf16), grad_keys, grad_values


def norm_forward(values, gain, shift):
    center = jnp.mean(values, axis=1, keepdims=True)
    inverse = lax.rsqrt(
        jnp.mean(values * values, axis=1, keepdims=True) - center * center + epsilon
    )
    scaled = (values - center) * inverse
    return scaled, inverse, scaled * gain + shift


def norm_backward(upstream, scaled, inverse, gain):
    through = upstream * gain
    grad = inverse * (
        through
        - jnp.mean(through, axis=1, keepdims=True)
        - scaled * jnp.mean(through * scaled, axis=1, keepdims=True)
    )
    return grad, jnp.sum(upstream * scaled, axis=0), jnp.sum(upstream, axis=0)


def exact_gelu(values):
    return jax.nn.gelu(values, approximate=False)


def shards(
    tokens,
    segments,
    triple_weight,
    pair_bias,
    merge_weight,
    merge_bias,
    first_gain,
    first_shift,
    expand_weight,
    expand_bias,
    shrink_weight,
    shrink_bias,
    second_gain,
    second_shift,
    cotangent,
):
    rows, cols = size("row"), size("col")
    count = tokens.shape[0]
    span = LEN // count
    special = rows == 2 and span == 2
    own = count // rows
    heads = D // HEAD // rows
    row, col, core = place("row"), place("col"), place("core")

    packed = jnp.concatenate(
        (
            pair_bias.reshape(-1),
            expand_bias,
            merge_bias,
            first_gain,
            first_shift,
            shrink_bias,
            second_gain,
            second_shift,
        )
    )
    everyone = lax.all_gather(packed, ("row", "col"), axis=0).reshape(rows, cols, -1)
    pair_size, hidden_size, row_size = pair_bias.shape[1], expand_bias.shape[0], merge_bias.shape[0]
    begin = 2 * pair_size + hidden_size
    pair_full = everyone[0, :, : 2 * pair_size].reshape(cols, 2, pair_size)
    query_bias, value_bias = pair_full[:, 0].reshape(-1), pair_full[:, 1].reshape(-1)
    hidden_bias = everyone[0, :, 2 * pair_size : begin].reshape(-1)
    vectors = everyone[:, 0, begin:].reshape(rows, 6, row_size).transpose(1, 0, 2).reshape(6, D)
    vectors = vectors.astype(f32)

    if special:
        half = col % 2
        other = pair(segments.astype(f32), "core").astype(jnp.int32)
        mine = jnp.where(half == core, segments, other)
        sequence = lax.dynamic_slice_in_dim(mine, (col // 2) * LEN, LEN).reshape(2, count)
        query_segment = lax.dynamic_index_in_dim(sequence, core, 0, keepdims=False)
        far_segment = lax.dynamic_index_in_dim(sequence, 1 - core, 0, keepdims=False)
        query_segment = own_first(query_segment)
        key_segment = jnp.concatenate((query_segment, own_first(far_segment)))
        tokens, cotangent = swap_sequences(tokens), swap_sequences(cotangent)
    else:
        query_segment = lax.dynamic_slice_in_dim(segments, col * count, count)
        key_segment = query_segment

    if special:
        groups = [
            spread(exchange_rows(my_quarter(group)))
            for group in three_groups(triple_weight, merge_weight, expand_weight, shrink_weight)
        ]
        attend_group = groups[0]
        first = jnp.where(core == 0, attend_group[0], attend_group[1])
        second = jnp.where(core == 0, attend_group[1], attend_group[0])
        first = first.reshape(heads, 2, HEAD, D)
        second = second.reshape(heads, 2, HEAD, D)
        weight_keys, weight_values = first[:, 0].reshape(-1, D), first[:, 1].reshape(-1, D)
        weight_queries, weight_merge = second[:, 0].reshape(-1, D), second[:, 1].reshape(-1, D)
        weight_expand, weight_shrink = groups[1].reshape(-1, D), groups[2].reshape(-1, D)
        bias_hidden = local_order(hidden_bias, hidden_size // 8).reshape(-1).astype(f32)

        def heads_order(vector):
            blocks = vector.reshape(cols, 2, 2, HEAD)
            blocks = lax.dynamic_index_in_dim(blocks, row, 1, keepdims=False)
            blocks = jnp.where(place("outer") == 0, blocks, blocks[:, ::-1])
            steps = [
                lax.dynamic_index_in_dim(blocks, (col - step) % cols, 0, keepdims=False)
                for step in range(cols)
            ]
            return jnp.stack(steps).transpose(1, 0, 2).reshape(-1)

        bias_queries, bias_values = heads_order(query_bias), heads_order(value_bias)
    else:
        triple = lax.all_gather(triple_weight, "col", axis=2, tiled=True)
        triple = lax.all_gather(triple, "row", axis=0, tiled=True).transpose(1, 2, 0)
        merge = lax.all_gather(merge_weight, "col", axis=0, tiled=True)
        merge = lax.all_gather(merge, "row", axis=1, tiled=True)
        expand = lax.all_gather(expand_weight, "col", axis=1, tiled=True)
        expand = lax.all_gather(expand, "row", axis=0, tiled=True).T
        shrink = lax.all_gather(shrink_weight, "col", axis=0, tiled=True)
        shrink = lax.all_gather(shrink, "row", axis=1, tiled=True)

        def mine_of(full):
            return lax.dynamic_slice_in_dim(full, row * (full.shape[0] // rows), full.shape[0] // rows)

        weight_queries, weight_keys, weight_values = (mine_of(triple[j]) for j in range(3))
        weight_merge, weight_expand, weight_shrink = mine_of(merge), mine_of(expand), mine_of(shrink)
        bias_hidden = mine_of(hidden_bias).astype(f32)
        bias_queries, bias_values = mine_of(query_bias), mine_of(value_bias)

    inputs = gather_features(tokens)
    head_shape = (-1, heads, HEAD)
    queries = (nt(inputs, weight_queries) + bias_queries.astype(f32)).astype(bf16)
    keys = nt(inputs, weight_keys).astype(bf16)
    values = (nt(inputs, weight_values) + bias_values.astype(f32)).astype(bf16)
    if special:
        keys_values = jnp.concatenate((keys, values), 1)
        all_keys_values = jnp.concatenate((keys_values, pair(keys_values, "core")), 0)
        all_keys = all_keys_values[:, : heads * HEAD]
        all_values = all_keys_values[:, heads * HEAD :]
    else:
        all_keys, all_values = keys, values
    queries_heads = queries.reshape(head_shape)
    keys_heads, values_heads = all_keys.reshape(head_shape), all_values.reshape(head_shape)
    attended, lse = attention_forward(
        queries_heads, keys_heads, values_heads, query_segment, key_segment
    )
    attended = attended.reshape(count, -1)
    branch = sum_tokens(nn(attended, weight_merge))
    residual = own_part(inputs).astype(f32) + (branch + vectors[0])
    scaled_one, inverse_one, normed_one = norm_forward(residual, vectors[1], vectors[2])
    normed_low = gather_tokens(normed_one.astype(bf16))
    pre_gelu = nt(normed_low, weight_expand) + bias_hidden
    hidden = exact_gelu(pre_gelu).astype(bf16)
    shrunk = sum_tokens(nn(hidden, weight_shrink))
    scaled_two, inverse_two, final = norm_forward(
        normed_one + (shrunk + vectors[3]), vectors[4], vectors[5]
    )
    layer_out = to_own_features(final.astype(bf16))

    live = (own_part(query_segment) != 0).astype(f32)[:, None]
    upstream = to_own_tokens(cotangent).astype(f32) * live
    grad_sum_two, grad_gain_two, grad_shift_two = norm_backward(
        upstream, scaled_two, inverse_two, vectors[4]
    )
    grad_shrunk_own = grad_sum_two.astype(bf16)
    grad_shrunk = gather_tokens(grad_shrunk_own)
    grad_hidden = nt(grad_shrunk, weight_shrink)
    grad_pre = jax.vjp(exact_gelu, pre_gelu)[1](grad_hidden)[0].astype(bf16)
    grad_normed = grad_sum_two + sum_tokens(nn(grad_pre, weight_expand))
    grad_res, grad_gain_one, grad_shift_one = norm_backward(
        grad_normed, scaled_one, inverse_one, vectors[1]
    )
    grad_branch_own = grad_res.astype(bf16)
    grad_branch = gather_tokens(grad_branch_own)
    grad_attended = nt(grad_branch, weight_merge).astype(bf16)
    grad_queries, grad_keys, grad_values = attention_backward(
        queries_heads,
        keys_heads,
        values_heads,
        query_segment,
        key_segment,
        lse,
        grad_attended.reshape(head_shape),
    )
    grad_queries = grad_queries.reshape(count, -1)
    grad_keys_values = jnp.concatenate(
        (grad_keys.reshape(-1, heads * HEAD), grad_values.reshape(-1, heads * HEAD)), 1
    )
    if special:
        grad_keys_values = grad_keys_values[:count] + pair(grad_keys_values[count:], "core")
    grad_keys_values = grad_keys_values.astype(bf16)
    grad_keys, grad_values = (
        grad_keys_values[:, : heads * HEAD],
        grad_keys_values[:, heads * HEAD :],
    )
    grad_entry = sum_tokens(
        nn(grad_queries, weight_queries)
        + nn(grad_keys, weight_keys)
        + nn(grad_values, weight_values)
    )
    grad_tokens = to_own_features(grad_res + grad_entry)
    if special:
        layer_out, grad_tokens = swap_sequences(layer_out), swap_sequences(grad_tokens)

    if special:
        half = hidden.shape[1] // 2
        units = hidden_size // 8
        narrow = collect(
            tn(hidden[:, :half], grad_shrunk).reshape(2, cols, units, D),
            tn(hidden[:, half:], grad_shrunk).reshape(2, cols, units, D),
        )
        widen = collect(
            tn(grad_pre[:, :half], normed_low).reshape(2, cols, units, D),
            tn(grad_pre[:, half:], normed_low).reshape(2, cols, units, D),
        )
        parts = (heads, HEAD, D)
        first = jnp.stack(
            (tn(grad_keys, inputs).reshape(parts), tn(grad_values, inputs).reshape(parts)), 1
        )
        second = jnp.stack(
            (tn(grad_queries, inputs).reshape(parts), tn(attended, grad_branch).reshape(parts)), 1
        )
        shape = (2, cols, 2 * HEAD, D)
        attend = collect(
            jnp.where(core == 0, first, second).reshape(shape),
            jnp.where(core == 0, second, first).reshape(shape),
        )
        grad_triple, grad_merge, grad_expand, grad_shrink = ungroup(attend, widen, narrow)
    else:

        def assemble(local, row_axis, col_axis):
            full = jnp.zeros((local.shape[0], local.shape[1] * rows, D), bf16)
            full = lax.dynamic_update_slice(
                full, local.astype(bf16), (0, row * local.shape[1], 0)
            )
            full = lax.psum_scatter(full, "row", scatter_dimension=2, tiled=True)
            full = lax.psum_scatter(full, "col", scatter_dimension=1, tiled=True)
            return lax.psum(full, ("outer", "core")).astype(f32)

        grad_triple = assemble(
            jnp.stack(
                (tn(grad_queries, inputs), tn(grad_keys, inputs), tn(grad_values, inputs))
            ),
            0,
            2,
        ).transpose(2, 0, 1)
        grad_merge = assemble(tn(attended, grad_branch)[None], 1, 0)[0]
        grad_expand = assemble(tn(grad_pre, normed_low)[None], 0, 1)[0].T
        grad_shrink = assemble(tn(hidden, grad_shrunk)[None], 1, 0)[0]

    def column_sums(values):
        return jnp.sum(values, axis=0, dtype=f32)

    sum_hidden = column_sums(grad_pre)
    sum_queries, sum_values = column_sums(grad_queries), column_sums(grad_values)
    if special:
        sum_hidden = global_order(sum_hidden, hidden_size // 8)

        def heads_back(local):
            blocks = local.reshape(2, cols, HEAD).transpose(1, 0, 2)
            blocks = jnp.where(place("outer") == 0, blocks, blocks[:, ::-1])
            full = jnp.zeros((cols, 2, 2, HEAD), f32)
            for step in range(cols):
                full = lax.dynamic_update_slice(
                    full, blocks[step][None, None], ((col - step) % cols, row, 0, 0)
                )
            return full.reshape(-1)

        sum_queries, sum_values = heads_back(sum_queries), heads_back(sum_values)
    else:

        def whole(local):
            full = jnp.zeros(local.shape[0] * rows, f32)
            return lax.dynamic_update_slice(full, local, (row * local.shape[0],))

        sum_hidden, sum_queries, sum_values = (
            whole(sum_hidden),
            whole(sum_queries),
            whole(sum_values),
        )
    sums = lax.psum(
        jnp.concatenate(
            (
                column_sums(grad_branch_own),
                grad_gain_one,
                grad_shift_one,
                column_sums(grad_shrunk_own),
                grad_gain_two,
                grad_shift_two,
                sum_queries,
                sum_values,
                sum_hidden,
            )
        ),
        ("outer", "core", "row", "col"),
    )

    def row_share(index):
        return lax.dynamic_slice_in_dim(sums, index * D + row * row_size, row_size)

    grad_pair = jnp.stack(
        [
            lax.dynamic_slice_in_dim(sums, index * D + col * pair_size, pair_size)
            for index in (6, 7)
        ]
    )
    grad_expand_bias = lax.dynamic_slice_in_dim(sums, 8 * D + col * hidden_size, hidden_size)
    return (
        layer_out,
        grad_tokens,
        grad_triple,
        grad_pair,
        grad_merge,
        row_share(0),
        row_share(1),
        row_share(2),
        grad_expand,
        grad_expand_bias,
        grad_shrink,
        row_share(3),
        row_share(4),
        row_share(5),
    )


def solution(mesh):
    sizes = mesh.shape
    axes = ("outer", "core", "row", "col")
    split = Mesh(
        mesh.devices.reshape(sizes["dp"] // 2, 2, sizes["row"], sizes["col"]), axes
    )
    dp = ("outer", "core")
    activations = P(("outer", "core", "col"), "row")
    return jax.shard_map(
        shards,
        mesh=split,
        in_specs=(
            activations,
            P(dp),
            P("row", None, "col"),
            P(None, "col"),
            P("col", "row"),
            P("row"),
            P("row"),
            P("row"),
            P("row", "col"),
            P("col"),
            P("col", "row"),
            P("row"),
            P("row"),
            P("row"),
            activations,
        ),
        out_specs=(
            activations,
            activations,
            P("row", None, "col"),
            P(None, "col"),
            P("col", "row"),
            P("row"),
            P("row"),
            P("row"),
            P("row", "col"),
            P("col"),
            P("col", "row"),
            P("row"),
            P("row"),
            P("row"),
        ),
        check_vma=False,
    )
```

time: 1840 us -> 612 us (0.33)
  waiting for transfers between devices: 1470 us -> 249 us
  starting transfers between devices: 2.29 us -> 84.8 us
  matrix products: 151 us -> 83.8 us
    reduce_scatter x12 -> x0, waiting for transfers between devices: 927 us -> none  [the longest x6 474 us: reduce_rows(): lax.psum_scatter(partial_rows(jnp.int32(0), lax.axis_size('row') * share)...]
    all_gather x12 -> x0, waiting for transfers between devices: 529 us -> none  [the longest x6 282 us: gather_cols(): return lax.all_gather(values, 'col', axis=0, tiled=True)]
    ppermute x0 -> x60, waiting for transfers between devices: none -> 249 us  [the longest x38 190 us: pair(): return lax.ppermute(values, axis, [(0, 1), (1, 0)])]
    ppermute x0 -> x60, starting transfers between devices: none -> 84.8 us  [the longest x38 27.6 us: pair(): return lax.ppermute(values, axis, [(0, 1), (1, 0)])]
    dot_general x23 -> x26, matrix products: 140 us -> 83.8 us  [the longest x6 27.6 us: nt(): lax.dot_general(left, right, (((1,), (1,)), ((), ())), preferred_element_...]
    convert_element_type x24 -> x12, other arithmetic: 55.8 us -> 16.2 us  [the longest x1 10.5 us: attention_backward(): grad_scores = (weights * (grad_weights - inner)).astype(bf16)]
    all_gather x0 -> x1, blocking collectives: none -> 31.6 us  [shards(): lax.all_gather(packed, ('row', 'col'), axis=0).reshape(rows, cols, -1)]
    psum x8 -> x1, blocking collectives: 71.4 us -> 40 us  [shards(): lax.psum(jnp.concatenate((column_sums(grad_branch_own), grad_gain_one, gr...]
  transfers between devices with their start and end apart: 25 -> 60, of which waited for: 25 -> 23; matrix products, arithmetic and copies ran while one was open for 2% -> 29% of each run, Pallas kernels for 0% -> 0%
where the time goes in v1:
time: 612 us; the launch traced here: 602 us
  waiting for transfers between devices  249 us (41%)
  starting transfers between devices  84.8 us (14%)
  matrix products  83.8 us (14%)
  other arithmetic  78.5 us (13%)
  blocking collectives  71.6 us (12%)
  local copies, waits for them, and re-layouts  31.7 us (5%)
    ppermute x38, waiting for transfers between devices, pair(): return lax.ppermute(values, axis, [(0, 1), (1, 0)])  190 us
    ppermute x9, waiting for transfers between devices, spread(): lax.ppermute(quarter, 'col', [(i, (i + step) % count) for i in range(coun...  41.4 us
    psum x1, blocking collectives, shards(): lax.psum(jnp.concatenate((column_sums(grad_branch_own), grad_gain_one, gr...  40 us
    all_gather x1, blocking collectives, shards(): lax.all_gather(packed, ('row', 'col'), axis=0).reshape(rows, cols, -1)  31.6 us
    dot_general x6, matrix products, nt(): lax.dot_general(left, right, (((1,), (1,)), ((), ())), preferred_element_...  27.6 us
    ppermute x38, starting transfers between devices, pair(): return lax.ppermute(values, axis, [(0, 1), (1, 0)])  27.6 us
    ppermute x9, starting transfers between devices, spread(): lax.ppermute(quarter, 'col', [(i, (i + step) % count) for i in range(coun...  20.9 us
    ppermute x4, starting transfers between devices, swap_sequences(): return lax.ppermute(values, ('core', 'col'), perm)  18.8 us
  transfers between devices with their start and end apart: 60, of which 23 were waited for; matrix products, arithmetic and copies ran while one was open for 29% of the time, Pallas kernels for 0%

profile of v1, /device:TPU:0, one launch (start us, length us, event | category | flops | bytes accessed | tf_op | source)
XLA Modules:
  0.0 602.3 jit_solution(5181047037961305632)
XLA Ops:
  11.3 31.6 %all-gather.1 = bf16[8,1,4608]{2,1,0:T(2,128)(2,1)S(1)} all-gather(bf16[1,1,4608]{2,1,0:T(2,128)(2,1)S(1)} %reshape.770), channel_id=2, replica_groups=mesh['outer'=2,'core'=2,'row'=2,'col'=4] {'row','col'}, dimensions={0}, use_global_device_ids=true | all-gather | bytes 82944 | tf_op jit(solution)/shard_map/all_gather | solution.py:307
  49.9 4.4 collective-permute-done.5
  54.3 8.9 %collective-permute-done.4 = bf16[128,1024]{1,0:T(8,128)(2,1)S(1)} collective-permute-done((bf16[128,1024]{1,0:T(8,128)(2,1)S(1)}, bf16[128,1024]{1,0:T(8,128)(2,1)S(1)}, u32[]{:S(2)}, u32[]{:S(2)}) %collective-permute-start.4) | collective-permute-done | bytes 262176 | tf_op jit(solution)/shard_map/ppermute | solution.py:145
  67.3 19.0 %collective-permute-done.6 = bf16[4,128,1024]{2,1,0:T(8,128)(2,1)S(1)} collective-permute-done((bf16[4,128,1024]{2,1,0:T(8,128)(2,1)}, bf16[4,128,1024]{2,1,0:T(8,128)(2,1)S(1)}, u32[]{:S(2)}, u32[]{:S(2)}) %collective-permute-start.6) | collective-permute-done | bytes 1048608 | tf_op jit(solution)/shard_map/ppermute | solution.py:24
  86.9 4.4 collective-permute-start.14
  99.3 16.0 %collective-permute-done.14 = bf16[128,1024]{1,0:T(8,128)(2,1)S(1)} collective-permute-done((bf16[128,1024]{1,0:T(8,128)(2,1)S(1)}, bf16[128,1024]{1,0:T(8,128)(2,1)S(1)}, u32[]{:S(2)}, u32[]{:S(2)}) %collective-permute-start.14) | collective-permute-done | bytes 262176 | tf_op jit(solution)/shard_map/ppermute | solution.py:145
  115.3 7.0 %collective-permute-start.19 = (bf16[128,1024]{1,0:T(8,128)(2,1)S(1)}, bf16[128,1024]{1,0:T(8,128)(2,1)S(1)}, u32[]{:S(2)}, u32[]{:S(2)}) collective-permute-start(bf16[128,1024]{1,0:T(8,128)(2,1)S(1)} %maximum_select_fusion.20), channel_id=1, source_target_pairs={{0,1},{1,2},{2,3},{3,0},{4,5},{5,6},{6,7},{7,4},{8,9},{9,10},{10,1... | collective-permute-start | bytes 786440 | tf_op jit(solution)/shard_map/ppermute | solution.py:145
  122.7 5.6 collective-permute-start.27
  128.3 9.3 %collective-permute-done.20 = bf16[128,1024]{1,0:T(8,128)(2,1)S(1)} collective-permute-done((bf16[128,1024]{1,0:T(8,128)(2,1)S(1)}, bf16[128,1024]{1,0:T(8,128)(2,1)S(1)}, u32[]{:S(2)}, u32[]{:S(2)}) %collective-permute-start.20) | collective-permute-done | bytes 262176 | tf_op jit(solution)/shard_map/ppermute | solution.py:145
  144.7 19.0 %collective-permute-done.16 = bf16[4,128,1024]{2,1,0:T(8,128)(2,1)S(1)} collective-permute-done((bf16[4,128,1024]{2,1,0:T(8,128)(2,1)S(1)}, bf16[4,128,1024]{2,1,0:T(8,128)(2,1)S(1)}, u32[]{:S(2)}, u32[]{:S(2)}) %collective-permute-start.16) | collective-permute-done | bytes 1048608 | tf_op jit(solution)/shard_map/ppermute | solution.py:24
  166.0 19.0 %collective-permute-done.22 = bf16[4,128,1024]{2,1,0:T(8,128)(2,1)S(1)} collective-permute-done((bf16[4,128,1024]{2,1,0:T(8,128)(2,1)S(1)}, bf16[4,128,1024]{2,1,0:T(8,128)(2,1)S(1)}, u32[]{:S(2)}, u32[]{:S(2)}) %collective-permute-start.22) | collective-permute-done | bytes 1048608 | tf_op jit(solution)/shard_map/ppermute | solution.py:24
  204.6 14.1 %collective-permute-done.10 = bf16[256,1024]{1,0:T(8,128)(2,1)S(1)} collective-permute-done((bf16[256,1024]{1,0:T(8,128)(2,1)S(1)}, bf16[256,1024]{1,0:T(8,128)(2,1)S(1)}, u32[]{:S(2)}, u32[]{:S(2)}) %collective-permute-start.10) | collective-permute-done | bytes 524320 | tf_op jit(solution)/shard_map/ppermute | solution.py:24
  228.2 7.0 %collective-permute-done.11 = bf16[256,1024]{1,0:T(8,128)(2,1)S(1)} collective-permute-done((bf16[256,1024]{1,0:T(8,128)(2,1)S(1)}, bf16[256,1024]{1,0:T(8,128)(2,1)S(1)}, u32[]{:S(2)}, u32[]{:S(2)}) %collective-permute-start.11) | collective-permute-done | bytes 524320 | tf_op jit(solution)/shard_map/ppermute | solution.py:24
  235.2 15.9 %multiply_convert_fusion.1 = (bf16[512,2048]{1,0:T(8,128)(2,1)S(1)}, f32[512,2048]{1,0:T(8,128)}, f32[512,2048]{1,0:T(8,128)}) fusion(f32[2048]{0:T(1024)S(1)} %bitcast.455, bf16[2048,1024]{1,0:T(8,128)(2,1)S(1)} %bitcast.376, bf16[256,1024]{1,0:T(8,128)(2,1)S(1)} %collective-permute-done.11, bf16[256,1024]{1,0:T(8,128)(2,1)S(1)} %fusion.46), kind=kOutput, calls=%fused_computation.25 | convolution fusion | flops 2218786816 | bytes 15736832 | tf_op jit(solution)/shard_map/dot_general | solution.py:36
  257.0 11.5 %collective-permute-done.24 = bf16[256,1024]{1,0:T(8,128)(2,1)S(1)} collective-permute-done((bf16[256,1024]{1,0:T(8,128)(2,1)S(1)}, bf16[256,1024]{1,0:T(8,128)(2,1)S(1)}, u32[]{:S(2)}, u32[]{:S(2)}) %collective-permute-start.24) | collective-permute-done | bytes 524320 | tf_op jit(solution)/shard_map/ppermute | solution.py:24
  276.7 14.9 %collective-permute-done.25 = bf16[256,512]{1,0:T(8,128)(2,1)} collective-permute-done((bf16[256,512]{1,0:T(8,128)(2,1)}, bf16[256,512]{1,0:T(8,128)(2,1)}, u32[]{:S(2)}, u32[]{:S(2)}) %collective-permute-start.25) | collective-permute-done | bytes 262176 | tf_op jit(solution)/shard_map/ppermute | solution.py:24
  295.4 8.8 %convert_reduce_fusion = (f32[2048]{0:T(1024)S(1)}, bf16[512,2048]{1,0:T(8,128)(2,1)S(1)}) fusion(f32[512,2048]{1,0:T(8,128)} %get-tuple-element.81, bf16[2048,1024]{1,0:T(8,128)(2,1)} %bitcast.379, bf16[256,1024]{1,0:T(8,128)(2,1)} %collective-permute-done.29, bf16[256,1024]{1,0:T(8,128)(2,1)} %get-tuple-element.72, f32[512,2048]{1,0:T(8,128)} %get-tuple-element.196, ...), kind=kOutput, calls=%fused_computation.21 | convolution fusion | flops 2167404544 | bytes 15745024 | tf_op jit(solution)/shard_map/dot_general | solution.py:36
  318.2 4.6 fusion.27
  326.9 12.7 %collective-permute-done.31 = bf16[256,1024]{1,0:T(8,128)(2,1)S(1)} collective-permute-done((bf16[256,1024]{1,0:T(8,128)(2,1)S(1)}, bf16[256,1024]{1,0:T(8,128)(2,1)S(1)}, u32[]{:S(2)}, u32[]{:S(2)}) %collective-permute-start.31) | collective-permute-done | bytes 524320 | tf_op jit(solution)/shard_map/ppermute | solution.py:24
  340.5 9.2 %multiply_reduce_fusion = (f32[8,512]{1,0:T(8,128)S(1)}, f32[8,512,1024]{2,1,0:T(8,128)}) fusion(f32[8,512,1024]{2,1,0:T(8,128)S(1)} %bitcast.357, f32[8,512]{1,0:T(8,128)S(1)} %log_add_fusion, bf16[512,8,64]{0,2,1:T(8,128)(2,1)S(1)} %bitcast.397, bf16[1024,8,64]{0,2,1:T(8,128)(2,1)} %bitcast.389), kind=kOutput, calls=%fused_computation.1 | convolution fusion | flops 549449728 | bytes 35160064 | tf_op jit(solution)/shard_map/qhd,khd->hqk/dot_general | solution.py:235
  353.6 10.5 %multiply_convert_fusion = bf16[8,512,1024]{2,1,0:T(8,128)(2,1)} fusion(f32[8,512,1024]{2,1,0:T(8,128)} %get-tuple-element.198, f32[8,512,1024]{2,1,0:T(8,128)S(1)} %bitcast.357, f32[8,512]{1,0:T(8,128)S(1)} %get-tuple-element.197, f32[8,512]{1,0:T(8,128)S(1)} %log_add_fusion), kind=kLoop, calls=%fused_computation | loop fusion | flops 16777216 | bytes 41975808 | tf_op jit(solution)/shard_map/convert_element_type | solution.py:237
  364.1 7.0 %convert_reduce_fusion.2 = (f32[8,64]{1,0:T(8,128)S(1)}, bf16[8,64,512]{2,1,0:T(8,128)(2,1)}) fusion(bf16[1024,8,64]{0,2,1:T(8,128)(2,1)S(1)} %bitcast.370, bf16[8,512,1024]{2,1,0:T(8,128)(2,1)} %multiply_convert_fusion), kind=kOutput, calls=%fused_computation.119 | convolution fusion | flops 537918976 | bytes 9963520 | tf_op jit(solution)/shard_map/hqk,khd->qhd/dot_general | solution.py:239
  388.8 18.1 %collective-permute-done.45 = bf16[4,128,1024]{2,1,0:T(8,128)(2,1)S(1)} collective-permute-done((bf16[4,128,1024]{2,1,0:T(8,128)(2,1)S(1)}, bf16[4,128,1024]{2,1,0:T(8,128)(2,1)S(1)}, u32[]{:S(2)}, u32[]{:S(2)}) %collective-permute-start.45) | collective-permute-done | bytes 1048608 | tf_op jit(solution)/shard_map/ppermute | solution.py:24
  413.5 15.5 %collective-permute-done.53 = bf16[4,128,1024]{2,1,0:T(8,128)(2,1)S(1)} collective-permute-done((bf16[4,128,1024]{2,1,0:T(8,128)(2,1)S(1)}, bf16[4,128,1024]{2,1,0:T(8,128)(2,1)S(1)}, u32[]{:S(2)}, u32[]{:S(2)}) %collective-permute-start.53) | collective-permute-done | bytes 1048608 | tf_op jit(solution)/shard_map/ppermute | solution.py:24
  448.3 40.0 %psum.7 = f32[12288]{0:T(1024)S(1)} all-reduce(f32[12288]{0:T(1024)S(1)} %constant_dynamic-update-slice_fusion.14), channel_id=1, replica_groups=mesh['outer'=2,'core'=2,'row'=2,'col'=4] {'outer','core','row','col'}, use_global_device_ids=true, to_apply=%region_20.21 | all-reduce | flops 12288 | bytes 98304 | tf_op jit(solution)/shard_map/psum | solution.py:525
  497.5 7.3 %collective-permute-done.55 = bf16[128,1024]{1,0:T(8,128)(2,1)S(1)} collective-permute-done((bf16[128,1024]{1,0:T(8,128)(2,1)S(1)}, bf16[128,1024]{1,0:T(8,128)(2,1)S(1)}, u32[]{:S(2)}, u32[]{:S(2)}) %collective-permute-start.55) | collective-permute-done | bytes 262176 | tf_op jit(solution)/shard_map/ppermute | solution.py:160
  517.0 15.1 %collective-permute-done.37 = bf16[4,128,1024]{2,1,0:T(8,128)(2,1)S(1)} collective-permute-done((bf16[4,128,1024]{2,1,0:T(8,128)(2,1)S(1)}, bf16[4,128,1024]{2,1,0:T(8,128)(2,1)S(1)}, u32[]{:S(2)}, u32[]{:S(2)}) %collective-permute-start.37) | collective-permute-done | bytes 1048608 | tf_op jit(solution)/shard_map/ppermute | solution.py:24
  532.7 6.2 %collective-permute-start.40 = (bf16[128,1024]{1,0:T(8,128)(2,1)S(1)}, bf16[128,1024]{1,0:T(8,128)(2,1)S(1)}, u32[]{:S(2)}, u32[]{:S(2)}) collective-permute-start(bf16[128,1024]{1,0:T(8,128)(2,1)S(1)} %get-tuple-element.107), channel_id=1, source_target_pairs={{0,1},{1,2},{2,3},{3,0},{4,5},{5,6},{6,7},{7,4},{8,9},{9,10},{10,1... | collective-permute-start | bytes 786440 | tf_op jit(solution)/shard_map/ppermute | solution.py:160
  548.2 6.7 %collective-permute-done.39 = bf16[128,1024]{1,0:T(8,128)(2,1)S(1)} collective-permute-done((bf16[128,1024]{1,0:T(8,128)(2,1)S(1)}, bf16[128,1024]{1,0:T(8,128)(2,1)S(1)}, u32[]{:S(2)}, u32[]{:S(2)}) %collective-permute-start.39) | collective-permute-done | bytes 262176 | tf_op jit(solution)/shard_map/ppermute | solution.py:160
  557.0 9.6 %collective-permute-start.35 = (f32[512,512]{1,0:T(8,128)}, f32[512,512]{1,0:T(8,128)}, u32[]{:S(2)}, u32[]{:S(2)}) collective-permute-start(f32[512,512]{1,0:T(8,128)} %maximum_select_fusion.2), channel_id=1, source_target_pairs={{0,0},{1,8},{2,2},{3,10},{8,1},{9,9},{10,3},{11,11},{4,4},{5,12},{... | collective-permute-start | bytes 3145736 | tf_op jit(solution)/shard_map/ppermute | solution.py:61
  574.2 9.7 %collective-permute-done.59 = bf16[2,2,128,512]{3,2,0,1:T(8,128)(2,1)} collective-permute-done((bf16[2,2,128,512]{3,2,0,1:T(8,128)(2,1)}, bf16[2,2,128,512]{3,2,0,1:T(8,128)(2,1)}, u32[]{:S(2)}, u32[]{:S(2)}) %collective-permute-start.59) | collective-permute-done | bytes 524320 | tf_op jit(solution)/shard_map/ppermute | solution.py:24
  586.9 7.8 %collective-permute-done.43 = bf16[2,2,128,512]{3,2,0,1:T(8,128)(2,1)} collective-permute-done((bf16[2,2,128,512]{3,2,0,1:T(8,128)(2,1)}, bf16[2,2,128,512]{3,2,0,1:T(8,128)(2,1)}, u32[]{:S(2)}, u32[]{:S(2)}) %collective-permute-start.43) | collective-permute-done | bytes 524320 | tf_op jit(solution)/shard_map/ppermute | solution.py:24
  (454 shorter events, 203.0 us)
Async XLA Ops:
  2.9 83.8 %collective-permute-start.12 = (bf16[128,512]{1,0:T(8,128)(2,1)}, bf16[128,512]{1,0:T(8,128)(2,1)S(1)}, u32[]{:S(2)}, u32[]{:S(2)}) collective-permute-start(bf16[128,512]{1,0:T(8,128)(2,1)} %get-tuple-element.124), channel_id=1, source_target_pairs={{0,4},{4,0},{1,5},{5,1},{2,6},{6,2},{3,7},{7,3},{8,12},{12,8},{9,1... | collective-permute-start | bytes 393224 | tf_op jit(solution)/shard_map/ppermute | solution.py:24
  5.9 87.4 %collective-permute-start = (bf16[512,512]{1,0:T(8,128)(2,1)}, bf16[512,512]{1,0:T(8,128)(2,1)S(1)}, u32[]{:S(2)}, u32[]{:S(2)}) collective-permute-start(bf16[512,512]{1,0:T(8,128)(2,1)} %param.15), channel_id=1, source_target_pairs={{0,0},{1,8},{2,2},{3,10},{8,1},{9,9},{10,3},{11,11},{4,4},{5,12},{... | collective-permute-start | bytes 1572872 | tf_op jit(solution)/shard_map/ppermute | solution.py:61
  9.5 34.1 %collective-permute-start.2 = (bf16[128,512]{1,0:T(8,128)(2,1)S(1)}, bf16[128,512]{1,0:T(8,128)(2,1)S(1)}, u32[]{:S(2)}, u32[]{:S(2)}) collective-permute-start(bf16[128,512]{1,0:T(8,128)(2,1)S(1)} %fusion.69), channel_id=1, source_target_pairs={{0,4},{4,0},{1,5},{5,1},{2,6},{6,2},{3,7},{7,3},{8,12},{12,8},{9,1... | collective-permute-start | bytes 393224 | tf_op jit(solution)/shard_map/ppermute | solution.py:24
  63.2 28.1 %collective-permute-start.18 = (bf16[128,512]{1,0:T(8,128)(2,1)}, bf16[128,512]{1,0:T(8,128)(2,1)S(1)}, u32[]{:S(2)}, u32[]{:S(2)}) collective-permute-start(bf16[128,512]{1,0:T(8,128)(2,1)} %get-tuple-element.115), channel_id=1, source_target_pairs={{0,4},{4,0},{1,5},{5,1},{2,6},{6,2},{3,7},{7,3},{8,12},{12,8},{9,1... | collective-permute-start | bytes 393224 | tf_op jit(solution)/shard_map/ppermute | solution.py:24
  86.5 55.6 %collective-permute-start.7 = (bf16[2,4,128,1024]{3,2,1,0:T(8,128)(2,1)S(1)}, bf16[2,4,128,1024]{3,2,1,0:T(8,128)(2,1)S(1)}, u32[]{:S(2)}, u32[]{:S(2)}) collective-permute-start(bf16[2,4,128,1024]{3,2,1,0:T(8,128)(2,1)S(1)} %pad_maximum_fusion.5), channel_id=1, source_target_pairs={{0,8},{8,0},{1,9},{9,1},{2,10},{10,2},{3,11},{11,3},{4,12},{12,4},... | collective-permute-start | bytes 6291464 | tf_op jit(solution)/shard_map/ppermute | solution.py:24
  86.9 28.4 %collective-permute-start.14 = (bf16[128,1024]{1,0:T(8,128)(2,1)S(1)}, bf16[128,1024]{1,0:T(8,128)(2,1)S(1)}, u32[]{:S(2)}, u32[]{:S(2)}) collective-permute-start(bf16[128,1024]{1,0:T(8,128)(2,1)S(1)} %maximum_select_fusion.18), channel_id=1, source_target_pairs={{0,2},{1,3},{2,0},{3,1},{4,6},{5,7},{6,4},{7,5},{8,10},{9,11},{10,... | collective-permute-start | bytes 786440 | tf_op jit(solution)/shard_map/ppermute | solution.py:145
  91.3 24.0 %collective-permute-start.13 = (bf16[128,1024]{1,0:T(8,128)(2,1)S(1)}, bf16[128,1024]{1,0:T(8,128)(2,1)S(1)}, u32[]{:S(2)}, u32[]{:S(2)}) collective-permute-start(bf16[128,1024]{1,0:T(8,128)(2,1)S(1)} %maximum_select_fusion.18), channel_id=1, source_target_pairs={{0,1},{1,2},{2,3},{3,0},{4,5},{5,6},{6,7},{7,4},{8,9},{9,10},{10,1... | collective-permute-start | bytes 786440 | tf_op jit(solution)/shard_map/ppermute | solution.py:145
  93.3 46.6 %collective-permute-start.1 = (bf16[512,512]{1,0:T(8,128)(2,1)S(1)}, bf16[512,512]{1,0:T(8,128)(2,1)S(1)}, u32[]{:S(2)}, u32[]{:S(2)}) collective-permute-start(bf16[512,512]{1,0:T(8,128)(2,1)S(1)} %collective-permute-done), channel_id=1, source_target_pairs={{0,4},{4,0},{1,5},{5,1},{2,6},{6,2},{3,7},{7,3},{8,12},{12,8},{9,1... | collective-permute-start | bytes 1572872 | tf_op jit(solution)/shard_map/ppermute | solution.py:24
  96.3 26.4 %collective-permute-start.21 = (bf16[128,1024]{1,0:T(8,128)(2,1)S(1)}, bf16[128,1024]{1,0:T(8,128)(2,1)S(1)}, u32[]{:S(2)}, u32[]{:S(2)}) collective-permute-start(bf16[128,1024]{1,0:T(8,128)(2,1)S(1)} %maximum_select_fusion.20), channel_id=1, source_target_pairs={{0,3},{1,0},{2,1},{3,2},{4,7},{5,4},{6,5},{7,6},{8,11},{9,8},{10,9... | collective-permute-start | bytes 786440 | tf_op jit(solution)/shard_map/ppermute | solution.py:145
  115.3 23.9 %collective-permute-start.19 = (bf16[128,1024]{1,0:T(8,128)(2,1)S(1)}, bf16[128,1024]{1,0:T(8,128)(2,1)S(1)}, u32[]{:S(2)}, u32[]{:S(2)}) collective-permute-start(bf16[128,1024]{1,0:T(8,128)(2,1)S(1)} %maximum_select_fusion.20), channel_id=1, source_target_pairs={{0,1},{1,2},{2,3},{3,0},{4,5},{5,6},{6,7},{7,4},{8,9},{9,10},{10,1... | collective-permute-start | bytes 786440 | tf_op jit(solution)/shard_map/ppermute | solution.py:145
  122.7 131.4 %collective-permute-start.27 = (bf16[512,512]{1,0:T(8,128)(2,1)}, bf16[512,512]{1,0:T(8,128)(2,1)}, u32[]{:S(2)}, u32[]{:S(2)}) collective-permute-start(bf16[512,512]{1,0:T(8,128)(2,1)} %param.29), channel_id=1, source_target_pairs={{0,0},{1,8},{2,2},{3,10},{8,1},{9,9},{10,3},{11,11},{4,4},{5,12},{... | collective-permute-start | bytes 1572872 | tf_op jit(solution)/shard_map/ppermute | solution.py:61
  137.6 26.1 %collective-permute-start.16 = (bf16[4,128,1024]{2,1,0:T(8,128)(2,1)S(1)}, bf16[4,128,1024]{2,1,0:T(8,128)(2,1)S(1)}, u32[]{:S(2)}, u32[]{:S(2)}) collective-permute-start(bf16[4,128,1024]{2,1,0:T(8,128)(2,1)S(1)} %get-tuple-element.121), channel_id=1, source_target_pairs={{0,16},{16,0},{1,17},{17,1},{2,18},{18,2},{3,19},{19,3},{4,20},{20... | collective-permute-start | bytes 3145736 | tf_op jit(solution)/shard_map/ppermute | solution.py:24
  139.3 45.7 %collective-permute-start.22 = (bf16[4,128,1024]{2,1,0:T(8,128)(2,1)S(1)}, bf16[4,128,1024]{2,1,0:T(8,128)(2,1)S(1)}, u32[]{:S(2)}, u32[]{:S(2)}) collective-permute-start(bf16[4,128,1024]{2,1,0:T(8,128)(2,1)S(1)} %get-tuple-element.112), channel_id=1, source_target_pairs={{0,16},{16,0},{1,17},{17,1},{2,18},{18,2},{3,19},{19,3},{4,20},{20... | collective-permute-start | bytes 3145736 | tf_op jit(solution)/shard_map/ppermute | solution.py:24
  144.3 44.2 %collective-permute-start.8 = (bf16[512,1024]{0,1:T(8,128)(2,1)S(1)}, bf16[512,1024]{0,1:T(8,128)(2,1)S(1)}, u32[]{:S(2)}, u32[]{:S(2)}) collective-permute-start(bf16[512,1024]{0,1:T(8,128)(2,1)S(1)} %pad_maximum_fusion.10), channel_id=1, source_target_pairs={{0,8},{8,0},{1,9},{9,1},{2,10},{10,2},{3,11},{11,3},{4,12},{12,4},... | collective-permute-start | bytes 3145736 | tf_op jit(solution)/shard_map/ppermute | solution.py:24
  166.0 56.0 %collective-permute-start.17 = (bf16[2,4,128,1024]{3,2,1,0:T(8,128)(2,1)}, bf16[2,4,128,1024]{3,2,1,0:T(8,128)(2,1)}, u32[]{:S(2)}, u32[]{:S(2)}) collective-permute-start(bf16[2,4,128,1024]{3,2,1,0:T(8,128)(2,1)} %get-tuple-element.98), channel_id=1, source_target_pairs={{0,8},{8,0},{1,9},{9,1},{2,10},{10,2},{3,11},{11,3},{4,12},{12,4},... | collective-permute-start | bytes 6291464 | tf_op jit(solution)/shard_map/ppermute | solution.py:24
  187.3 37.4 %collective-permute-start.23 = (bf16[2,4,128,1024]{3,2,1,0:T(8,128)(2,1)}, bf16[2,4,128,1024]{3,2,1,0:T(8,128)(2,1)}, u32[]{:S(2)}, u32[]{:S(2)}) collective-permute-start(bf16[2,4,128,1024]{3,2,1,0:T(8,128)(2,1)} %get-tuple-element.90), channel_id=1, source_target_pairs={{0,8},{8,0},{1,9},{9,1},{2,10},{10,2},{3,11},{11,3},{4,12},{12,4},... | collective-permute-start | bytes 6291464 | tf_op jit(solution)/shard_map/ppermute | solution.py:24
  293.6 29.2 %collective-permute-start.26 = (bf16[512,512]{1,0:T(8,128)(2,1)}, bf16[512,512]{1,0:T(8,128)(2,1)S(1)}, u32[]{:S(2)}, u32[]{:S(2)}) collective-permute-start(bf16[512,512]{1,0:T(8,128)(2,1)} %maximum_select_fusion.6), channel_id=1, source_target_pairs={{0,0},{1,8},{2,2},{3,10},{8,1},{9,9},{10,3},{11,11},{4,4},{5,12},{... | collective-permute-start | bytes 1572872 | tf_op jit(solution)/shard_map/ppermute | solution.py:61
  310.4 65.9 %collective-permute-start.44 = (bf16[2,4,128,1024]{3,2,1,0:T(8,128)(2,1)}, bf16[2,4,128,1024]{3,2,1,0:T(8,128)(2,1)}, u32[]{:S(2)}, u32[]{:S(2)}) collective-permute-start(bf16[2,4,128,1024]{3,2,1,0:T(8,128)(2,1)} %bitcast.142), channel_id=1, source_target_pairs={{0,8},{8,0},{1,9},{9,1},{2,10},{10,2},{3,11},{11,3},{4,12},{12,4},... | collective-permute-start | bytes 6291464 | tf_op jit(solution)/shard_map/ppermute | solution.py:24
  314.3 68.1 %collective-permute-start.52 = (bf16[2,4,128,1024]{3,2,1,0:T(8,128)(2,1)}, bf16[2,4,128,1024]{3,2,1,0:T(8,128)(2,1)}, u32[]{:S(2)}, u32[]{:S(2)}) collective-permute-start(bf16[2,4,128,1024]{3,2,1,0:T(8,128)(2,1)} %bitcast.159), channel_id=1, source_target_pairs={{0,8},{8,0},{1,9},{9,1},{2,10},{10,2},{3,11},{11,3},{4,12},{12,4},... | collective-permute-start | bytes 6291464 | tf_op jit(solution)/shard_map/ppermute | solution.py:24
  374.4 57.6 %collective-permute-start.32 = (f32[512,1024]{0,1:T(8,128)}, f32[512,1024]{0,1:T(8,128)}, u32[]{:S(2)}, u32[]{:S(2)}) collective-permute-start(f32[512,1024]{0,1:T(8,128)} %pad_maximum_fusion.4), channel_id=1, source_target_pairs={{0,8},{8,0},{1,9},{9,1},{2,10},{10,2},{3,11},{11,3},{4,12},{12,4},... | collective-permute-start | bytes 6291464 | tf_op jit(solution)/shard_map/ppermute | solution.py:24
  380.8 26.0 %collective-permute-start.45 = (bf16[4,128,1024]{2,1,0:T(8,128)(2,1)S(1)}, bf16[4,128,1024]{2,1,0:T(8,128)(2,1)S(1)}, u32[]{:S(2)}, u32[]{:S(2)}) collective-permute-start(bf16[4,128,1024]{2,1,0:T(8,128)(2,1)S(1)} %fusion.24), channel_id=1, source_target_pairs={{0,16},{16,0},{1,17},{17,1},{2,18},{18,2},{3,19},{19,3},{4,20},{20... | collective-permute-start | bytes 3145736 | tf_op jit(solution)/shard_map/ppermute | solution.py:24
  385.4 43.5 %collective-permute-start.53 = (bf16[4,128,1024]{2,1,0:T(8,128)(2,1)S(1)}, bf16[4,128,1024]{2,1,0:T(8,128)(2,1)S(1)}, u32[]{:S(2)}, u32[]{:S(2)}) collective-permute-start(bf16[4,128,1024]{2,1,0:T(8,128)(2,1)S(1)} %fusion.25), channel_id=1, source_target_pairs={{0,16},{16,0},{1,17},{17,1},{2,18},{18,2},{3,19},{19,3},{4,20},{20... | collective-permute-start | bytes 3145736 | tf_op jit(solution)/shard_map/ppermute | solution.py:24
  409.6 79.5 %collective-permute-start.48 = (bf16[128,1024]{1,0:T(8,128)(2,1)}, bf16[128,1024]{1,0:T(8,128)(2,1)S(1)}, u32[]{:S(2)}, u32[]{:S(2)}) collective-permute-start(bf16[128,1024]{1,0:T(8,128)(2,1)} %get-tuple-element.104), channel_id=1, source_target_pairs={{0,1},{1,2},{2,3},{3,0},{4,5},{5,6},{6,7},{7,4},{8,9},{9,10},{10,1... | collective-permute-start | bytes 786440 | tf_op jit(solution)/shard_map/ppermute | solution.py:160
  409.6 82.6 %collective-permute-start.47 = (bf16[128,1024]{1,0:T(8,128)(2,1)}, bf16[128,1024]{1,0:T(8,128)(2,1)}, u32[]{:S(2)}, u32[]{:S(2)}) collective-permute-start(bf16[128,1024]{1,0:T(8,128)(2,1)} %get-tuple-element.105), channel_id=1, source_target_pairs={{0,2},{1,3},{2,0},{3,1},{4,6},{5,7},{6,4},{7,5},{8,10},{9,11},{10,... | collective-permute-start | bytes 786440 | tf_op jit(solution)/shard_map/ppermute | solution.py:160
  409.6 84.1 %collective-permute-start.46 = (bf16[128,1024]{1,0:T(8,128)(2,1)}, bf16[128,1024]{1,0:T(8,128)(2,1)}, u32[]{:S(2)}, u32[]{:S(2)}) collective-permute-start(bf16[128,1024]{1,0:T(8,128)(2,1)} %get-tuple-element.103), channel_id=1, source_target_pairs={{0,3},{1,0},{2,1},{3,2},{4,7},{5,4},{6,5},{7,6},{8,11},{9,8},{10,9... | collective-permute-start | bytes 786440 | tf_op jit(solution)/shard_map/ppermute | solution.py:160
  431.6 65.8 %collective-permute-start.56 = (bf16[128,1024]{1,0:T(8,128)(2,1)}, bf16[128,1024]{1,0:T(8,128)(2,1)}, u32[]{:S(2)}, u32[]{:S(2)}) collective-permute-start(bf16[128,1024]{1,0:T(8,128)(2,1)} %get-tuple-element.101), channel_id=1, source_target_pairs={{0,1},{1,2},{2,3},{3,0},{4,5},{5,6},{6,7},{7,4},{8,9},{9,10},{10,1... | collective-permute-start | bytes 786440 | tf_op jit(solution)/shard_map/ppermute | solution.py:160
  438.6 67.5 %collective-permute-start.36 = (bf16[2,4,128,1024]{3,2,1,0:T(8,128)(2,1)}, bf16[2,4,128,1024]{3,2,1,0:T(8,128)(2,1)}, u32[]{:S(2)}, u32[]{:S(2)}) collective-permute-start(bf16[2,4,128,1024]{3,2,1,0:T(8,128)(2,1)} %bitcast.100), channel_id=1, source_target_pairs={{0,8},{8,0},{1,9},{9,1},{2,10},{10,2},{3,11},{11,3},{4,12},{12,4},... | collective-permute-start | bytes 6291464 | tf_op jit(solution)/shard_map/ppermute | solution.py:24
  512.8 28.6 %collective-permute-start.50 = (bf16[2,128,512]{2,1,0:T(8,128)(2,1)S(1)}, bf16[2,128,512]{2,1,0:T(8,128)(2,1)S(1)}, u32[]{:S(2)}, u32[]{:S(2)}) collective-permute-start(bf16[2,128,512]{2,1,0:T(8,128)(2,1)S(1)} %get-tuple-element.148), channel_id=1, source_target_pairs={{0,8},{8,0},{1,9},{9,1},{2,10},{10,2},{3,11},{11,3},{4,12},{12,4},... | collective-permute-start | bytes 786440 | tf_op jit(solution)/shard_map/ppermute | solution.py:24
  516.7 51.3 %collective-permute-start.58 = (bf16[2,128,512]{2,1,0:T(8,128)(2,1)S(1)}, bf16[2,128,512]{2,1,0:T(8,128)(2,1)S(1)}, u32[]{:S(2)}, u32[]{:S(2)}) collective-permute-start(bf16[2,128,512]{2,1,0:T(8,128)(2,1)S(1)} %get-tuple-element.145), channel_id=1, source_target_pairs={{0,8},{8,0},{1,9},{9,1},{2,10},{10,2},{3,11},{11,3},{4,12},{12,4},... | collective-permute-start | bytes 786440 | tf_op jit(solution)/shard_map/ppermute | solution.py:24
  546.9 25.0 %collective-permute-start.51 = (bf16[2,2,128,512]{3,2,0,1:T(8,128)(2,1)S(1)}, bf16[2,2,128,512]{3,2,0,1:T(8,128)(2,1)S(1)}, u32[]{:S(2)}, u32[]{:S(2)}) collective-permute-start(bf16[2,2,128,512]{3,2,0,1:T(8,128)(2,1)S(1)} %maximum_select_fusion.12), channel_id=1, source_target_pairs={{0,16},{16,0},{1,17},{17,1},{2,18},{18,2},{3,19},{19,3},{4,20},{20... | collective-permute-start | bytes 1572872 | tf_op jit(solution)/shard_map/ppermute | solution.py:24
  557.0 29.8 %collective-permute-start.35 = (f32[512,512]{1,0:T(8,128)}, f32[512,512]{1,0:T(8,128)}, u32[]{:S(2)}, u32[]{:S(2)}) collective-permute-start(f32[512,512]{1,0:T(8,128)} %maximum_select_fusion.2), channel_id=1, source_target_pairs={{0,0},{1,8},{2,2},{3,10},{8,1},{9,9},{10,3},{11,11},{4,4},{5,12},{... | collective-permute-start | bytes 3145736 | tf_op jit(solution)/shard_map/ppermute | solution.py:61
  571.2 23.6 %collective-permute-start.43 = (bf16[2,2,128,512]{3,2,0,1:T(8,128)(2,1)}, bf16[2,2,128,512]{3,2,0,1:T(8,128)(2,1)}, u32[]{:S(2)}, u32[]{:S(2)}) collective-permute-start(bf16[2,2,128,512]{3,2,0,1:T(8,128)(2,1)} %maximum_select_fusion.10), channel_id=1, source_target_pairs={{0,16},{16,0},{1,17},{17,1},{2,18},{18,2},{3,19},{19,3},{4,20},{20... | collective-permute-start | bytes 1572872 | tf_op jit(solution)/shard_map/ppermute | solution.py:24
  (95 other events, 1074.9 us)

commit v2 on v1

v2 whole, which is shorter than its diff:
```python
import functools

import jax
import jax.numpy as jnp
from jax import lax
from jax.experimental import pallas as pl
from jax.experimental.pallas import tpu as pltpu
from jax.sharding import Mesh, PartitionSpec as P

D = 1024
HEAD = 64
LEN = 1024
epsilon = 1e-05
masked_score = -1e30
bf16 = jnp.bfloat16
f32 = jnp.float32


def size(axis):
    return lax.axis_size(axis)


def place(axis):
    return lax.axis_index(axis)


def pair(values, axis):
    return lax.ppermute(values, axis, [(0, 1), (1, 0)])


def after(values, *others):
    return lax.optimization_barrier((values,) + others)[0]


def shift(values, step):
    count = size("col")
    return lax.ppermute(values, "col", [(i, (i + step) % count) for i in range(count)])


def by_place(bit, own, other, axis):
    return jnp.where(
        bit == 0,
        jnp.concatenate((own, other), axis),
        jnp.concatenate((other, own), axis),
    )


def nt(left, right, kind=f32):
    return lax.dot_general(
        left, right, (((1,), (1,)), ((), ())), preferred_element_type=f32
    ).astype(kind)


def nn(left, right, kind=f32):
    return lax.dot_general(
        left, right, (((1,), (0,)), ((), ())), preferred_element_type=f32
    ).astype(kind)


def tn(left, right, kind=f32):
    return lax.dot_general(
        left, right, (((0,), (0,)), ((), ())), preferred_element_type=f32
    ).astype(kind)


def swap_sequences(values):
    count = size("col")
    perm = []
    for core in range(2):
        for col in range(count):
            half, other = col % 2, col - col % 2
            target = (half, other + core)
            perm.append((core * count + col, target[0] * count + target[1]))
    return lax.ppermute(values, ("core", "col"), perm)


def own_first(values):
    if size("row") != 2:
        return values
    half = values.shape[0] // 2
    return jnp.where(place("row") == 0, values, jnp.roll(values, half, axis=0))


def own_part(values):
    share = values.shape[0] // size("row")
    if size("row") == 2:
        return values[:share]
    return lax.dynamic_slice_in_dim(values, place("row") * share, share)


def gather_features(values):
    if size("row") == 2:
        full = by_place(place("row"), values, pair(values, "row"), 1)
        return own_first(full)
    return lax.all_gather(values, "row", axis=1, tiled=True)


def gather_tokens(values):
    if size("row") == 2:
        return jnp.concatenate((values, pair(values, "row")), 0)
    return lax.all_gather(values, "row", axis=0, tiled=True)


def sum_tokens(partial):
    if size("row") == 2:
        share = partial.shape[0] // 2
        return partial[:share] + pair(partial[share:].astype(bf16), "row").astype(f32)
    return lax.psum_scatter(partial, "row", scatter_dimension=0, tiled=True)


def to_own_tokens(values):
    if size("row") == 2:
        bit = place("row")
        ordered = own_first(values)
        share = values.shape[0] // 2
        return by_place(bit, ordered[:share], pair(ordered[share:], "row"), 1)
    return lax.all_to_all(values, "row", 0, 1, tiled=True)


def to_own_features(values):
    if size("row") == 2:
        bit = place("row")
        half = values.shape[1] // 2
        low, high = values[:, :half], values[:, half:]
        own = jnp.where(bit == 0, low, high)
        other = pair(jnp.where(bit == 0, high, low), "row")
        return by_place(bit, own, other, 0)
    return lax.all_to_all(values, "row", 1, 0, tiled=True)


def sum_features(partial, addend):
    if size("row") == 2:
        half = partial.shape[1] // 2
        low, high = partial[:, :half], partial[:, half:]
        bit = place("row")
        got = pair(jnp.where(bit == 0, high, low).astype(bf16), "row").astype(f32)
        got = jnp.roll(got, partial.shape[0] // 2, axis=0)
        return own_first(jnp.where(bit == 0, low, high) + got) + addend
    return lax.psum_scatter(partial, "row", scatter_dimension=1, tiled=True) + addend


def three_groups(triple, merge, expand, shrink):
    depth = triple.shape[0]
    heads = triple.transpose(1, 2, 0).reshape(3, 2, 2, 1, HEAD, depth)
    out = merge.reshape(1, 2, 2, 1, HEAD, depth)
    keys_values = jnp.concatenate((heads[1], heads[2]), 3 - 1)
    queries_merge = jnp.concatenate((heads[0], out[0]), 3 - 1)
    attend = jnp.stack((keys_values, queries_merge), 2).reshape(2, 2, 2, 2 * HEAD, depth)
    widen = expand.T.reshape(2, 2, 2, -1, depth)
    narrow = shrink.reshape(2, 2, 2, -1, depth)
    return attend, widen, narrow


def my_quarter(group):
    some = lax.dynamic_index_in_dim(group, place("outer"), 1, keepdims=False)
    return lax.dynamic_index_in_dim(some, place("core"), 1, keepdims=False)


def exchange_rows(quarter):
    bit = place("row")
    mine = jnp.where(bit == 0, quarter[0], quarter[1])
    other = pair(jnp.where(bit == 0, quarter[1], quarter[0]), "row")
    return by_place(bit, mine, other, 1)


STEPS = (1, 3, 2)


def own_core_half(parts, pairs):
    count = size("col")
    return jnp.stack(
        [jnp.stack([group[step] for step in range(count)]) for group in (parts, pairs)]
    )


def gather_attend(quarter):
    parts = {0: quarter}
    for step in STEPS:
        parts[step] = shift(quarter, step)
    pairs = {step: pair(parts[step], "outer") for step in (0,) + STEPS}
    return own_core_half(parts, pairs), parts[2], pairs[2]


BACK = (2, 1, 3)


def collect_outer(own, other):
    total = own + pair(other, "core").astype(f32)
    return total[0], total[1].astype(bf16)


def collect_send(mates):
    return {step: pair(mates[step], "outer") for step in BACK + (0,)}


def collect_add(own, got, step):
    return own[step] + got[step].astype(f32)


def collect_rest(sums):
    last = sums[0]
    for step in BACK:
        last = last + sums[step].astype(f32)
    return last


def collect_block(last):
    bit = place("row")
    half = last.shape[1] // 2
    low, high = last[:, :half].astype(bf16), last[:, half:].astype(bf16)
    mine = jnp.where(bit == 0, low, high)
    got = pair(jnp.where(bit == 0, high, low), "row")
    block = jnp.stack((jnp.where(bit == 0, mine, got), jnp.where(bit == 0, got, mine)))
    block = by_place(place("outer"), block[:, None], pair(block, "outer")[:, None], 1)
    block = by_place(place("core"), block[:, :, None], pair(block, "core")[:, :, None], 2)
    return block.astype(f32)


def ungroup(attend, widen, narrow):
    depth = attend.shape[-1]
    heads = attend.reshape(4, 2, 2, HEAD, depth)
    keys, values = heads[:, 0, 0], heads[:, 0, 1]
    queries, merge = heads[:, 1, 0], heads[:, 1, 1]
    triple = jnp.stack((queries, keys, values)).reshape(3, 4 * HEAD, depth).transpose(2, 0, 1)
    return (
        triple,
        merge.reshape(4 * HEAD, depth),
        widen.reshape(-1, depth).T,
        narrow.reshape(-1, depth),
    )


def flip(values, axis, bit):
    return jnp.where(bit == 0, values, jnp.flip(values, axis))


def dot(left, right, left_dim, right_dim):
    return lax.dot_general(
        left, right, (((left_dim,), (right_dim,)), ((), ())), preferred_element_type=f32
    )


def params():
    return pltpu.CompilerParams(vmem_limit_bytes=56 << 20)


def anywhere(arrays):
    return [pl.BlockSpec(memory_space=pl.ANY) for _ in arrays]


def attend_forward_kernel(q_ref, kv_ref, qs_ref, ks_ref, *rest):
    out_ref, lse_ref = rest[-2:]
    same = ks_ref[...] == qs_ref[...]
    for head in range(2):
        part = slice(head * HEAD, (head + 1) * HEAD)
        keys = kv_ref[:, 2 * head * HEAD : (2 * head + 1) * HEAD]
        values = kv_ref[:, (2 * head + 1) * HEAD : (2 * head + 2) * HEAD]
        queries = q_ref[:, part] * jnp.asarray(HEAD**-0.5, bf16)
        scores = jnp.where(same, dot(keys, queries, 1, 1), masked_score)
        top = jnp.max(scores, axis=0, keepdims=True)
        weights = jnp.exp(scores - top)
        total = jnp.sum(weights, axis=0, keepdims=True)
        low = (weights * (1.0 / total)).astype(bf16)
        out_ref[part] = dot(values, low, 0, 0).astype(bf16)
        lse_ref[0, head : head + 1] = top + jnp.log(total)


def attend_forward(queries, keys_values, query_segment, key_segment, begin, steps, *earlier):
    tokens = queries.shape[0]
    width = steps * 2 * HEAD
    keys = keys_values.shape[0]
    return pl.pallas_call(
        attend_forward_kernel,
        grid=(steps,),
        in_specs=[
            pl.BlockSpec((tokens, 2 * HEAD), lambda i: (0, begin + i)),
            pl.BlockSpec((keys, 4 * HEAD), lambda i: (0, begin + i)),
            pl.BlockSpec((1, tokens), lambda i: (0, 0)),
            pl.BlockSpec((keys, 1), lambda i: (0, 0)),
        ]
        + anywhere(earlier),
        out_specs=[
            pl.BlockSpec((2 * HEAD, tokens), lambda i: (i, 0)),
            pl.BlockSpec((1, 2, tokens), lambda i: (i, 0, 0)),
        ],
        out_shape=[
            jax.ShapeDtypeStruct((width, tokens), bf16),
            jax.ShapeDtypeStruct((steps, 2, tokens), f32),
        ],
        compiler_params=params(),
        cost_estimate=pl.CostEstimate(
            flops=4 * tokens * keys * width * 4,
            bytes_accessed=4 << 20,
            transcendentals=tokens * keys * width // HEAD,
        ),
    )(queries, keys_values, query_segment, key_segment, *earlier)


def attend_backward_kernel(
    q_ref, kv_ref, g_ref, qs_ref, ks_ref, lse_ref, *rest
):
    dq_ref, near_ref, far_ref = rest[-3:]
    same = ks_ref[...] == qs_ref[...]
    scale = HEAD**-0.5
    near = near_ref.shape[0]
    for head in range(2):
        part = slice(head * HEAD, (head + 1) * HEAD)
        key_part = slice(2 * head * HEAD, (2 * head + 1) * HEAD)
        value_part = slice((2 * head + 1) * HEAD, (2 * head + 2) * HEAD)
        keys, values = kv_ref[:, key_part], kv_ref[:, value_part]
        queries = q_ref[:, part] * jnp.asarray(scale, bf16)
        grad = g_ref[:, part]
        scores = jnp.where(same, dot(keys, queries, 1, 1), masked_score)
        weights = jnp.exp(scores - lse_ref[0, head : head + 1])
        grad_weights = dot(values, grad, 1, 1)
        inner = jnp.sum(weights * grad_weights, axis=0, keepdims=True)
        grad_scores = (weights * (grad_weights - inner)).astype(bf16)
        dq_ref[part] = (dot(keys, grad_scores, 0, 0) * scale).astype(bf16)
        grad_keys = dot(grad_scores, queries, 1, 0)
        grad_values = dot(weights.astype(bf16), grad, 1, 0)
        near_ref[:, key_part], far_ref[:, key_part] = grad_keys[:near], grad_keys[near:]
        near_ref[:, value_part], far_ref[:, value_part] = grad_values[:near], grad_values[near:]


def attend_backward(
    queries, keys_values, grad, query_segment, key_segment, lse, begin, steps, *earlier
):
    tokens = queries.shape[0]
    keys = keys_values.shape[0]
    key_block = pl.BlockSpec((tokens, 4 * HEAD), lambda i: (0, i))
    return pl.pallas_call(
        attend_backward_kernel,
        grid=(steps,),
        in_specs=[
            pl.BlockSpec((tokens, 2 * HEAD), lambda i: (0, begin + i)),
            pl.BlockSpec((keys, 4 * HEAD), lambda i: (0, begin + i)),
            pl.BlockSpec((tokens, 2 * HEAD), lambda i: (0, begin + i)),
            pl.BlockSpec((1, tokens), lambda i: (0, 0)),
            pl.BlockSpec((keys, 1), lambda i: (0, 0)),
            pl.BlockSpec((1, 2, tokens), lambda i: (i, 0, 0)),
        ]
        + anywhere(earlier),
        out_specs=[pl.BlockSpec((2 * HEAD, tokens), lambda i: (i, 0)), key_block, key_block],
        out_shape=[
            jax.ShapeDtypeStruct((2 * HEAD * steps, tokens), bf16),
            jax.ShapeDtypeStruct((tokens, 4 * HEAD * steps), f32),
            jax.ShapeDtypeStruct((tokens, 4 * HEAD * steps), f32),
        ],
        compiler_params=params(),
        cost_estimate=pl.CostEstimate(
            flops=10 * tokens * keys * steps * 2 * HEAD * 4,
            bytes_accessed=8 << 20,
            transcendentals=tokens * keys * steps * 2,
        ),
    )(queries, keys_values, grad, query_segment, key_segment, lse, *earlier)


def attend_weights_kernel(
    which_ref, dkv_ref, dq_ref, out_in_ref, x_ref, g_ref, *rest, added, cols
):
    add_ref = rest[0] if added else None
    out_refs = rest[-cols:]

    def put(rows, value):
        value = value.reshape(cols, -1, D)
        for step, out_ref in enumerate(out_refs):
            term = value[step]
            if added:
                term = term + add_ref[0, step, rows].astype(f32)
            out_ref[rows] = term.astype(out_ref.dtype)

    @pl.when(which_ref[0] == 0)
    def _():
        put(slice(0, 2 * HEAD), dot(dkv_ref[...], x_ref[...], 0, 0))

    @pl.when(which_ref[0] == 1)
    def _():
        put(slice(0, HEAD), dot(dq_ref[...], x_ref[...], 1, 0))
        put(slice(HEAD, 2 * HEAD), dot(out_in_ref[...], g_ref[...], 1, 0))


def attend_weights(which, dkv, dq, out_in, x, g, begin, cols, kind, add=None, earlier=()):
    tokens = x.shape[0]
    full = pl.BlockSpec((tokens, D), lambda i, w: (0, 0))
    rows = pl.BlockSpec((cols * HEAD, tokens), lambda i, w: (begin, 0))
    specs = [pl.BlockSpec((tokens, cols * 2 * HEAD), lambda i, w: (0, begin)), rows, rows, full, full]
    given = [dkv, dq, out_in, x, g]
    if add is not None:
        specs.append(pl.BlockSpec((1, cols, 2 * HEAD, D), lambda i, w: (begin, 0, 0, 0)))
        given.append(add)
    return pl.pallas_call(
        functools.partial(attend_weights_kernel, added=add is not None, cols=cols),
        grid_spec=pltpu.PrefetchScalarGridSpec(
            num_scalar_prefetch=1,
            grid=(1,),
            in_specs=specs + anywhere(earlier),
            out_specs=[pl.BlockSpec((2 * HEAD, D), lambda i, w: (0, 0))] * cols,
        ),
        out_shape=[jax.ShapeDtypeStruct((2 * HEAD, D), kind)] * cols,
        compiler_params=params(),
        cost_estimate=pl.CostEstimate(
            flops=4 * tokens * D * cols * HEAD, bytes_accessed=6 << 20, transcendentals=0
        ),
    )(which, *given, *earlier)


def attend_far_kernel(which_ref, dkv_ref, dq_ref, out_in_ref, x_ref, g_ref, *rest):
    out_ref = rest[-1]
    cols = out_ref.shape[1]

    @pl.when(which_ref[0] == 0)
    def _():
        value = dot(dkv_ref[...], x_ref[...], 0, 0)
        out_ref[0] = value.reshape(cols, 2 * HEAD, D).astype(out_ref.dtype)

    @pl.when(which_ref[0] == 1)
    def _():
        for part, value in enumerate(
            (dot(dq_ref[...], x_ref[...], 1, 0), dot(out_in_ref[...], g_ref[...], 1, 0))
        ):
            rows = slice(part * HEAD, (part + 1) * HEAD)
            out_ref[0, :, rows] = value.reshape(cols, HEAD, D).astype(out_ref.dtype)


def attend_far_weights(which, dkv, dq, out_in, x, g, cols, *earlier):
    tokens = x.shape[0]
    full = pl.BlockSpec((tokens, D), lambda i, w: (0, 0))
    rows = pl.BlockSpec((cols * HEAD, tokens), lambda i, w: (i, 0))
    return pl.pallas_call(
        attend_far_kernel,
        grid_spec=pltpu.PrefetchScalarGridSpec(
            num_scalar_prefetch=1,
            grid=(2,),
            in_specs=[
                pl.BlockSpec((tokens, cols * 2 * HEAD), lambda i, w: (0, i)), rows, rows, full, full
            ]
            + anywhere(earlier),
            out_specs=pl.BlockSpec((1, cols, 2 * HEAD, D), lambda i, w: (i, 0, 0, 0)),
        ),
        out_shape=jax.ShapeDtypeStruct((2, cols, 2 * HEAD, D), bf16),
        compiler_params=params(),
        cost_estimate=pl.CostEstimate(
            flops=8 * tokens * D * cols * HEAD, bytes_accessed=6 << 20, transcendentals=0
        ),
    )(which, dkv, dq, out_in, x, g, *earlier)


def hidden_forward_kernel(x_ref,own_ref,far_ref,bias_ref,hidden_ref,slope_ref,keep_ref,send_ref,total):
    step=pl.program_id(0)
    units=own_ref.shape[2]//2
    width=own_ref.shape[1]*units
    @pl.when(step==0)
    def _(): total[...]=jnp.zeros_like(total)
    for core,ref in enumerate((own_ref,far_ref)):
        expand=ref[0,:,:units].reshape(width,D)
        shrink=ref[0,:,units:].reshape(width,D)
        u=dot(x_ref[...],expand,1,1)+bias_ref[0,core:core+1]
        normal=0.5*(1.0+lax.erf(u*(0.5**0.5)))
        slope_ref[core]=normal+u*(jnp.exp(-0.5*u*u)*((0.5/jnp.pi)**0.5))
        hidden=(u*normal).astype(bf16)
        hidden_ref[core]=hidden
        total[...]+=dot(hidden,shrink,1,0)
    @pl.when(step==pl.num_programs(0)-1)
    def _():
        half=total.shape[0]//2
        keep_ref[...]=total[:half]
        send_ref[...]=total[half:].astype(bf16)


def hidden_forward(x,own,far,bias):
    tokens=x.shape[0]; outer,cols,two,_=own.shape; units=two//2; pairs=2
    steps=outer*cols//pairs; width=pairs*units; per=cols//pairs
    block=pl.BlockSpec((1,pairs,two,D),lambda i:(i//per,i%per,0,0))
    wide=pl.BlockSpec((2,tokens,width),lambda i:(0,0,i))
    half=pl.BlockSpec((tokens//2,D),lambda i:(0,0))
    return pl.pallas_call(hidden_forward_kernel,grid=(steps,),
      in_specs=[pl.BlockSpec((tokens,D),lambda i:(0,0)),block,block,pl.BlockSpec((1,2,width),lambda i:(i,0,0))],
      out_specs=[wide,wide,half,half],
      out_shape=[jax.ShapeDtypeStruct((2,tokens,steps*width),bf16),jax.ShapeDtypeStruct((2,tokens,steps*width),f32),
                 jax.ShapeDtypeStruct((tokens//2,D),f32),jax.ShapeDtypeStruct((tokens//2,D),bf16)],
      scratch_shapes=[pltpu.VMEM((tokens,D),f32)],compiler_params=params(),
      cost_estimate=pl.CostEstimate(flops=8*tokens*D*steps*width,bytes_accessed=20<<20,transcendentals=4*tokens*steps*width))(x,own,far,bias)


def hidden_backward_kernel(g_ref,own_ref,far_ref,slope_ref,grad_ref,sum_ref,keep_ref,send_ref,total):
    step=pl.program_id(0)
    units=own_ref.shape[2]//2
    width=own_ref.shape[1]*units
    @pl.when(step==0)
    def _(): total[...]=jnp.zeros_like(total)
    for core,ref in enumerate((own_ref,far_ref)):
        expand=ref[0,:,:units].reshape(width,D)
        shrink=ref[0,:,units:].reshape(width,D)
        grad=(dot(g_ref[...],shrink,1,1)*slope_ref[core]).astype(bf16)
        grad_ref[core]=grad
        sum_ref[0,core:core+1]=jnp.sum(grad.astype(f32),axis=0,keepdims=True)
        total[...]+=dot(grad,expand,1,0)
    @pl.when(step==pl.num_programs(0)-1)
    def _():
        half=total.shape[0]//2
        keep_ref[...]=total[:half]
        send_ref[...]=total[half:].astype(bf16)


def hidden_backward(g,own,far,slope):
    tokens=g.shape[0]; outer,cols,two,_=own.shape; units=two//2; pairs=2
    steps=outer*cols//pairs; width=pairs*units; per=cols//pairs
    block=pl.BlockSpec((1,pairs,two,D),lambda i:(i//per,i%per,0,0))
    wide=pl.BlockSpec((2,tokens,width),lambda i:(0,0,i))
    half=pl.BlockSpec((tokens//2,D),lambda i:(0,0))
    return pl.pallas_call(hidden_backward_kernel,grid=(steps,),
      in_specs=[pl.BlockSpec((tokens,D),lambda i:(0,0)),block,block,wide],
      out_specs=[wide,pl.BlockSpec((1,2,width),lambda i:(i,0,0)),half,half],
      out_shape=[jax.ShapeDtypeStruct((2,tokens,steps*width),bf16),jax.ShapeDtypeStruct((steps,2,width),f32),
                 jax.ShapeDtypeStruct((tokens//2,D),f32),jax.ShapeDtypeStruct((tokens//2,D),bf16)],
      scratch_shapes=[pltpu.VMEM((tokens,D),f32)],compiler_params=params(),
      cost_estimate=pl.CostEstimate(flops=8*tokens*D*steps*width,bytes_accessed=20<<20,transcendentals=0))(g,own,far,slope)


def hidden_weights_kernel(grad_ref,hidden_ref,x_ref,g_ref,*rest):
    out_ref=rest[-1]; add_ref=rest[0] if len(rest)>=2 else None
    cols,two,_=out_ref.shape[-3:]; units=two//2
    for part,(left,right) in enumerate(((grad_ref,x_ref),(hidden_ref,g_ref))):
        rows=slice(part*units,(part+1)*units)
        value=dot(left[0],right[...],0,0).reshape(cols,units,D)
        if add_ref is not None: value=value+add_ref[0,:,rows].astype(f32)
        out_ref[0,:,rows]=value.astype(out_ref.dtype)


def hidden_weights(grad,hidden,x,g,core,begin,count,cols,kind,add=None,earlier=()):
    tokens=x.shape[0]; width=grad.shape[2]//2; units=width//cols
    left=pl.BlockSpec((1,tokens,width),lambda i:(core,0,begin+i))
    full=pl.BlockSpec((tokens,D),lambda i:(0,0))
    specs=[left,left,full,full]; args=[grad,hidden,x,g]
    if add is not None:
        specs.append(pl.BlockSpec((1,cols,2*units,D),lambda i:(begin+i,0,0,0))); args.append(add)
    specs+=anywhere(earlier); args+=earlier
    return pl.pallas_call(hidden_weights_kernel,grid=(count,),in_specs=specs,
      out_specs=pl.BlockSpec((1,cols,2*units,D),lambda i:(i,0,0,0)),
      out_shape=jax.ShapeDtypeStruct((count,cols,2*units,D),kind),compiler_params=params(),
      cost_estimate=pl.CostEstimate(flops=4*tokens*D*width*count,bytes_accessed=8<<20,transcendentals=0))(*args)


def hidden_own_kernel(grad_ref, hidden_ref, x_ref, g_ref, add_ref, *rest, cols):
    out_refs = rest[-cols:]
    units = out_refs[0].shape[0] // 2
    for part, (left, right) in enumerate(((grad_ref, x_ref), (hidden_ref, g_ref))):
        rows = slice(part * units, (part + 1) * units)
        value = dot(left[0], right[...], 0, 0).reshape(cols, units, D)
        for step, out_ref in enumerate(out_refs):
            term = value[step] + add_ref[0, step, rows].astype(f32)
            out_ref[rows] = term.astype(out_ref.dtype)


def hidden_own_weights(grad, hidden, x, g, begin, cols, kind, add, *earlier):
    tokens = x.shape[0]
    width = grad.shape[2] // 2
    units = width // cols
    left = pl.BlockSpec((1, tokens, width), lambda i: (0, 0, begin))
    full = pl.BlockSpec((tokens, D), lambda i: (0, 0))
    return pl.pallas_call(
        functools.partial(hidden_own_kernel, cols=cols),
        grid=(1,),
        in_specs=[
            left, left, full, full, pl.BlockSpec((1, cols, 2 * units, D), lambda i: (begin, 0, 0, 0))
        ]
        + anywhere(earlier),
        out_specs=[pl.BlockSpec((2 * units, D), lambda i: (0, 0))] * cols,
        out_shape=[jax.ShapeDtypeStruct((2 * units, D), kind)] * cols,
        compiler_params=params(),
        cost_estimate=pl.CostEstimate(
            flops=4 * tokens * D * width, bytes_accessed=8 << 20, transcendentals=0
        ),
    )(grad, hidden, x, g, add, *earlier)


def layer(
    tokens, segments, triple_weight, pair_bias, merge_weight, merge_bias, first_gain, first_shift,
    expand_weight, expand_bias, shrink_weight, shrink_bias, second_gain, second_shift, cotangent,
):
    cols = size("col")
    count = tokens.shape[0]
    own = count // 2
    heads = D // HEAD // 2
    row, col, core, outer = place("row"), place("col"), place("core"), place("outer")
    row_size, pair_size, hidden_size = merge_bias.shape[0], pair_bias.shape[1], expand_bias.shape[0]

    tokens = swap_sequences(tokens)
    row_vectors = jnp.stack(
        (merge_bias, first_gain, first_shift, shrink_bias, second_gain, second_shift)
    )
    column = jnp.concatenate(
        [
            lax.dynamic_slice_in_dim(vector, row * (vector.shape[0] // 2), vector.shape[0] // 2)
            for vector in (pair_bias[0], pair_bias[1], expand_bias)
        ]
    )
    groups = [
        my_quarter(group)
        for group in three_groups(triple_weight, merge_weight, expand_weight, shrink_weight)
    ]
    quarter, row_vectors, column = lax.optimization_barrier(
        (exchange_rows(groups[0]), row_vectors, column)
    )
    parts = {0: quarter}
    for step in STEPS:
        parts[step] = shift(quarter, step)
    inputs = gather_features(tokens)
    other_quarter = exchange_rows(jnp.concatenate((groups[1], groups[2]), 1))

    half = col % 2
    other = pair(segments.astype(f32), "core").astype(jnp.int32)
    sequence = lax.dynamic_slice_in_dim(
        jnp.where(half == core, segments, other), (col // 2) * LEN, LEN
    ).reshape(2, count)
    query_segment = own_first(lax.dynamic_index_in_dim(sequence, core, 0, keepdims=False))
    far_segment = own_first(lax.dynamic_index_in_dim(sequence, 1 - core, 0, keepdims=False))
    key_segment = jnp.concatenate((query_segment, far_segment))
    segment_row, segment_column = query_segment[None], key_segment[:, None]
    segment_column = jnp.broadcast_to(segment_column, (2 * count, 1))

    vectors = by_place(row, row_vectors, pair(row_vectors, "row"), 1)
    column = jnp.stack([column] + [shift(column, step) for step in range(1, cols)])

    pairs = {step: pair(parts[step], "outer") for step in (0, 1, 3)}
    parts[2], other_quarter, vectors, column, inputs, segment_column, cotangent = (
        lax.optimization_barrier(
            (parts[2], other_quarter, vectors, column, inputs, segment_column, cotangent)
        )
    )
    pairs[2] = pair(parts[2], "outer")
    cotangent = swap_sequences(cotangent)
    other_parts = {0: other_quarter}
    for step in (1, 3):
        other_parts[step] = shift(other_quarter, step)
    attend_own = own_core_half(parts, pairs)
    attend_far = pair(attend_own, "core")
    other_pairs = {0: pair(other_quarter, "outer")}
    upstream = to_own_tokens(cotangent)

    vectors = vectors.astype(f32)
    short = pair_size // 2
    bias_pair = column[:, : 2 * short].reshape(cols, 2, 2, HEAD)
    bias_pair = flip(bias_pair, 2, outer).transpose(1, 2, 0, 3).reshape(2, heads, HEAD).astype(f32)
    bias_queries = bias_pair[0].reshape(-1)
    bias_keys_values = jnp.stack((jnp.zeros_like(bias_pair[1]), bias_pair[1]), 1).reshape(-1)
    bias_hidden = column[:, 2 * short :].reshape(cols, 2, 2, -1)
    bias_hidden = flip(flip(bias_hidden, 1, outer), 2, core).transpose(1, 0, 2, 3)
    bias_hidden = bias_hidden.reshape(2 * cols // 2, 2, 2, -1).transpose(0, 2, 1, 3)
    bias_hidden = bias_hidden.reshape(cols, 2, -1).astype(f32)

    weight_keys_values = jnp.where(core == 0, attend_own, attend_far).reshape(-1, D)
    second = jnp.where(core == 0, attend_far, attend_own).reshape(heads, 2, HEAD, D)
    weight_queries, weight_merge = second[:, 0].reshape(-1, D), second[:, 1].reshape(-1, D)

    cut = heads * HEAD // 2
    steps = heads // 4
    keys_values = (nt(inputs, weight_keys_values) + bias_keys_values).astype(bf16)
    far_keys_values = pair(keys_values, "core")
    queries = (nt(inputs, weight_queries) + bias_queries).astype(bf16)
    keys_values = jnp.concatenate((keys_values, far_keys_values), 0)
    queries, other_parts[1], other_parts[3], other_pairs[0] = lax.optimization_barrier(
        (queries, other_parts[1], other_parts[3], other_pairs[0])
    )
    other_parts[2], other_quarter = lax.optimization_barrier((other_quarter, other_parts[3]))
    other_parts[2] = shift(other_parts[2], 2)
    other_parts[3] = other_quarter
    for step in (1, 3):
        other_pairs[step] = pair(other_parts[step], "outer")
    attention = (queries, keys_values, segment_row, segment_column)
    attended_first, lse_first = attend_forward(*attention, 0, steps)
    attended_second, lse_second = attend_forward(
        *attention, steps, steps, lse_first, other_pairs[1]
    )
    attended_first, attended_second, upstream, other_pairs[3], other_parts[2] = (
        lax.optimization_barrier(
            (attended_first, attended_second, upstream, other_pairs[3], other_parts[2])
        )
    )
    other_pairs[2] = pair(other_parts[2], "outer")
    attended = jnp.concatenate((attended_first, attended_second), 0)
    branch = tn(attended, weight_merge)
    branch = sum_tokens(branch)
    residual = inputs[:own].astype(f32) + (branch + vectors[0])
    scaled_one, inverse_one, normed_one = norm_forward(residual, vectors[1], vectors[2])
    normed_low = gather_tokens(normed_one.astype(bf16))
    other_parts, other_pairs, normed_one = lax.optimization_barrier(
        (other_parts, other_pairs, normed_one)
    )

    other_own = own_core_half(other_parts, other_pairs)
    other_far = pair(other_own, "core")
    hidden, slope, keep, send = hidden_forward(normed_low, other_own, other_far, bias_hidden)
    shrunk = keep + pair(send, "row").astype(f32)
    scaled_two, inverse_two, final = norm_forward(
        normed_one + (shrunk + vectors[3]), vectors[4], vectors[5]
    )
    live = (query_segment[:own] != 0).astype(f32)[:, None]
    upstream = upstream.astype(f32) * live
    grad_sum_two, grad_gain_two, grad_shift_two = norm_backward(
        upstream, scaled_two, inverse_two, vectors[4]
    )
    grad_shrunk_own = grad_sum_two.astype(bf16)
    grad_shrunk = gather_tokens(grad_shrunk_own)
    grad_pre, sum_hidden, keep, send = hidden_backward(grad_shrunk, other_own, other_far, slope)
    got_normed = pair(send, "row")
    part = (grad_pre, hidden, normed_low, grad_shrunk)
    far = hidden_weights(*part, 1, 0, 2, cols, bf16)
    grad_normed = grad_sum_two + (keep + got_normed.astype(f32))
    grad_res, grad_gain_one, grad_shift_one = norm_backward(
        grad_normed, scaled_one, inverse_one, vectors[1]
    )
    grad_branch_own = grad_res.astype(bf16)
    grad_branch = gather_tokens(grad_branch_own)
    far, grad_branch_own = lax.optimization_barrier((far, grad_branch_own))
    far = pair(far, "core")
    mates = hidden_own_weights(*part, 1, cols, bf16, far)
    grad_branch, mates = lax.optimization_barrier((grad_branch, mates))
    hidden_got = collect_send(mates)

    grad_attended = nt(grad_branch, weight_merge, bf16)
    shared = (queries, keys_values, grad_attended, segment_row, segment_column)
    dq_first, near_first, far_first = attend_backward(*shared, lse_first, 0, steps)
    late_out, late_res, far_first = lax.optimization_barrier(
        (final.astype(bf16), grad_res, far_first)
    )
    far_first = pair(far_first, "core")
    hidden_got[2], dq_first = lax.optimization_barrier((hidden_got[2], dq_first))
    hidden_own = hidden_own_weights(*part, 0, cols, f32, far, dq_first)
    hidden_last = {2: collect_add(hidden_own, hidden_got, 2).astype(bf16)}
    dq_second, near_second, far_second = attend_backward(
        *shared, lse_second, steps, steps, hidden_last[2]
    )
    hidden_last[2] = shift(hidden_last[2], -2)
    far_second = pair(far_second, "core")
    layer_out, grad_res_columns = to_own_features(late_out), to_own_features(late_res)
    hidden_got[1], dq_second = lax.optimization_barrier((hidden_got[1], dq_second))
    hidden_last[1] = shift(collect_add(hidden_own, hidden_got, 1).astype(bf16), -1)
    grad_queries = jnp.concatenate((dq_first, dq_second), 0)
    grad_keys_values = jnp.concatenate(
        ((near_first + far_first).astype(bf16), (near_second + far_second).astype(bf16)), 1
    )

    part = (grad_keys_values, grad_queries, attended, inputs, grad_branch)
    far = attend_far_weights((1 - core).reshape(1), *part, cols, hidden_last[2])
    far_got = pair(far, "core")
    grad_entry = nn(grad_keys_values, weight_keys_values) + tn(grad_queries, weight_queries)
    grad_tokens = sum_features(grad_entry, grad_res_columns)
    hidden_got[3], far_got = lax.optimization_barrier((hidden_got[3], far_got))
    hidden_last[3] = shift(collect_add(hidden_own, hidden_got, 3).astype(bf16), -3)
    which = core.reshape(1)
    mates = attend_weights(which, *part, 1, cols, bf16, far_got, (hidden_last[1],))
    got = collect_send(mates)
    attend_own_sums = attend_weights(
        which, *part, 0, cols, f32, far_got, (hidden_got[0], hidden_last[3])
    )
    grad_tokens, layer_out = lax.optimization_barrier((grad_tokens, layer_out))
    layer_out, grad_tokens = swap_sequences(layer_out), swap_sequences(grad_tokens)
    sums = {2: collect_add(attend_own_sums, got, 2)}
    sums[2] = shift(sums[2].astype(bf16), -2)
    hidden_last[0] = collect_add(hidden_own, hidden_got, 0)
    hidden_rest = collect_rest(hidden_last)
    got[1], hidden_rest = lax.optimization_barrier((got[1], hidden_rest))
    for step in (1, 3, 0):
        sums[step] = collect_add(attend_own_sums, got, step)
    for step in (1, 3):
        sums[step] = shift(sums[step].astype(bf16), -step)
    units = hidden_size // 8
    both = collect_block(hidden_rest)
    widen, narrow = both[:, :, :, :units], both[:, :, :, units:]
    attend_rest = collect_rest(sums)
    attend = collect_block(attend_rest)
    grad_triple, grad_merge, grad_expand, grad_shrink = ungroup(attend, widen, narrow)

    sum_rows = jnp.stack(
        (
            jnp.sum(grad_branch_own, axis=0, dtype=f32),
            grad_gain_one,
            grad_shift_one,
            jnp.sum(grad_shrunk_own, axis=0, dtype=f32),
            grad_gain_two,
            grad_shift_two,
        )
    )
    sum_queries = jnp.sum(grad_queries, axis=1, dtype=f32)
    sum_values = jnp.sum(grad_keys_values, axis=0, dtype=f32).reshape(heads, 2, HEAD)[:, 1]
    sum_pair = jnp.stack((sum_queries, sum_values.reshape(-1))).reshape(2, 2, cols, HEAD)
    sum_pair = flip(sum_pair.transpose(2, 0, 1, 3), 2, outer).reshape(cols, -1)
    sum_hidden = sum_hidden.reshape(2, cols // 2, 2, 2, -1).transpose(1, 3, 0, 2, 4)
    sum_hidden = flip(flip(sum_hidden.reshape(cols, 2, 2, -1), 1, outer), 2, core).reshape(cols, -1)
    sum_columns = jnp.concatenate((sum_pair, sum_hidden), 1)
    length = sum_columns.shape[1]
    sum_columns = jnp.concatenate(
        [
            lax.dynamic_index_in_dim(sum_columns, (col - place_of) % cols, 0, keepdims=False)
            for place_of in range(cols)
        ]
    )
    total = jnp.concatenate((sum_columns, sum_rows.reshape(-1)))
    for bit in (1, 2):
        total = total + lax.ppermute(total, "col", [(i, i ^ bit) for i in range(cols)])
    total = total + pair(total, "core")
    total = total + pair(total, "outer")
    mine = lax.dynamic_slice_in_dim(total, col * length, length)
    sum_rows = total[cols * length :].reshape(6, 2, row_size)
    low, high = sum_rows[:, 0].reshape(-1), sum_rows[:, 1].reshape(-1)
    got = pair(jnp.concatenate((mine, jnp.where(row == 0, high, low))), "row")
    totals = (jnp.where(row == 0, low, high) + got[length:]).reshape(6, row_size)
    got = got[:length]
    short = 2 * HEAD
    grad_pair = by_place(
        row, mine[: 2 * short].reshape(2, short), got[: 2 * short].reshape(2, short), 1
    )
    grad_expand_bias = by_place(row, mine[2 * short :], got[2 * short :], 0)
    return (
        layer_out, grad_tokens, grad_triple, grad_pair, grad_merge, totals[0], totals[1], totals[2],
        grad_expand, grad_expand_bias, grad_shrink, totals[3], totals[4], totals[5],
    )


def masked(scores, query_segment, key_segment):
    same = query_segment[:, None] == key_segment[None, :]
    return jnp.where(same[None], scores, masked_score)


def attention_forward(queries, keys, values, query_segment, key_segment):
    scores = jnp.einsum("qhd,khd->hqk", queries, keys, preferred_element_type=f32)
    scores = masked(scores * HEAD**-0.5, query_segment, key_segment)
    top = jnp.max(scores, axis=-1, keepdims=True)
    weights = jnp.exp(scores - top)
    total = jnp.sum(weights, axis=-1, keepdims=True)
    low = (weights / total).astype(bf16)
    attended = jnp.einsum("hqk,khd->qhd", low, values, preferred_element_type=f32)
    return attended.astype(bf16), top + jnp.log(total)


def attention_backward(queries, keys, values, query_segment, key_segment, lse, grad):
    scores = jnp.einsum("qhd,khd->hqk", queries, keys, preferred_element_type=f32)
    scores = masked(scores * HEAD**-0.5, query_segment, key_segment)
    weights = jnp.exp(scores - lse)
    grad_weights = jnp.einsum("qhd,khd->hqk", grad, values, preferred_element_type=f32)
    inner = jnp.sum(weights * grad_weights, axis=-1, keepdims=True)
    grad_scores = (weights * (grad_weights - inner)).astype(bf16)
    scale = HEAD**-0.5
    grad_queries = jnp.einsum("hqk,khd->qhd", grad_scores, keys, preferred_element_type=f32) * scale
    grad_keys = jnp.einsum("hqk,qhd->khd", grad_scores, queries, preferred_element_type=f32) * scale
    grad_values = jnp.einsum(
        "hqk,qhd->khd", weights.astype(bf16), grad, preferred_element_type=f32
    )
    return grad_queries.astype(bf16), grad_keys, grad_values


def norm_forward(values, gain, shift):
    center = jnp.mean(values, axis=1, keepdims=True)
    inverse = lax.rsqrt(
        jnp.mean(values * values, axis=1, keepdims=True) - center * center + epsilon
    )
    scaled = (values - center) * inverse
    return scaled, inverse, scaled * gain + shift


def norm_backward(upstream, scaled, inverse, gain):
    through = upstream * gain
    grad = inverse * (
        through
        - jnp.mean(through, axis=1, keepdims=True)
        - scaled * jnp.mean(through * scaled, axis=1, keepdims=True)
    )
    return grad, jnp.sum(upstream * scaled, axis=0), jnp.sum(upstream, axis=0)


def exact_gelu(values):
    return jax.nn.gelu(values, approximate=False)


def layer_anywhere(
    tokens,
    segments,
    triple_weight,
    pair_bias,
    merge_weight,
    merge_bias,
    first_gain,
    first_shift,
    expand_weight,
    expand_bias,
    shrink_weight,
    shrink_bias,
    second_gain,
    second_shift,
    cotangent,
):
    rows, cols = size("row"), size("col")
    count = tokens.shape[0]
    own = count // rows
    heads = D // HEAD // rows
    row, col = place("row"), place("col")

    query_segment = lax.dynamic_slice_in_dim(segments, col * count, count)
    key_segment = query_segment

    row_size, pair_size, hidden_size = merge_bias.shape[0], pair_bias.shape[1], expand_bias.shape[0]
    row_vectors = jnp.stack(
        (merge_bias, first_gain, first_shift, shrink_bias, second_gain, second_shift)
    )
    vectors = lax.all_gather(row_vectors, "row", axis=1, tiled=True)

    def mine_of(full, axis=0):
        share = full.shape[axis] // rows
        return lax.dynamic_slice_in_dim(full, row * share, share, axis)

    bias_pair = mine_of(lax.all_gather(pair_bias, "col", axis=1, tiled=True), 1)
    bias_queries, bias_values = bias_pair[0], bias_pair[1]
    bias_hidden = mine_of(lax.all_gather(expand_bias, "col", axis=0, tiled=True)).astype(f32)
    vectors = vectors.astype(f32)

    triple = lax.all_gather(triple_weight, "col", axis=2, tiled=True)
    triple = lax.all_gather(triple, "row", axis=0, tiled=True).transpose(1, 2, 0)
    merge = lax.all_gather(merge_weight, "col", axis=0, tiled=True)
    merge = lax.all_gather(merge, "row", axis=1, tiled=True)
    expand = lax.all_gather(expand_weight, "col", axis=1, tiled=True)
    expand = lax.all_gather(expand, "row", axis=0, tiled=True).T
    shrink = lax.all_gather(shrink_weight, "col", axis=0, tiled=True)
    shrink = lax.all_gather(shrink, "row", axis=1, tiled=True)

    weight_queries, weight_keys, weight_values = (mine_of(triple[j]) for j in range(3))
    weight_merge, weight_expand, weight_shrink = mine_of(merge), mine_of(expand), mine_of(shrink)

    inputs = gather_features(tokens)
    head_shape = (-1, heads, HEAD)
    queries = (nt(inputs, weight_queries) + bias_queries.astype(f32)).astype(bf16)
    keys = nt(inputs, weight_keys).astype(bf16)
    values = (nt(inputs, weight_values) + bias_values.astype(f32)).astype(bf16)
    all_keys, all_values = keys, values
    queries_heads = queries.reshape(head_shape)
    keys_heads, values_heads = all_keys.reshape(head_shape), all_values.reshape(head_shape)
    attended, lse = attention_forward(
        queries_heads, keys_heads, values_heads, query_segment, key_segment
    )
    attended = attended.reshape(count, -1)
    branch = sum_tokens(nn(attended, weight_merge))
    residual = own_part(inputs).astype(f32) + (branch + vectors[0])
    scaled_one, inverse_one, normed_one = norm_forward(residual, vectors[1], vectors[2])
    normed_low = gather_tokens(normed_one.astype(bf16))
    pre_gelu = nt(normed_low, weight_expand) + bias_hidden
    hidden = exact_gelu(pre_gelu).astype(bf16)
    shrunk = sum_tokens(nn(hidden, weight_shrink))
    scaled_two, inverse_two, final = norm_forward(
        normed_one + (shrunk + vectors[3]), vectors[4], vectors[5]
    )

    live = (own_part(query_segment) != 0).astype(f32)[:, None]
    upstream = to_own_tokens(cotangent).astype(f32) * live
    grad_sum_two, grad_gain_two, grad_shift_two = norm_backward(
        upstream, scaled_two, inverse_two, vectors[4]
    )
    grad_shrunk_own = grad_sum_two.astype(bf16)
    grad_shrunk = gather_tokens(grad_shrunk_own)
    grad_hidden = nt(grad_shrunk, weight_shrink)
    grad_pre = jax.vjp(exact_gelu, pre_gelu)[1](grad_hidden)[0].astype(bf16)
    grad_normed = grad_sum_two + sum_tokens(nn(grad_pre, weight_expand))
    grad_res, grad_gain_one, grad_shift_one = norm_backward(
        grad_normed, scaled_one, inverse_one, vectors[1]
    )
    grad_branch_own = grad_res.astype(bf16)
    grad_branch = gather_tokens(grad_branch_own)
    grad_attended = nt(grad_branch, weight_merge).astype(bf16)
    late_out, late_res, grad_attended = lax.optimization_barrier(
        (final.astype(bf16), grad_res, grad_attended)
    )
    layer_out, grad_res_columns = to_own_features(late_out), to_own_features(late_res)
    grad_queries, grad_keys, grad_values = attention_backward(
        queries_heads,
        keys_heads,
        values_heads,
        query_segment,
        key_segment,
        lse,
        grad_attended.reshape(head_shape),
    )
    grad_queries = grad_queries.reshape(count, -1)
    grad_keys_values = jnp.concatenate(
        (grad_keys.reshape(-1, heads * HEAD), grad_values.reshape(-1, heads * HEAD)), 1
    )
    grad_keys_values = grad_keys_values.astype(bf16)
    grad_keys, grad_values = (
        grad_keys_values[:, : heads * HEAD],
        grad_keys_values[:, heads * HEAD :],
    )
    grad_entry = (
        nn(grad_queries, weight_queries)
        + nn(grad_keys, weight_keys)
        + nn(grad_values, weight_values)
    )
    grad_tokens = sum_features(grad_entry, grad_res_columns)

    def assemble(local, row_axis, col_axis):
        full = jnp.zeros((local.shape[0], local.shape[1] * rows, D), bf16)
        full = lax.dynamic_update_slice(
            full, local.astype(bf16), (0, row * local.shape[1], 0)
        )
        full = lax.psum_scatter(full, "row", scatter_dimension=2, tiled=True)
        full = lax.psum_scatter(full, "col", scatter_dimension=1, tiled=True)
        return lax.psum(full, ("outer", "core")).astype(f32)

    grad_triple = assemble(
        jnp.stack(
            (tn(grad_queries, inputs), tn(grad_keys, inputs), tn(grad_values, inputs))
        ),
        0,
        2,
    ).transpose(2, 0, 1)
    grad_merge = assemble(tn(attended, grad_branch)[None], 1, 0)[0]
    grad_expand = assemble(tn(grad_pre, normed_low)[None], 0, 1)[0].T
    grad_shrink = assemble(tn(hidden, grad_shrunk)[None], 1, 0)[0]

    def column_sums(values):
        return jnp.sum(values, axis=0, dtype=f32)

    sum_hidden = column_sums(grad_pre)
    sum_queries, sum_values = column_sums(grad_queries), column_sums(grad_values)
    sum_rows = jnp.stack(
        (
            column_sums(grad_branch_own),
            grad_gain_one,
            grad_shift_one,
            column_sums(grad_shrunk_own),
            grad_gain_two,
            grad_shift_two,
        )
    )
    everywhere = ("outer", "core", "col")
    row_totals = lax.psum_scatter(sum_rows, "row", scatter_dimension=1, tiled=True)
    row_totals = lax.psum(row_totals, everywhere)

    def whole(local):
        full = jnp.zeros(local.shape[:-1] + (local.shape[-1] * rows,), f32)
        full = lax.dynamic_update_slice_in_dim(full, local, row * local.shape[-1], -1)
        full = lax.psum(full, everywhere + ("row",))
        share = full.shape[-1] // cols
        return lax.dynamic_slice_in_dim(full, col * share, share, -1)

    grad_pair = whole(jnp.stack((sum_queries, sum_values)))
    grad_expand_bias = whole(sum_hidden)

    return (
        layer_out,
        grad_tokens,
        grad_triple,
        grad_pair,
        grad_merge,
        row_totals[0],
        row_totals[1],
        row_totals[2],
        grad_expand,
        grad_expand_bias,
        grad_shrink,
        row_totals[3],
        row_totals[4],
        row_totals[5],
    )


def shards(tokens, *others):
    sizes = [size(axis) for axis in ("outer", "core", "row", "col")]
    if sizes == [2, 2, 2, 4] and 2 * tokens.shape[0] == LEN:
        return layer(tokens, *others)
    return layer_anywhere(tokens, *others)


def solution(mesh):
    sizes = mesh.shape
    axes = ("outer", "core", "row", "col")
    split = Mesh(
        mesh.devices.reshape(sizes["dp"] // 2, 2, sizes["row"], sizes["col"]), axes
    )
    dp = ("outer", "core")
    activations = P(("outer", "core", "col"), "row")
    return jax.shard_map(
        shards,
        mesh=split,
        in_specs=(
            activations,
            P(dp),
            P("row", None, "col"),
            P(None, "col"),
            P("col", "row"),
            P("row"),
            P("row"),
            P("row"),
            P("row", "col"),
            P("col"),
            P("col", "row"),
            P("row"),
            P("row"),
            P("row"),
            activations,
        ),
        out_specs=(
            activations,
            activations,
            P("row", None, "col"),
            P(None, "col"),
            P("col", "row"),
            P("row"),
            P("row"),
            P("row"),
            P("row", "col"),
            P("col"),
            P("col", "row"),
            P("row"),
            P("row"),
            P("row"),
        ),
        check_vma=False,
    )
```

time: 612 us -> 451 us (0.74)
  the two profiles are of different devices: /device:TPU:0 before, /device:TPU:17 now
where the time goes in v2:
time: 451 us; the launch traced here: 443 us
  waiting for transfers between devices  182 us (40%)
  Pallas kernels  87.5 us (19%)
  starting transfers between devices  86.9 us (19%)
  other arithmetic  49.3 us (11%)
  local copies, waits for them, and re-layouts  26.5 us (6%)
  matrix products  8.14 us (2%)
    ppermute x47, waiting for transfers between devices, pair(): return lax.ppermute(values, axis, [(0, 1), (1, 0)])  102 us
    ppermute x15, waiting for transfers between devices, shift(): lax.ppermute(values, 'col', [(i, (i + step) % count) for i in range(count)])  66.6 us
    ppermute x47, starting transfers between devices, pair(): return lax.ppermute(values, axis, [(0, 1), (1, 0)])  37.9 us
    ppermute x15, starting transfers between devices, shift(): lax.ppermute(values, 'col', [(i, (i + step) % count) for i in range(count)])  29.4 us
    pallas_call x2, Pallas kernels, attend_backward(): pl.pallas_call(attend_backward_kernel, grid=(steps,), in_specs=[pl.BlockS...  18.9 us
    ppermute x4, starting transfers between devices, swap_sequences(): return lax.ppermute(values, ('core', 'col'), perm)  16.5 us
    pallas_call x2, Pallas kernels, attend_forward(): pl.pallas_call(attend_forward_kernel, grid=(steps,), in_specs=[pl.BlockSp...  13.4 us
    pallas_call x1, Pallas kernels, hidden_forward(): pl.pallas_call(hidden_forward_kernel, grid=(steps,), in_specs=[pl.BlockSp...  13.1 us
  transfers between devices with their start and end apart: 68, of which 26 were waited for; matrix products, arithmetic and copies ran while one was open for 11% of the time, Pallas kernels for 13%

profile of v2, /device:TPU:17, one launch (start us, length us, event | category | flops | bytes accessed | tf_op | source)
XLA Modules:
  0.0 443.3 jit_solution(1517619421101943849)
XLA Ops:
  13.9 5.8 %collective-permute-done.7 = bf16[512,512]{1,0:T(8,128)(2,1)S(1)} collective-permute-done((bf16[512,512]{1,0:T(8,128)(2,1)}, bf16[512,512]{1,0:T(8,128)(2,1)S(1)}, u32[]{:S(2)}, u32[]{:S(2)}) %collective-permute-start.7) | collective-permute-done | bytes 524320 | tf_op jit(solution)/shard_map/ppermute | solution.py:74
  40.6 7.2 %collective-permute-done.1 = bf16[128,1024]{1,0:T(8,128)(2,1)S(1)} collective-permute-done((bf16[128,1024]{1,0:T(8,128)(2,1)S(1)}, bf16[128,1024]{1,0:T(8,128)(2,1)S(1)}, u32[]{:S(2)}, u32[]{:S(2)}) %collective-permute-start.1) | collective-permute-done | bytes 262176 | tf_op jit(solution)/shard_map/ppermute | solution.py:37
  49.2 7.0 %collective-permute-done.14 = bf16[128,1024]{1,0:T(8,128)(2,1)S(1)} collective-permute-done((bf16[128,1024]{1,0:T(8,128)(2,1)S(1)}, bf16[128,1024]{1,0:T(8,128)(2,1)S(1)}, u32[]{:S(2)}, u32[]{:S(2)}) %collective-permute-start.14) | collective-permute-done | bytes 262176 | tf_op jit(solution)/shard_map/ppermute | solution.py:28
  67.5 6.9 %collective-permute-done.22 = bf16[512,512]{1,0:T(8,128)(2,1)} collective-permute-done((bf16[512,512]{1,0:T(8,128)(2,1)}, bf16[512,512]{1,0:T(8,128)(2,1)}, u32[]{:S(2)}, u32[]{:S(2)}) %collective-permute-start.22) | collective-permute-done | bytes 524320 | tf_op jit(solution)/shard_map/ppermute | solution.py:74
  83.7 5.5 %collective-permute-done.18 = bf16[256,1024]{1,0:T(8,128)(2,1)} collective-permute-done((bf16[256,1024]{1,0:T(8,128)(2,1)}, bf16[256,1024]{1,0:T(8,128)(2,1)}, u32[]{:S(2)}, u32[]{:S(2)}) %collective-permute-start.18) | collective-permute-done | bytes 524320 | tf_op jit(solution)/shard_map/ppermute | solution.py:37
  93.7 8.8 %collective-permute-start.25 = (bf16[256,1024]{1,0:T(8,128)(2,1)S(1)}, bf16[256,1024]{1,0:T(8,128)(2,1)S(1)}, u32[]{:S(2)}, u32[]{:S(2)}) collective-permute-start(bf16[256,1024]{1,0:T(8,128)(2,1)S(1)} %copy-done.25), channel_id=1, source_target_pairs={{0,2},{1,3},{2,0},{3,1},{4,6},{5,7},{6,4},{7,5},{8,10},{9,11},{10,... | collective-permute-start | bytes 1572872 | tf_op jit(solution)/shard_map/ppermute | solution.py:37
  105.5 6.9 %shard_map.254 = (bf16[256,512]{1,0:T(8,128)(2,1)}, f32[2,2,512]{2,1,0:T(2,128)}) custom-call(bf16[512,512]{1,0:T(8,128)(2,1)} %fusion.1.q_ref, bf16[1024,1024]{1,0:T(8,128)(2,1)} %pad_maximum_fusion.2.kv_ref, s32[1,512]{1,0:T(1,128)} %get-tuple-element.235.qs_ref, s32[1024,1]{1,0:T(8,128)} %copy.68.ks_ref), custom_call_target="tpu_custom_call" | custom-call | flops 2147483648 | bytes 4194304 | tf_op jit(solution)/shard_map/pallas_call | solution.py:272
  112.4 6.5 %shard_map.255 = (bf16[256,512]{1,0:T(8,128)(2,1)}, f32[2,2,512]{2,1,0:T(2,128)}) custom-call(bf16[512,512]{1,0:T(8,128)(2,1)} %fusion.1.q_ref, bf16[1024,1024]{1,0:T(8,128)(2,1)} %pad_maximum_fusion.2.kv_ref, s32[1,512]{1,0:T(1,128)} %get-tuple-element.235.qs_ref, s32[1024,1]{1,0:T(8,128)} %copy.68.ks_ref, f32[2,2,512]{2,1,0:T(2,128)} %get-tuple-element.108.rest_0_.lse_ref, ...), custom_call_target="tpu_custom_call" | custom-call | flops 2147483648 | bytes 4194304 | tf_op jit(solution)/shard_map/pallas_call | solution.py:272
  118.9 5.9 %collective-permute-done.25 = bf16[256,1024]{1,0:T(8,128)(2,1)S(1)} collective-permute-done((bf16[256,1024]{1,0:T(8,128)(2,1)S(1)}, bf16[256,1024]{1,0:T(8,128)(2,1)S(1)}, u32[]{:S(2)}, u32[]{:S(2)}) %collective-permute-start.25) | collective-permute-done | bytes 524320 | tf_op jit(solution)/shard_map/ppermute | solution.py:37
  127.2 12.5 %collective-permute-done.26 = bf16[256,1024]{1,0:T(8,128)(2,1)S(1)} collective-permute-done((bf16[256,1024]{1,0:T(8,128)(2,1)S(1)}, bf16[256,1024]{1,0:T(8,128)(2,1)S(1)}, u32[]{:S(2)}, u32[]{:S(2)}) %collective-permute-start.26) | collective-permute-done | bytes 524320 | tf_op jit(solution)/shard_map/ppermute | solution.py:28
  148.8 12.7 %collective-permute-done.28 = bf16[256,1024]{1,0:T(8,128)(2,1)S(1)} collective-permute-done((bf16[256,1024]{1,0:T(8,128)(2,1)S(1)}, bf16[256,1024]{1,0:T(8,128)(2,1)S(1)}, u32[]{:S(2)}, u32[]{:S(2)}) %collective-permute-start.28) | collective-permute-done | bytes 524320 | tf_op jit(solution)/shard_map/ppermute | solution.py:28
  162.6 13.1 %shard_map.256 = (bf16[2,512,1024]{2,1,0:T(8,128)(2,1)}, f32[2,512,1024]{2,1,0:T(8,128)}, f32[256,1024]{1,0:T(8,128)}, bf16[256,1024]{1,0:T(8,128)(2,1)}) custom-call(bf16[512,1024]{1,0:T(8,128)(2,1)} %pad_maximum_fusion.3.x_ref, bf16[2,4,256,1024]{3,2,1,0:T(8,128)(2,1)} %pad_maximum_fusion.own_ref, ...), custom_call_target="tpu_custom_call" | custom-call | flops 4294967296 | bytes 20971520 | tf_op jit(solution)/shard_map/pallas_call | solution.py:476
  175.9 12.7 %collective-permute-done.30 = bf16[256,1024]{1,0:T(8,128)(2,1)S(1)} collective-permute-done((bf16[256,1024]{1,0:T(8,128)(2,1)}, bf16[256,1024]{1,0:T(8,128)(2,1)S(1)}, u32[]{:S(2)}, u32[]{:S(2)}) %collective-permute-start.30) | collective-permute-done | bytes 524320 | tf_op jit(solution)/shard_map/ppermute | solution.py:28
  191.6 11.5 %collective-permute-done.31 = bf16[256,1024]{1,0:T(8,128)(2,1)S(1)} collective-permute-done((bf16[256,1024]{1,0:T(8,128)(2,1)S(1)}, bf16[256,1024]{1,0:T(8,128)(2,1)S(1)}, u32[]{:S(2)}, u32[]{:S(2)}) %collective-permute-start.31) | collective-permute-done | bytes 524320 | tf_op jit(solution)/shard_map/ppermute | solution.py:28
  204.1 11.9 %shard_map.257 = (bf16[2,512,1024]{2,1,0:T(8,128)(2,1)}, f32[4,2,256]{2,1,0:T(2,128)}, f32[256,1024]{1,0:T(8,128)}, bf16[256,1024]{1,0:T(8,128)(2,1)}) custom-call(bf16[512,1024]{1,0:T(8,128)(2,1)} %pad_maximum_fusion.4.g_ref, bf16[2,4,256,1024]{3,2,1,0:T(8,128)(2,1)} %pad_maximum_fusion.own_ref, bf16[2,4,256,1024]{3,2,1,0:T(8,128)(2,1)} %collective-permute-done.29.far_ref, ...), custom_call_target="tpu_custom_call" | custom-call | flops 4294967296 | bytes 20971520 | tf_op jit(solution)/shard_map/pallas_call | solution.py:511
  216.3 5.9 %shard_map.258 = bf16[2,4,256,1024]{3,2,1,0:T(8,128)(2,1)} custom-call(bf16[2,512,1024]{2,1,0:T(8,128)(2,1)} %get-tuple-element.136.grad_ref, bf16[2,512,1024]{2,1,0:T(8,128)(2,1)} %get-tuple-element.137.hidden_ref, bf16[512,1024]{1,0:T(8,128)(2,1)} %pad_maximum_fusion.3.x_ref, bf16[512,1024]{1,0:T(8,128)(2,1)} %pad_maximum_fusion.4.g_ref), custom_call_target="tpu_custom_call" | custom-call | flops 2147483648 | bytes 8388608 | tf_op jit(solution)/shard_map/pallas_call | solution.py:538
  222.2 4.9 %collective-permute-done.32 = bf16[256,1024]{1,0:T(8,128)(2,1)S(1)} collective-permute-done((bf16[256,1024]{1,0:T(8,128)(2,1)}, bf16[256,1024]{1,0:T(8,128)(2,1)S(1)}, u32[]{:S(2)}, u32[]{:S(2)}) %collective-permute-start.32) | collective-permute-done | bytes 524320 | tf_op jit(solution)/shard_map/ppermute | solution.py:28
  233.8 13.1 %collective-permute-done.33 = bf16[256,1024]{1,0:T(8,128)(2,1)S(1)} collective-permute-done((bf16[256,1024]{1,0:T(8,128)(2,1)S(1)}, bf16[256,1024]{1,0:T(8,128)(2,1)S(1)}, u32[]{:S(2)}, u32[]{:S(2)}) %collective-permute-start.33) | collective-permute-done | bytes 524320 | tf_op jit(solution)/shard_map/ppermute | solution.py:28
  247.0 5.5 %shard_map.259 = (bf16[256,1024]{1,0:T(8,128)(2,1)}, bf16[256,1024]{1,0:T(8,128)(2,1)}, bf16[256,1024]{1,0:T(8,128)(2,1)}, bf16[256,1024]{1,0:T(8,128)(2,1)}) custom-call(bf16[2,512,1024]{2,1,0:T(8,128)(2,1)} %get-tuple-element.136.grad_ref, bf16[2,512,1024]{2,1,0:T(8,128)(2,1)} %get-tuple-element.137.hidden_ref, bf16[512,1024]{1,0:T(8,128)(2,1)} %pad_maximum_fusion.3.x_ref, ...), custom_call_target="tpu_custom_call" | custom-call | flops 1073741824 | bytes 8388608 | tf_op jit(solution)/shard_map/pallas_call | solution.py:561
  254.2 9.3 %shard_map.260 = (bf16[256,512]{1,0:T(8,128)(2,1)}, f32[512,512]{1,0:T(8,128)}, f32[512,512]{1,0:T(8,128)}) custom-call(bf16[512,512]{1,0:T(8,128)(2,1)} %fusion.1.q_ref, bf16[1024,1024]{1,0:T(8,128)(2,1)} %pad_maximum_fusion.2.kv_ref, bf16[512,512]{1,0:T(8,128)(2,1)} %convolution_convert_fusion.g_ref, s32[1,512]{1,0:T(1,128)} %get-tuple-element.235.qs_ref, ...), custom_call_target="tpu_custom_call" | custom-call | flops 5368709120 | bytes 8388608 | tf_op jit(solution)/shard_map/pallas_call | solution.py:331
  266.7 5.8 %shard_map.261 = (f32[256,1024]{1,0:T(8,128)}, f32[256,1024]{1,0:T(8,128)}, f32[256,1024]{1,0:T(8,128)}, f32[256,1024]{1,0:T(8,128)}) custom-call(bf16[2,512,1024]{2,1,0:T(8,128)(2,1)} %get-tuple-element.136.grad_ref, bf16[2,512,1024]{2,1,0:T(8,128)(2,1)} %get-tuple-element.137.hidden_ref, bf16[512,1024]{1,0:T(8,128)(2,1)} %pad_maximum_fusion.3.x_ref, ...), custom_call_target="tpu_custom_call" | custom-call | flops 1073741824 | bytes 8388608 | tf_op jit(solution)/shard_map/pallas_call | solution.py:561
  274.6 9.6 %shard_map.262 = (bf16[256,512]{1,0:T(8,128)(2,1)}, f32[512,512]{1,0:T(8,128)}, f32[512,512]{1,0:T(8,128)}) custom-call(bf16[512,512]{1,0:T(8,128)(2,1)} %fusion.1.q_ref, bf16[1024,1024]{1,0:T(8,128)(2,1)} %pad_maximum_fusion.2.kv_ref, bf16[512,512]{1,0:T(8,128)(2,1)} %convolution_convert_fusion.g_ref, s32[1,512]{1,0:T(1,128)} %get-tuple-element.235.qs_ref, ...), custom_call_target="tpu_custom_call" | custom-call | flops 5368709120 | bytes 8388608 | tf_op jit(solution)/shard_map/pallas_call | solution.py:331
  296.9 14.7 %collective-permute-done.45.rest_0_ = bf16[256,1024]{1,0:T(8,128)(2,1)S(1)} collective-permute-done((bf16[256,1024]{1,0:T(8,128)(2,1)}, bf16[256,1024]{1,0:T(8,128)(2,1)S(1)}, u32[]{:S(2)}, u32[]{:S(2)}) %collective-permute-start.45) | collective-permute-done | bytes 524320 | tf_op jit(solution)/shard_map/ppermute | solution.py:37
  312.4 4.6 %shard_map.263 = bf16[2,4,128,1024]{3,2,1,0:T(8,128)(2,1)} custom-call(s32[1]{0:T(128)} %bitcast.65.which_ref, bf16[512,1024]{1,0:T(8,128)(2,1)} %pad_maximum_fusion.6.dkv_ref, bf16[512,512]{1,0:T(8,128)(2,1)} %copy-done.4, bf16[512,512]{1,0:T(8,128)(2,1)} %copy-done.6, bf16[512,1024]{1,0:T(8,128)(2,1)} %copy-done.2, bf16[512,1024]{1,0:T(8,128)(2,1)} %copy-done.3, ...), custom_call_target="tpu_custom_call" | custom-call | flops 1073741824 | bytes 6291456 | tf_op jit(solution)/shard_map/pallas_call | solution.py:429
  329.2 11.2 %collective-permute-done.64 = f32[3840]{0:T(1024)S(1)} collective-permute-done((f32[3840]{0:T(1024)S(1)}, f32[3840]{0:T(1024)S(1)}, u32[]{:S(2)}, u32[]{:S(2)}) %collective-permute-start.64) | collective-permute-done | bytes 15392 | tf_op jit(solution)/shard_map/ppermute | solution.py:28
  346.8 8.6 %collective-permute-done.49.rest_1_ = bf16[256,1024]{1,0:T(8,128)(2,1)S(1)} collective-permute-done((bf16[256,1024]{1,0:T(8,128)(2,1)}, bf16[256,1024]{1,0:T(8,128)(2,1)S(1)}, u32[]{:S(2)}, u32[]{:S(2)}) %collective-permute-start.49) | collective-permute-done | bytes 524320 | tf_op jit(solution)/shard_map/ppermute | solution.py:37
  356.2 4.0 shard_map.265
  362.8 7.2 %collective-permute-done.48.rest_2_ = bf16[256,1024]{1,0:T(8,128)(2,1)S(1)} collective-permute-done((bf16[256,1024]{1,0:T(8,128)(2,1)S(1)}, bf16[256,1024]{1,0:T(8,128)(2,1)S(1)}, u32[]{:S(2)}, u32[]{:S(2)}) %collective-permute-start.48) | collective-permute-done | bytes 524320 | tf_op jit(solution)/shard_map/ppermute | solution.py:37
  372.7 4.5 %shard_map.264 = (f32[128,1024]{1,0:T(8,128)}, f32[128,1024]{1,0:T(8,128)}, f32[128,1024]{1,0:T(8,128)}, f32[128,1024]{1,0:T(8,128)}) custom-call(s32[1]{0:T(128)} %bitcast.64.which_ref, bf16[512,1024]{1,0:T(8,128)(2,1)} %pad_maximum_fusion.6.dkv_ref, bf16[512,512]{1,0:T(8,128)(2,1)} %copy-done.4, bf16[512,512]{1,0:T(8,128)(2,1)} %copy-done.6, ...), custom_call_target="tpu_custom_call" | custom-call | flops 536870912 | bytes 6291456 | tf_op jit(solution)/shard_map/pallas_call | solution.py:391
  382.5 8.1 %collective-permute-start.43 = (f32[512,512]{1,0:T(8,128)S(1)}, f32[512,512]{1,0:T(8,128)S(1)}, u32[]{:S(2)}, u32[]{:S(2)}) collective-permute-start(f32[512,512]{1,0:T(8,128)S(1)} %fusion.4), channel_id=1, source_target_pairs={{0,0},{1,8},{2,2},{3,10},{8,1},{9,9},{10,3},{11,11},{4,4},{5,12},{... | collective-permute-start | bytes 3145736 | tf_op jit(solution)/shard_map/ppermute | solution.py:74
  391.4 9.0 %collective-permute-done.54 = bf16[128,1024]{1,0:T(8,128)(2,1)S(1)} collective-permute-done((bf16[128,1024]{1,0:T(8,128)(2,1)S(1)}, bf16[128,1024]{1,0:T(8,128)(2,1)S(1)}, u32[]{:S(2)}, u32[]{:S(2)}) %collective-permute-start.54) | collective-permute-done | bytes 262176 | tf_op jit(solution)/shard_map/ppermute | solution.py:37
  414.0 10.2 %collective-permute-done.58 = bf16[2,128,512]{2,1,0:T(8,128)(2,1)S(1)} collective-permute-done((bf16[2,128,512]{2,1,0:T(8,128)(2,1)S(1)}, bf16[2,128,512]{2,1,0:T(8,128)(2,1)S(1)}, u32[]{:S(2)}, u32[]{:S(2)}) %collective-permute-start.58) | collective-permute-done | bytes 262176 | tf_op jit(solution)/shard_map/ppermute | solution.py:28
  (422 shorter events, 169.8 us)
Async XLA Ops:
  4.0 17.0 %collective-permute-start = (bf16[128,512]{1,0:T(8,128)(2,1)}, bf16[128,512]{1,0:T(8,128)(2,1)S(1)}, u32[]{:S(2)}, u32[]{:S(2)}) collective-permute-start(bf16[128,512]{1,0:T(8,128)(2,1)} %fusion.11), channel_id=1, source_target_pairs={{0,4},{4,0},{1,5},{5,1},{2,6},{6,2},{3,7},{7,3},{8,12},{12,8},{9,1... | collective-permute-start | bytes 393224 | tf_op jit(solution)/shard_map/ppermute | solution.py:28
  8.5 23.7 %collective-permute-start.2 = (bf16[256,512]{1,0:T(8,128)(2,1)S(1)}, bf16[256,512]{1,0:T(8,128)(2,1)S(1)}, u32[]{:S(2)}, u32[]{:S(2)}) collective-permute-start(bf16[256,512]{1,0:T(8,128)(2,1)S(1)} %get-tuple-element.271), channel_id=1, source_target_pairs={{0,4},{4,0},{1,5},{5,1},{2,6},{6,2},{3,7},{7,3},{8,12},{12,8},{9,1... | collective-permute-start | bytes 786440 | tf_op jit(solution)/shard_map/ppermute | solution.py:28
  19.8 20.0 %collective-permute-start.8 = (bf16[512,512]{1,0:T(8,128)(2,1)S(1)}, bf16[512,512]{1,0:T(8,128)(2,1)S(1)}, u32[]{:S(2)}, u32[]{:S(2)}) collective-permute-start(bf16[512,512]{1,0:T(8,128)(2,1)S(1)} %collective-permute-done.7), channel_id=1, source_target_pairs={{0,4},{4,0},{1,5},{5,1},{2,6},{6,2},{3,7},{7,3},{8,12},{12,8},{9,1... | collective-permute-start | bytes 1572872 | tf_op jit(solution)/shard_map/ppermute | solution.py:28
  28.8 19.0 %collective-permute-start.1 = (bf16[128,1024]{1,0:T(8,128)(2,1)S(1)}, bf16[128,1024]{1,0:T(8,128)(2,1)S(1)}, u32[]{:S(2)}, u32[]{:S(2)}) collective-permute-start(bf16[128,1024]{1,0:T(8,128)(2,1)S(1)} %maximum_select_fusion.14), channel_id=1, source_target_pairs={{0,2},{1,3},{2,0},{3,1},{4,6},{5,7},{6,4},{7,5},{8,10},{9,11},{10,... | collective-permute-start | bytes 786440 | tf_op jit(solution)/shard_map/ppermute | solution.py:37
  32.2 17.0 %collective-permute-start.12 = (bf16[128,1024]{1,0:T(8,128)(2,1)S(1)}, bf16[128,1024]{1,0:T(8,128)(2,1)S(1)}, u32[]{:S(2)}, u32[]{:S(2)}) collective-permute-start(bf16[128,1024]{1,0:T(8,128)(2,1)S(1)} %maximum_select_fusion.14), channel_id=1, source_target_pairs={{0,16},{16,0},{1,17},{17,1},{2,18},{18,2},{3,19},{19,3},{4,20},{20... | collective-permute-start | bytes 786440 | tf_op jit(solution)/shard_map/ppermute | solution.py:28
  57.9 17.6 %collective-permute-start.16 = (bf16[2,4,128,1024]{3,2,1,0:T(8,128)(2,1)}, bf16[2,4,128,1024]{3,2,1,0:T(8,128)(2,1)}, u32[]{:S(2)}, u32[]{:S(2)}) collective-permute-start(bf16[2,4,128,1024]{3,2,1,0:T(8,128)(2,1)} %pad_maximum_fusion.1), channel_id=1, source_target_pairs={{0,8},{8,0},{1,9},{9,1},{2,10},{10,2},{3,11},{11,3},{4,12},{12,4},... | collective-permute-start | bytes 6291464 | tf_op jit(solution)/shard_map/ppermute | solution.py:28
  61.5 22.2 %collective-permute-start.17 = (bf16[256,1024]{1,0:T(8,128)(2,1)}, bf16[256,1024]{1,0:T(8,128)(2,1)}, u32[]{:S(2)}, u32[]{:S(2)}) collective-permute-start(bf16[256,1024]{1,0:T(8,128)(2,1)} %maximum_select_fusion.8), channel_id=1, source_target_pairs={{0,1},{1,2},{2,3},{3,0},{4,5},{5,6},{6,7},{7,4},{8,9},{9,10},{10,1... | collective-permute-start | bytes 1572872 | tf_op jit(solution)/shard_map/ppermute | solution.py:37
  65.1 24.1 %collective-permute-start.18 = (bf16[256,1024]{1,0:T(8,128)(2,1)}, bf16[256,1024]{1,0:T(8,128)(2,1)}, u32[]{:S(2)}, u32[]{:S(2)}) collective-permute-start(bf16[256,1024]{1,0:T(8,128)(2,1)} %maximum_select_fusion.8), channel_id=1, source_target_pairs={{0,3},{1,0},{2,1},{3,2},{4,7},{5,4},{6,5},{7,6},{8,11},{9,8},{10,9... | collective-permute-start | bytes 1572872 | tf_op jit(solution)/shard_map/ppermute | solution.py:37
  66.0 23.3 %collective-permute-start.19 = (bf16[256,1024]{1,0:T(8,128)(2,1)}, bf16[256,1024]{1,0:T(8,128)(2,1)}, u32[]{:S(2)}, u32[]{:S(2)}) collective-permute-start(bf16[256,1024]{1,0:T(8,128)(2,1)} %maximum_select_fusion.8), channel_id=1, source_target_pairs={{0,16},{16,0},{1,17},{17,1},{2,18},{18,2},{3,19},{19,3},{4,20},{20... | collective-permute-start | bytes 1572872 | tf_op jit(solution)/shard_map/ppermute | solution.py:28
  79.7 22.8 %collective-permute-start.20 = (bf16[512,1024]{1,0:T(8,128)(2,1)}, bf16[512,1024]{1,0:T(8,128)(2,1)}, u32[]{:S(2)}, u32[]{:S(2)}) collective-permute-start(bf16[512,1024]{1,0:T(8,128)(2,1)} %add_convert_fusion), channel_id=1, source_target_pairs={{0,8},{8,0},{1,9},{9,1},{2,10},{10,2},{3,11},{11,3},{4,12},{12,4},... | collective-permute-start | bytes 3145736 | tf_op jit(solution)/shard_map/ppermute | solution.py:28
  89.2 23.1 %collective-permute-start.21 = (bf16[256,1024]{1,0:T(8,128)(2,1)}, bf16[256,1024]{1,0:T(8,128)(2,1)}, u32[]{:S(2)}, u32[]{:S(2)}) collective-permute-start(bf16[256,1024]{1,0:T(8,128)(2,1)} %collective-permute-done.17), channel_id=1, source_target_pairs={{0,16},{16,0},{1,17},{17,1},{2,18},{18,2},{3,19},{19,3},{4,20},{20... | collective-permute-start | bytes 1572872 | tf_op jit(solution)/shard_map/ppermute | solution.py:28
  93.3 25.5 %collective-permute-start.24 = (bf16[256,1024]{1,0:T(8,128)(2,1)}, bf16[256,1024]{1,0:T(8,128)(2,1)S(1)}, u32[]{:S(2)}, u32[]{:S(2)}) collective-permute-start(bf16[256,1024]{1,0:T(8,128)(2,1)} %collective-permute-done.18), channel_id=1, source_target_pairs={{0,16},{16,0},{1,17},{17,1},{2,18},{18,2},{3,19},{19,3},{4,20},{20... | collective-permute-start | bytes 1572872 | tf_op jit(solution)/shard_map/ppermute | solution.py:28
  93.7 31.1 %collective-permute-start.25 = (bf16[256,1024]{1,0:T(8,128)(2,1)S(1)}, bf16[256,1024]{1,0:T(8,128)(2,1)S(1)}, u32[]{:S(2)}, u32[]{:S(2)}) collective-permute-start(bf16[256,1024]{1,0:T(8,128)(2,1)S(1)} %copy-done.25), channel_id=1, source_target_pairs={{0,2},{1,3},{2,0},{3,1},{4,6},{5,7},{6,4},{7,5},{8,10},{9,11},{10,... | collective-permute-start | bytes 1572872 | tf_op jit(solution)/shard_map/ppermute | solution.py:37
  229.7 17.3 %collective-permute-start.34 = (bf16[2,4,256,1024]{3,2,1,0:T(8,128)(2,1)}, bf16[2,4,256,1024]{3,2,1,0:T(8,128)(2,1)}, u32[]{:S(2)}, u32[]{:S(2)}) collective-permute-start(bf16[2,4,256,1024]{3,2,1,0:T(8,128)(2,1)} %shard_map.258), channel_id=1, source_target_pairs={{0,8},{8,0},{1,9},{9,1},{2,10},{10,2},{3,11},{11,3},{4,12},{12,4},... | collective-permute-start | bytes 12582920 | tf_op jit(solution)/shard_map/ppermute | solution.py:28
  263.5 28.5 %collective-permute-start.35 = (f32[512,512]{1,0:T(8,128)}, f32[512,512]{1,0:T(8,128)}, u32[]{:S(2)}, u32[]{:S(2)}) collective-permute-start(f32[512,512]{1,0:T(8,128)} %get-tuple-element.146), channel_id=1, source_target_pairs={{0,8},{8,0},{1,9},{9,1},{2,10},{10,2},{3,11},{11,3},{4,12},{12,4},... | collective-permute-start | bytes 3145736 | tf_op jit(solution)/shard_map/ppermute | solution.py:28
  264.6 24.1 %collective-permute-start.38 = (bf16[256,1024]{1,0:T(8,128)(2,1)S(1)}, bf16[256,1024]{1,0:T(8,128)(2,1)S(1)}, u32[]{:S(2)}, u32[]{:S(2)}) collective-permute-start(bf16[256,1024]{1,0:T(8,128)(2,1)S(1)} %copy-done.56), channel_id=1, source_target_pairs={{0,16},{16,0},{1,17},{17,1},{2,18},{18,2},{3,19},{19,3},{4,20},{20... | collective-permute-start | bytes 1572872 | tf_op jit(solution)/shard_map/ppermute | solution.py:28
  265.9 77.2 %collective-permute-start.44 = (bf16[256,1024]{1,0:T(8,128)(2,1)}, bf16[256,1024]{1,0:T(8,128)(2,1)}, u32[]{:S(2)}, u32[]{:S(2)}) collective-permute-start(bf16[256,1024]{1,0:T(8,128)(2,1)} %get-tuple-element.162), channel_id=1, source_target_pairs={{0,16},{16,0},{1,17},{17,1},{2,18},{18,2},{3,19},{19,3},{4,20},{20... | collective-permute-start | bytes 1572872 | tf_op jit(solution)/shard_map/ppermute | solution.py:28
  266.1 21.5 %collective-permute-start.41 = (bf16[256,512]{1,0:T(8,128)(2,1)S(1)}, bf16[256,512]{1,0:T(8,128)(2,1)S(1)}, u32[]{:S(2)}, u32[]{:S(2)}) collective-permute-start(bf16[256,512]{1,0:T(8,128)(2,1)S(1)} %get-tuple-element.263), channel_id=1, source_target_pairs={{0,4},{4,0},{1,5},{5,1},{2,6},{6,2},{3,7},{7,3},{8,12},{12,8},{9,1... | collective-permute-start | bytes 786440 | tf_op jit(solution)/shard_map/ppermute | solution.py:28
  287.7 74.0 %collective-permute-start.47 = (bf16[256,1024]{1,0:T(8,128)(2,1)}, bf16[256,1024]{1,0:T(8,128)(2,1)}, u32[]{:S(2)}, u32[]{:S(2)}) collective-permute-start(bf16[256,1024]{1,0:T(8,128)(2,1)} %get-tuple-element.164), channel_id=1, source_target_pairs={{0,16},{16,0},{1,17},{17,1},{2,18},{18,2},{3,19},{19,3},{4,20},{20... | collective-permute-start | bytes 1572872 | tf_op jit(solution)/shard_map/ppermute | solution.py:28
  288.7 22.9 %collective-permute-start.45 = (bf16[256,1024]{1,0:T(8,128)(2,1)}, bf16[256,1024]{1,0:T(8,128)(2,1)S(1)}, u32[]{:S(2)}, u32[]{:S(2)}) collective-permute-start(bf16[256,1024]{1,0:T(8,128)(2,1)} %add_convert_fusion.4.rest_0_), channel_id=1, source_target_pairs={{0,2},{1,3},{2,0},{3,1},{4,6},{5,7},{6,4},{7,5},{8,10},{9,11},{10,... | collective-permute-start | bytes 1572872 | tf_op jit(solution)/shard_map/ppermute | solution.py:37
  295.7 22.5 %collective-permute-start.60 = (f32[9216]{0:T(1024)S(1)}, f32[9216]{0:T(1024)S(1)}, u32[]{:S(2)}, u32[]{:S(2)}) collective-permute-start(f32[9216]{0:T(1024)S(1)} %constant_dynamic-update-slice_fusion.7), channel_id=1, source_target_pairs={{0,1},{1,0},{2,3},{3,2},{4,5},{5,4},{6,7},{7,6},{8,9},{9,8},{10,11... | collective-permute-start | bytes 110600 | tf_op jit(solution)/shard_map/ppermute | solution.py:801
  317.1 26.0 %collective-permute-start.46 = (bf16[2,4,128,1024]{3,2,1,0:T(8,128)(2,1)}, bf16[2,4,128,1024]{3,2,1,0:T(8,128)(2,1)S(1)}, u32[]{:S(2)}, u32[]{:S(2)}) collective-permute-start(bf16[2,4,128,1024]{3,2,1,0:T(8,128)(2,1)} %shard_map.263), channel_id=1, source_target_pairs={{0,8},{8,0},{1,9},{9,1},{2,10},{10,2},{3,11},{11,3},{4,12},{12,4},... | collective-permute-start | bytes 6291464 | tf_op jit(solution)/shard_map/ppermute | solution.py:28
  340.4 41.6 %collective-permute-start.40 = (f32[256,512]{1,0:T(8,128)}, f32[256,512]{1,0:T(8,128)S(1)}, u32[]{:S(2)}, u32[]{:S(2)}) collective-permute-start(f32[256,512]{1,0:T(8,128)} %get-tuple-element.249), channel_id=1, source_target_pairs={{0,4},{4,0},{1,5},{5,1},{2,6},{6,2},{3,7},{7,3},{8,12},{12,8},{9,1... | collective-permute-start | bytes 1572872 | tf_op jit(solution)/shard_map/ppermute | solution.py:28
  344.7 25.3 %collective-permute-start.48 = (bf16[256,1024]{1,0:T(8,128)(2,1)S(1)}, bf16[256,1024]{1,0:T(8,128)(2,1)S(1)}, u32[]{:S(2)}, u32[]{:S(2)}) collective-permute-start(bf16[256,1024]{1,0:T(8,128)(2,1)S(1)} %add_convert_fusion.2), channel_id=1, source_target_pairs={{0,1},{1,2},{2,3},{3,0},{4,5},{5,6},{6,7},{7,4},{8,9},{9,10},{10,1... | collective-permute-start | bytes 1572872 | tf_op jit(solution)/shard_map/ppermute | solution.py:37
  360.2 18.2 %collective-permute-start.53 = (bf16[128,1024]{1,0:T(8,128)(2,1)}, bf16[128,1024]{1,0:T(8,128)(2,1)S(1)}, u32[]{:S(2)}, u32[]{:S(2)}) collective-permute-start(bf16[128,1024]{1,0:T(8,128)(2,1)} %get-tuple-element.174), channel_id=1, source_target_pairs={{0,16},{16,0},{1,17},{17,1},{2,18},{18,2},{3,19},{19,3},{4,20},{20... | collective-permute-start | bytes 786440 | tf_op jit(solution)/shard_map/ppermute | solution.py:28
  361.7 20.2 %collective-permute-start.55 = (bf16[128,1024]{1,0:T(8,128)(2,1)}, bf16[128,1024]{1,0:T(8,128)(2,1)S(1)}, u32[]{:S(2)}, u32[]{:S(2)}) collective-permute-start(bf16[128,1024]{1,0:T(8,128)(2,1)} %get-tuple-element.178), channel_id=1, source_target_pairs={{0,16},{16,0},{1,17},{17,1},{2,18},{18,2},{3,19},{19,3},{4,20},{20... | collective-permute-start | bytes 786440 | tf_op jit(solution)/shard_map/ppermute | solution.py:28
  370.0 20.6 %collective-permute-start.50 = (bf16[128,1024]{1,0:T(8,128)(2,1)}, bf16[128,1024]{1,0:T(8,128)(2,1)S(1)}, u32[]{:S(2)}, u32[]{:S(2)}) collective-permute-start(bf16[128,1024]{1,0:T(8,128)(2,1)} %get-tuple-element.170), channel_id=1, source_target_pairs={{0,16},{16,0},{1,17},{17,1},{2,18},{18,2},{3,19},{19,3},{4,20},{20... | collective-permute-start | bytes 786440 | tf_op jit(solution)/shard_map/ppermute | solution.py:28
  379.6 20.9 %collective-permute-start.54 = (bf16[128,1024]{1,0:T(8,128)(2,1)S(1)}, bf16[128,1024]{1,0:T(8,128)(2,1)S(1)}, u32[]{:S(2)}, u32[]{:S(2)}) collective-permute-start(bf16[128,1024]{1,0:T(8,128)(2,1)S(1)} %add_convert_fusion.9), channel_id=1, source_target_pairs={{0,3},{1,0},{2,1},{3,2},{4,7},{5,4},{6,5},{7,6},{8,11},{9,8},{10,9... | collective-permute-start | bytes 786440 | tf_op jit(solution)/shard_map/ppermute | solution.py:37
  382.0 22.4 %collective-permute-start.56 = (bf16[128,1024]{1,0:T(8,128)(2,1)S(1)}, bf16[128,1024]{1,0:T(8,128)(2,1)S(1)}, u32[]{:S(2)}, u32[]{:S(2)}) collective-permute-start(bf16[128,1024]{1,0:T(8,128)(2,1)S(1)} %add_convert_fusion.8), channel_id=1, source_target_pairs={{0,1},{1,2},{2,3},{3,0},{4,5},{5,6},{6,7},{7,4},{8,9},{9,10},{10,1... | collective-permute-start | bytes 786440 | tf_op jit(solution)/shard_map/ppermute | solution.py:37
  382.5 45.4 %collective-permute-start.43 = (f32[512,512]{1,0:T(8,128)S(1)}, f32[512,512]{1,0:T(8,128)S(1)}, u32[]{:S(2)}, u32[]{:S(2)}) collective-permute-start(f32[512,512]{1,0:T(8,128)S(1)} %fusion.4), channel_id=1, source_target_pairs={{0,0},{1,8},{2,2},{3,10},{8,1},{9,9},{10,3},{11,11},{4,4},{5,12},{... | collective-permute-start | bytes 3145736 | tf_op jit(solution)/shard_map/ppermute | solution.py:74
  405.9 20.2 %collective-permute-start.66 = (bf16[2,256,512]{2,1,0:T(8,128)(2,1)S(1)}, bf16[2,256,512]{2,1,0:T(8,128)(2,1)S(1)}, u32[]{:S(2)}, u32[]{:S(2)}) collective-permute-start(bf16[2,256,512]{2,1,0:T(8,128)(2,1)S(1)} %get-tuple-element.261), channel_id=1, source_target_pairs={{0,16},{16,0},{1,17},{17,1},{2,18},{18,2},{3,19},{19,3},{4,20},{20... | collective-permute-start | bytes 1572872 | tf_op jit(solution)/shard_map/ppermute | solution.py:28
  410.4 17.4 %collective-permute-start.42 = (bf16[512,512]{1,0:T(8,128)(2,1)S(1)}, bf16[512,512]{1,0:T(8,128)(2,1)S(1)}, u32[]{:S(2)}, u32[]{:S(2)}) collective-permute-start(bf16[512,512]{1,0:T(8,128)(2,1)S(1)} %copy-done.39), channel_id=1, source_target_pairs={{0,0},{1,8},{2,2},{3,10},{8,1},{9,9},{10,3},{11,11},{4,4},{5,12},{... | collective-permute-start | bytes 1572872 | tf_op jit(solution)/shard_map/ppermute | solution.py:74
  (94 other events, 867.5 us)

commit v3 on v2

--- a/solution.py
+++ b/solution.py
@@ -32,9 +32,17 @@
     return lax.optimization_barrier((values,) + others)[0]
 
 
+def together(*arrays):
+    return lax.optimization_barrier(arrays)
+
+
 def shift(values, step):
     count = size("col")
     return lax.ppermute(values, "col", [(i, (i + step) % count) for i in range(count)])
+
+
+def across(values, bits):
+    return lax.ppermute(values, "col", [(i, i ^ bits) for i in range(size("col"))])
 
 
 def by_place(bit, own, other, axis):
@@ -137,6 +145,11 @@
         got = jnp.roll(got, partial.shape[0] // 2, axis=0)
         return own_first(jnp.where(bit == 0, low, high) + got) + addend
     return lax.psum_scatter(partial, "row", scatter_dimension=1, tiled=True) + addend
+
+
+def halves(values):
+    middle = values.shape[0] // 2
+    return values[:middle], values[middle:]
 
 
 def three_groups(triple, merge, expand, shrink):
@@ -164,6 +177,7 @@
 
 
 STEPS = (1, 3, 2)
+BACK = (2, 1, 3)
 
 
 def own_core_half(parts, pairs):
@@ -181,53 +195,22 @@
     return own_core_half(parts, pairs), parts[2], pairs[2]
 
 
-BACK = (2, 1, 3)
-
-
-def collect_outer(own, other):
-    total = own + pair(other, "core").astype(f32)
-    return total[0], total[1].astype(bf16)
-
-
-def collect_send(mates):
-    return {step: pair(mates[step], "outer") for step in BACK + (0,)}
-
-
-def collect_add(own, got, step):
-    return own[step] + got[step].astype(f32)
-
-
-def collect_rest(sums):
-    last = sums[0]
-    for step in BACK:
-        last = last + sums[step].astype(f32)
-    return last
-
-
-def collect_block(last):
+def collect_row(last):
     bit = place("row")
     half = last.shape[1] // 2
     low, high = last[:, :half].astype(bf16), last[:, half:].astype(bf16)
     mine = jnp.where(bit == 0, low, high)
     got = pair(jnp.where(bit == 0, high, low), "row")
-    block = jnp.stack((jnp.where(bit == 0, mine, got), jnp.where(bit == 0, got, mine)))
-    block = by_place(place("outer"), block[:, None], pair(block, "outer")[:, None], 1)
-    block = by_place(place("core"), block[:, :, None], pair(block, "core")[:, :, None], 2)
-    return block.astype(f32)
-
-
-def ungroup(attend, widen, narrow):
+    return jnp.stack((jnp.where(bit == 0, mine, got), jnp.where(bit == 0, got, mine)))
+
+
+def ungroup(attend):
     depth = attend.shape[-1]
     heads = attend.reshape(4, 2, 2, HEAD, depth)
     keys, values = heads[:, 0, 0], heads[:, 0, 1]
     queries, merge = heads[:, 1, 0], heads[:, 1, 1]
     triple = jnp.stack((queries, keys, values)).reshape(3, 4 * HEAD, depth).transpose(2, 0, 1)
-    return (
-        triple,
-        merge.reshape(4 * HEAD, depth),
-        widen.reshape(-1, depth).T,
-        narrow.reshape(-1, depth),
-    )
+    return triple, merge.reshape(4 * HEAD, depth)
 
 
 def flip(values, axis, bit):
@@ -248,13 +231,17 @@
     return [pl.BlockSpec(memory_space=pl.ANY) for _ in arrays]
 
 
-def attend_forward_kernel(q_ref, kv_ref, qs_ref, ks_ref, *rest):
-    out_ref, lse_ref = rest[-2:]
+def pick(near_ref, far_ref, begin):
+    part = slice(begin, begin + HEAD)
+    return jnp.concatenate((near_ref[:, part], far_ref[:, part]), 0)
+
+
+def attend_forward_kernel(q_ref, near_ref, far_ref, qs_ref, ks_ref, out_ref, lse_ref):
     same = ks_ref[...] == qs_ref[...]
     for head in range(2):
         part = slice(head * HEAD, (head + 1) * HEAD)
-        keys = kv_ref[:, 2 * head * HEAD : (2 * head + 1) * HEAD]
-        values = kv_ref[:, (2 * head + 1) * HEAD : (2 * head + 2) * HEAD]
+        keys = pick(near_ref, far_ref, 2 * head * HEAD)
+        values = pick(near_ref, far_ref, (2 * head + 1) * HEAD)
         queries = q_ref[:, part] * jnp.asarray(HEAD**-0.5, bf16)
         scores = jnp.where(same, dot(keys, queries, 1, 1), masked_score)
         top = jnp.max(scores, axis=0, keepdims=True)
@@ -265,20 +252,20 @@
         lse_ref[0, head : head + 1] = top + jnp.log(total)
 
 
-def attend_forward(queries, keys_values, query_segment, key_segment, begin, steps, *earlier):
-    tokens = queries.shape[0]
-    width = steps * 2 * HEAD
-    keys = keys_values.shape[0]
+def attend_forward(queries, near, far, query_segment, key_segment):
+    tokens, width = queries.shape
+    steps = width // (2 * HEAD)
+    block = pl.BlockSpec((tokens, 4 * HEAD), lambda i: (0, i))
     return pl.pallas_call(
         attend_forward_kernel,
         grid=(steps,),
         in_specs=[
-            pl.BlockSpec((tokens, 2 * HEAD), lambda i: (0, begin + i)),
-            pl.BlockSpec((keys, 4 * HEAD), lambda i: (0, begin + i)),
+            pl.BlockSpec((tokens, 2 * HEAD), lambda i: (0, i)),
+            block,
+            block,
             pl.BlockSpec((1, tokens), lambda i: (0, 0)),
-            pl.BlockSpec((keys, 1), lambda i: (0, 0)),
-        ]
-        + anywhere(earlier),
+            pl.BlockSpec((2 * tokens, 1), lambda i: (0, 0)),
+        ],
         out_specs=[
             pl.BlockSpec((2 * HEAD, tokens), lambda i: (i, 0)),
             pl.BlockSpec((1, 2, tokens), lambda i: (i, 0, 0)),
@@ -289,17 +276,16 @@
         ],
         compiler_params=params(),
         cost_estimate=pl.CostEstimate(
-            flops=4 * tokens * keys * width * 4,
+            flops=32 * tokens * tokens * width,
             bytes_accessed=4 << 20,
-            transcendentals=tokens * keys * width // HEAD,
+            transcendentals=2 * tokens * tokens * width // HEAD,
         ),
-    )(queries, keys_values, query_segment, key_segment, *earlier)
+    )(queries, near, far, query_segment, key_segment)
 
 
 def attend_backward_kernel(
-    q_ref, kv_ref, g_ref, qs_ref, ks_ref, lse_ref, *rest
+    q_ref, kv_ref, far_kv_ref, g_ref, qs_ref, ks_ref, lse_ref, dq_ref, near_ref, far_ref
 ):
-    dq_ref, near_ref, far_ref = rest[-3:]
     same = ks_ref[...] == qs_ref[...]
     scale = HEAD**-0.5
     near = near_ref.shape[0]
@@ -307,7 +293,8 @@
         part = slice(head * HEAD, (head + 1) * HEAD)
         key_part = slice(2 * head * HEAD, (2 * head + 1) * HEAD)
         value_part = slice((2 * head + 1) * HEAD, (2 * head + 2) * HEAD)
-        keys, values = kv_ref[:, key_part], kv_ref[:, value_part]
+        keys = pick(kv_ref, far_kv_ref, key_part.start)
+        values = pick(kv_ref, far_kv_ref, value_part.start)
         queries = q_ref[:, part] * jnp.asarray(scale, bf16)
         grad = g_ref[:, part]
         scores = jnp.where(same, dot(keys, queries, 1, 1), masked_score)
@@ -322,24 +309,23 @@
         near_ref[:, value_part], far_ref[:, value_part] = grad_values[:near], grad_values[near:]
 
 
-def attend_backward(
-    queries, keys_values, grad, query_segment, key_segment, lse, begin, steps, *earlier
-):
+def attend_backward(queries, near, far, grad, query_segment, key_segment, lse, begin, steps):
     tokens = queries.shape[0]
-    keys = keys_values.shape[0]
+    block = pl.BlockSpec((tokens, 4 * HEAD), lambda i: (0, begin + i))
+    query_block = pl.BlockSpec((tokens, 2 * HEAD), lambda i: (0, begin + i))
     key_block = pl.BlockSpec((tokens, 4 * HEAD), lambda i: (0, i))
     return pl.pallas_call(
         attend_backward_kernel,
         grid=(steps,),
         in_specs=[
-            pl.BlockSpec((tokens, 2 * HEAD), lambda i: (0, begin + i)),
-            pl.BlockSpec((keys, 4 * HEAD), lambda i: (0, begin + i)),
-            pl.BlockSpec((tokens, 2 * HEAD), lambda i: (0, begin + i)),
+            query_block,
+            block,
+            block,
+            query_block,
             pl.BlockSpec((1, tokens), lambda i: (0, 0)),
-            pl.BlockSpec((keys, 1), lambda i: (0, 0)),
-            pl.BlockSpec((1, 2, tokens), lambda i: (i, 0, 0)),
-        ]
-        + anywhere(earlier),
+            pl.BlockSpec((2 * tokens, 1), lambda i: (0, 0)),
+            pl.BlockSpec((1, 2, tokens), lambda i: (begin + i, 0, 0)),
+        ],
         out_specs=[pl.BlockSpec((2 * HEAD, tokens), lambda i: (i, 0)), key_block, key_block],
         out_shape=[
             jax.ShapeDtypeStruct((2 * HEAD * steps, tokens), bf16),
@@ -348,11 +334,11 @@
         ],
         compiler_params=params(),
         cost_estimate=pl.CostEstimate(
-            flops=10 * tokens * keys * steps * 2 * HEAD * 4,
+            flops=160 * tokens * tokens * steps * HEAD,
             bytes_accessed=8 << 20,
-            transcendentals=tokens * keys * steps * 2,
+            transcendentals=4 * tokens * tokens * steps,
         ),
-    )(queries, keys_values, grad, query_segment, key_segment, lse, *earlier)
+    )(queries, near, far, grad, query_segment, key_segment, lse)
 
 
 def attend_weights_kernel(
@@ -445,133 +431,147 @@
     )(which, dkv, dq, out_in, x, g, *earlier)
 
 
-def hidden_forward_kernel(x_ref,own_ref,far_ref,bias_ref,hidden_ref,slope_ref,keep_ref,send_ref,total):
-    step=pl.program_id(0)
-    units=own_ref.shape[2]//2
-    width=own_ref.shape[1]*units
-    @pl.when(step==0)
-    def _(): total[...]=jnp.zeros_like(total)
-    for core,ref in enumerate((own_ref,far_ref)):
-        expand=ref[0,:,:units].reshape(width,D)
-        shrink=ref[0,:,units:].reshape(width,D)
-        u=dot(x_ref[...],expand,1,1)+bias_ref[0,core:core+1]
-        normal=0.5*(1.0+lax.erf(u*(0.5**0.5)))
-        slope_ref[core]=normal+u*(jnp.exp(-0.5*u*u)*((0.5/jnp.pi)**0.5))
-        hidden=(u*normal).astype(bf16)
-        hidden_ref[core]=hidden
-        total[...]+=dot(hidden,shrink,1,0)
-    @pl.when(step==pl.num_programs(0)-1)
+SPARE = 8
+
+
+def units_of(weights):
+    units = (weights.shape[2] - SPARE) // 2
+    expand = weights[:, :, :units].reshape(-1, D)
+    shrink = weights[:, :, units : 2 * units].reshape(-1, D)
+    return expand, shrink
+
+
+def finish(total, keep_ref, send_ref):
+    @pl.when(pl.program_id(0) == pl.num_programs(0) - 1)
     def _():
-        half=total.shape[0]//2
-        keep_ref[...]=total[:half]
-        send_ref[...]=total[half:].astype(bf16)
-
-
-def hidden_forward(x,own,far,bias):
-    tokens=x.shape[0]; outer,cols,two,_=own.shape; units=two//2; pairs=2
-    steps=outer*cols//pairs; width=pairs*units; per=cols//pairs
-    block=pl.BlockSpec((1,pairs,two,D),lambda i:(i//per,i%per,0,0))
-    wide=pl.BlockSpec((2,tokens,width),lambda i:(0,0,i))
-    half=pl.BlockSpec((tokens//2,D),lambda i:(0,0))
-    return pl.pallas_call(hidden_forward_kernel,grid=(steps,),
-      in_specs=[pl.BlockSpec((tokens,D),lambda i:(0,0)),block,block,pl.BlockSpec((1,2,width),lambda i:(i,0,0))],
-      out_specs=[wide,wide,half,half],
-      out_shape=[jax.ShapeDtypeStruct((2,tokens,steps*width),bf16),jax.ShapeDtypeStruct((2,tokens,steps*width),f32),
-                 jax.ShapeDtypeStruct((tokens//2,D),f32),jax.ShapeDtypeStruct((tokens//2,D),bf16)],
-      scratch_shapes=[pltpu.VMEM((tokens,D),f32)],compiler_params=params(),
-      cost_estimate=pl.CostEstimate(flops=8*tokens*D*steps*width,bytes_accessed=20<<20,transcendentals=4*tokens*steps*width))(x,own,far,bias)
-
-
-def hidden_backward_kernel(g_ref,own_ref,far_ref,slope_ref,grad_ref,sum_ref,keep_ref,send_ref,total):
-    step=pl.program_id(0)
-    units=own_ref.shape[2]//2
-    width=own_ref.shape[1]*units
-    @pl.when(step==0)
-    def _(): total[...]=jnp.zeros_like(total)
-    for core,ref in enumerate((own_ref,far_ref)):
-        expand=ref[0,:,:units].reshape(width,D)
-        shrink=ref[0,:,units:].reshape(width,D)
-        grad=(dot(g_ref[...],shrink,1,1)*slope_ref[core]).astype(bf16)
-        grad_ref[core]=grad
-        sum_ref[0,core:core+1]=jnp.sum(grad.astype(f32),axis=0,keepdims=True)
-        total[...]+=dot(grad,expand,1,0)
-    @pl.when(step==pl.num_programs(0)-1)
+        half = total.shape[0] // 2
+        keep_ref[...] = total[:half]
+        send_ref[...] = total[half:].astype(bf16)
+
+
+def add_to(total, term):
+    @pl.when(pl.program_id(0) == 0)
     def _():
-        half=total.shape[0]//2
-        keep_ref[...]=total[:half]
-        send_ref[...]=total[half:].astype(bf16)
-
-
-def hidden_backward(g,own,far,slope):
-    tokens=g.shape[0]; outer,cols,two,_=own.shape; units=two//2; pairs=2
-    steps=outer*cols//pairs; width=pairs*units; per=cols//pairs
-    block=pl.BlockSpec((1,pairs,two,D),lambda i:(i//per,i%per,0,0))
-    wide=pl.BlockSpec((2,tokens,width),lambda i:(0,0,i))
-    half=pl.BlockSpec((tokens//2,D),lambda i:(0,0))
-    return pl.pallas_call(hidden_backward_kernel,grid=(steps,),
-      in_specs=[pl.BlockSpec((tokens,D),lambda i:(0,0)),block,block,wide],
-      out_specs=[wide,pl.BlockSpec((1,2,width),lambda i:(i,0,0)),half,half],
-      out_shape=[jax.ShapeDtypeStruct((2,tokens,steps*width),bf16),jax.ShapeDtypeStruct((steps,2,width),f32),
-                 jax.ShapeDtypeStruct((tokens//2,D),f32),jax.ShapeDtypeStruct((tokens//2,D),bf16)],
-      scratch_shapes=[pltpu.VMEM((tokens,D),f32)],compiler_params=params(),
-      cost_estimate=pl.CostEstimate(flops=8*tokens*D*steps*width,bytes_accessed=20<<20,transcendentals=0))(g,own,far,slope)
-
-
-def hidden_weights_kernel(grad_ref,hidden_ref,x_ref,g_ref,*rest):
-    out_ref=rest[-1]; add_ref=rest[0] if len(rest)>=2 else None
-    cols,two,_=out_ref.shape[-3:]; units=two//2
-    for part,(left,right) in enumerate(((grad_ref,x_ref),(hidden_ref,g_ref))):
-        rows=slice(part*units,(part+1)*units)
-        value=dot(left[0],right[...],0,0).reshape(cols,units,D)
-        if add_ref is not None: value=value+add_ref[0,:,rows].astype(f32)
-        out_ref[0,:,rows]=value.astype(out_ref.dtype)
-
-
-def hidden_weights(grad,hidden,x,g,core,begin,count,cols,kind,add=None,earlier=()):
-    tokens=x.shape[0]; width=grad.shape[2]//2; units=width//cols
-    left=pl.BlockSpec((1,tokens,width),lambda i:(core,0,begin+i))
-    full=pl.BlockSpec((tokens,D),lambda i:(0,0))
-    specs=[left,left,full,full]; args=[grad,hidden,x,g]
-    if add is not None:
-        specs.append(pl.BlockSpec((1,cols,2*units,D),lambda i:(begin+i,0,0,0))); args.append(add)
-    specs+=anywhere(earlier); args+=earlier
-    return pl.pallas_call(hidden_weights_kernel,grid=(count,),in_specs=specs,
-      out_specs=pl.BlockSpec((1,cols,2*units,D),lambda i:(i,0,0,0)),
-      out_shape=jax.ShapeDtypeStruct((count,cols,2*units,D),kind),compiler_params=params(),
-      cost_estimate=pl.CostEstimate(flops=4*tokens*D*width*count,bytes_accessed=8<<20,transcendentals=0))(*args)
-
-
-def hidden_own_kernel(grad_ref, hidden_ref, x_ref, g_ref, add_ref, *rest, cols):
-    out_refs = rest[-cols:]
-    units = out_refs[0].shape[0] // 2
+        total[...] = term
+
+    @pl.when(pl.program_id(0) > 0)
+    def _():
+        total[...] += term
+
+
+def hidden_forward_kernel(
+    x_ref, bias_ref, weights_ref, hidden_ref, slope_ref, keep_ref, send_ref, total
+):
+    expand, shrink = units_of(weights_ref[0, 0:1])
+    u = dot(x_ref[...], expand, 1, 1) + bias_ref[0]
+    normal = 0.5 * (1.0 + lax.erf(u * (0.5**0.5)))
+    slope_ref[...] = normal + u * (jnp.exp(-0.5 * u * u) * ((0.5 / jnp.pi) ** 0.5))
+    hidden = (u * normal).astype(bf16)
+    hidden_ref[...] = hidden
+    add_to(total, dot(hidden, shrink, 1, 0))
+    finish(total, keep_ref, send_ref)
+
+
+def hidden_specs(tokens, weights):
+    outer, core, cols, rows, _ = weights.shape
+    units = (rows - SPARE) // 2
+    steps, width = outer * core, cols * units
+    block = pl.BlockSpec((1, 1, cols, rows, D), lambda i: (i // core, i % core, 0, 0, 0))
+    wide = pl.BlockSpec((tokens, width), lambda i: (0, i))
+    half = pl.BlockSpec((tokens // 2, D), lambda i: (0, 0))
+    half_shapes = [
+        jax.ShapeDtypeStruct((tokens // 2, D), f32),
+        jax.ShapeDtypeStruct((tokens // 2, D), bf16),
+    ]
+    full = pl.BlockSpec((tokens, D), lambda i: (0, 0))
+    row = pl.BlockSpec((1, 1, width), lambda i: (i, 0, 0))
+    cost = pl.CostEstimate(
+        flops=4 * tokens * D * steps * width, bytes_accessed=20 << 20, transcendentals=0
+    )
+    return steps, width, block, wide, half, half_shapes, full, row, cost
+
+
+def hidden_forward(x, weights, bias):
+    tokens = x.shape[0]
+    steps, width, block, wide, half, half_shapes, full, row, cost = hidden_specs(tokens, weights)
+    shape = (tokens, steps * width)
+    return pl.pallas_call(
+        hidden_forward_kernel,
+        grid=(steps,),
+        in_specs=[full, row, block],
+        out_specs=[wide, wide, half, half],
+        out_shape=[jax.ShapeDtypeStruct(shape, bf16), jax.ShapeDtypeStruct(shape, f32)]
+        + half_shapes,
+        scratch_shapes=[pltpu.VMEM((tokens, D), f32)],
+        compiler_params=params(),
+        cost_estimate=cost,
+    )(x, bias, weights)
+
+
+def hidden_backward_kernel(
+    g_ref, slope_ref, weights_ref, grad_ref, sum_ref, keep_ref, send_ref, total
+):
+    expand, shrink = units_of(weights_ref[0, 0:1])
+    grad = (dot(g_ref[...], shrink, 1, 1) * slope_ref[...]).astype(bf16)
+    grad_ref[...] = grad
+    sum_ref[0] = jnp.sum(grad.astype(f32), axis=0, keepdims=True)
+    add_to(total, dot(grad, expand, 1, 0))
+    finish(total, keep_ref, send_ref)
+
+
+def hidden_backward(g, weights, slope):
+    tokens = g.shape[0]
+    steps, width, block, wide, half, half_shapes, full, row, cost = hidden_specs(tokens, weights)
+    return pl.pallas_call(
+        hidden_backward_kernel,
+        grid=(steps,),
+        in_specs=[full, wide, block],
+        out_specs=[wide, row, half, half],
+        out_shape=[
+            jax.ShapeDtypeStruct((tokens, steps * width), bf16),
+            jax.ShapeDtypeStruct((steps, 1, width), f32),
+        ]
+        + half_shapes,
+        scratch_shapes=[pltpu.VMEM((tokens, D), f32)],
+        compiler_params=params(),
+        cost_estimate=cost,
+    )(g, slope, weights)
+
+
+def hidden_weights_kernel(grad_ref, hidden_ref, x_ref, g_ref, sum_ref, out_ref):
+    cols, rows, _ = out_ref.shape[2:]
+    units = (rows - SPARE) // 2
     for part, (left, right) in enumerate(((grad_ref, x_ref), (hidden_ref, g_ref))):
-        rows = slice(part * units, (part + 1) * units)
-        value = dot(left[0], right[...], 0, 0).reshape(cols, units, D)
-        for step, out_ref in enumerate(out_refs):
-            term = value[step] + add_ref[0, step, rows].astype(f32)
-            out_ref[rows] = term.astype(out_ref.dtype)
-
-
-def hidden_own_weights(grad, hidden, x, g, begin, cols, kind, add, *earlier):
+        value = dot(left[...], right[...], 0, 0).reshape(cols, units, D)
+        out_ref[0, 0, :, part * units : (part + 1) * units] = value.astype(bf16)
+    first = lax.broadcasted_iota(jnp.int32, (cols, SPARE, units), 1) == 0
+    sums = jnp.where(first, sum_ref[0][:, None, :], 0.0).astype(bf16)
+    out_ref[0, 0, :, 2 * units :] = jnp.zeros((cols, SPARE, D), bf16)
+    for begin in (0, D // 2):
+        out_ref[0, 0, :, 2 * units :, begin : begin + units] = sums
+
+
+def hidden_weights(grad, hidden, x, g, sums, shape):
     tokens = x.shape[0]
-    width = grad.shape[2] // 2
-    units = width // cols
-    left = pl.BlockSpec((1, tokens, width), lambda i: (0, 0, begin))
+    outer, core, cols, rows, _ = shape
+    width = grad.shape[1] // (outer * core)
+    wide = pl.BlockSpec((tokens, width), lambda i: (0, i))
     full = pl.BlockSpec((tokens, D), lambda i: (0, 0))
     return pl.pallas_call(
-        functools.partial(hidden_own_kernel, cols=cols),
-        grid=(1,),
+        hidden_weights_kernel,
+        grid=(outer * core,),
         in_specs=[
-            left, left, full, full, pl.BlockSpec((1, cols, 2 * units, D), lambda i: (begin, 0, 0, 0))
-        ]
-        + anywhere(earlier),
-        out_specs=[pl.BlockSpec((2 * units, D), lambda i: (0, 0))] * cols,
-        out_shape=[jax.ShapeDtypeStruct((2 * units, D), kind)] * cols,
+            wide, wide, full, full, pl.BlockSpec((1, cols, width // cols), lambda i: (i, 0, 0))
+        ],
+        out_specs=pl.BlockSpec(
+            (1, 1, cols, rows, D), lambda i: (i // core, i % core, 0, 0, 0)
+        ),
+        out_shape=jax.ShapeDtypeStruct(shape, bf16),
         compiler_params=params(),
         cost_estimate=pl.CostEstimate(
-            flops=4 * tokens * D * width, bytes_accessed=8 << 20, transcendentals=0
+            flops=4 * tokens * D * grad.shape[1], bytes_accessed=16 << 20, transcendentals=0
         ),
-    )(grad, hidden, x, g, add, *earlier)
+    )(grad, hidden, x, g, sums)
 
 
 def layer(
@@ -585,7 +585,9 @@
     row, col, core, outer = place("row"), place("col"), place("core"), place("outer")
     row_size, pair_size, hidden_size = merge_bias.shape[0], pair_bias.shape[1], expand_bias.shape[0]
 
-    tokens = swap_sequences(tokens)
+    step_of = lax.optimization_barrier
+    groups = three_groups(triple_weight, merge_weight, expand_weight, shrink_weight)
+    attend_group = my_quarter(groups[0])
     row_vectors = jnp.stack(
         (merge_bias, first_gain, first_shift, shrink_bias, second_gain, second_shift)
     )
@@ -595,102 +597,113 @@
             for vector in (pair_bias[0], pair_bias[1], expand_bias)
         ]
     )
-    groups = [
-        my_quarter(group)
-        for group in three_groups(triple_weight, merge_weight, expand_weight, shrink_weight)
-    ]
-    quarter, row_vectors, column = lax.optimization_barrier(
-        (exchange_rows(groups[0]), row_vectors, column)
-    )
-    parts = {0: quarter}
-    for step in STEPS:
-        parts[step] = shift(quarter, step)
-    inputs = gather_features(tokens)
-    other_quarter = exchange_rows(jnp.concatenate((groups[1], groups[2]), 1))
-
-    half = col % 2
-    other = pair(segments.astype(f32), "core").astype(jnp.int32)
+    moved = swap_sequences(tokens)
+    quarter = exchange_rows(attend_group)
+    pair_column, hidden_column = column[:pair_size], column[pair_size:].reshape(4, -1)
+    pair_column = pair_column.reshape(2, 2, HEAD)
+    pair_column = lax.dynamic_index_in_dim(pair_column, outer, 1, keepdims=False)
+    pair_column = lax.dynamic_index_in_dim(pair_column, 1 - core, 0)
+    moved_cotangent = swap_sequences(cotangent)
+    hidden_column = lax.dynamic_index_in_dim(hidden_column, 2 * outer + core, 0)
+    v = step_of(
+        dict(
+            quarter=quarter, moved=moved, other=segments.astype(f32), rows=row_vectors, pairs=pair_column,
+            hidden=hidden_column, cot=moved_cotangent,
+        )
+    )
+
+    def beside(rows, value):
+        spare = jnp.pad(value, ((0, SPARE - 1), (0, D - value.shape[1])))
+        return jnp.concatenate((rows, spare), 0)
+
+    quarter, moved = beside(v["quarter"], v["pairs"]), v["moved"]
+    parts = {0: quarter, 1: shift(quarter, 1), 3: shift(quarter, 3)}
+    pairs = {0: pair(quarter, "outer")}
+    got_tokens = pair(moved, "row")
+    other_group = jnp.concatenate([my_quarter(group) for group in groups[1:]], 1)
+    v.update(
+        quarter=quarter, parts=parts, pairs=pairs, moved=moved, got=got_tokens, group=other_group
+    )
+    v = step_of(v)
+    parts, pairs, quarter = v["parts"], v["pairs"], v["quarter"]
+    parts[2] = shift(quarter, 2)
+    pairs[1], pairs[3] = pair(parts[1], "outer"), pair(parts[3], "outer")
+    v["inputs"] = own_first(by_place(row, v["moved"], v["got"], 1))
+    v["vectors"] = by_place(row, v["rows"], pair(v["rows"], "row"), 1)
+    v["other"] = pair(v["other"], "core")
+    v["group"] = exchange_rows(v["group"])
+    v = step_of(v)
+    parts, pairs = v["parts"], v["pairs"]
+    pairs[2] = pair(parts[2], "outer")
+    mine = beside(v["group"], v["hidden"])
+    hidden_all = lax.all_gather(mine, ("outer", "core", "col"), axis=0)
+    hidden_all = hidden_all.reshape(2, 2, cols, -1, D)
+    v = step_of(v)
+    parts, pairs = v["parts"], v["pairs"]
+    rows = 2 * HEAD
+
+    def without(group):
+        return {step: group[step][:rows] for step in range(cols)}
+
+    attend_own = own_core_half(without(parts), without(pairs))
+    v["attend_own"], v["attend_other"] = attend_own, pair(attend_own, "core")
+    bias_own = jnp.stack(
+        [group[step][rows, :HEAD] for group in (parts, pairs) for step in range(cols)]
+    ).astype(f32)
+    v["bias_own"], v["bias_other"] = bias_own, pair(bias_own, "core")
+    other = v["other"].astype(jnp.int32)
     sequence = lax.dynamic_slice_in_dim(
-        jnp.where(half == core, segments, other), (col // 2) * LEN, LEN
+        jnp.where(col % 2 == core, segments, other), (col // 2) * LEN, LEN
     ).reshape(2, count)
     query_segment = own_first(lax.dynamic_index_in_dim(sequence, core, 0, keepdims=False))
     far_segment = own_first(lax.dynamic_index_in_dim(sequence, 1 - core, 0, keepdims=False))
     key_segment = jnp.concatenate((query_segment, far_segment))
     segment_row, segment_column = query_segment[None], key_segment[:, None]
-    segment_column = jnp.broadcast_to(segment_column, (2 * count, 1))
-
-    vectors = by_place(row, row_vectors, pair(row_vectors, "row"), 1)
-    column = jnp.stack([column] + [shift(column, step) for step in range(1, cols)])
-
-    pairs = {step: pair(parts[step], "outer") for step in (0, 1, 3)}
-    parts[2], other_quarter, vectors, column, inputs, segment_column, cotangent = (
-        lax.optimization_barrier(
-            (parts[2], other_quarter, vectors, column, inputs, segment_column, cotangent)
+    vectors = v["vectors"].astype(f32)
+    v = step_of(
+        dict(
+            own=v["attend_own"], other=v["attend_other"], cot=v["cot"], inputs=v["inputs"],
+            vectors=vectors, biases=(v["bias_own"], v["bias_other"]),
         )
     )
-    pairs[2] = pair(parts[2], "outer")
-    cotangent = swap_sequences(cotangent)
-    other_parts = {0: other_quarter}
-    for step in (1, 3):
-        other_parts[step] = shift(other_quarter, step)
-    attend_own = own_core_half(parts, pairs)
-    attend_far = pair(attend_own, "core")
-    other_pairs = {0: pair(other_quarter, "outer")}
-    upstream = to_own_tokens(cotangent)
-
-    vectors = vectors.astype(f32)
-    short = pair_size // 2
-    bias_pair = column[:, : 2 * short].reshape(cols, 2, 2, HEAD)
-    bias_pair = flip(bias_pair, 2, outer).transpose(1, 2, 0, 3).reshape(2, heads, HEAD).astype(f32)
-    bias_queries = bias_pair[0].reshape(-1)
-    bias_keys_values = jnp.stack((jnp.zeros_like(bias_pair[1]), bias_pair[1]), 1).reshape(-1)
-    bias_hidden = column[:, 2 * short :].reshape(cols, 2, 2, -1)
-    bias_hidden = flip(flip(bias_hidden, 1, outer), 2, core).transpose(1, 0, 2, 3)
-    bias_hidden = bias_hidden.reshape(2 * cols // 2, 2, 2, -1).transpose(0, 2, 1, 3)
-    bias_hidden = bias_hidden.reshape(cols, 2, -1).astype(f32)
-
-    weight_keys_values = jnp.where(core == 0, attend_own, attend_far).reshape(-1, D)
-    second = jnp.where(core == 0, attend_far, attend_own).reshape(heads, 2, HEAD, D)
+    attend_own, attend_other, inputs, vectors = v["own"], v["other"], v["inputs"], v["vectors"]
+    first = jnp.where(core == 0, attend_own, attend_other)
+    second = jnp.where(core == 0, attend_other, attend_own)
+    bias_values = jnp.where(core == 0, v["biases"][0], v["biases"][1])
+    bias_keys_values = jnp.stack((jnp.zeros_like(bias_values), bias_values), 1).reshape(-1)
+    bias_queries = jnp.where(core == 0, v["biases"][1], v["biases"][0]).reshape(-1)
+    weight_keys_values = first.reshape(-1, D)
+    second = second.reshape(heads, 2, HEAD, D)
     weight_queries, weight_merge = second[:, 0].reshape(-1, D), second[:, 1].reshape(-1, D)
 
     cut = heads * HEAD // 2
     steps = heads // 4
     keys_values = (nt(inputs, weight_keys_values) + bias_keys_values).astype(bf16)
-    far_keys_values = pair(keys_values, "core")
-    queries = (nt(inputs, weight_queries) + bias_queries).astype(bf16)
-    keys_values = jnp.concatenate((keys_values, far_keys_values), 0)
-    queries, other_parts[1], other_parts[3], other_pairs[0] = lax.optimization_barrier(
-        (queries, other_parts[1], other_parts[3], other_pairs[0])
-    )
-    other_parts[2], other_quarter = lax.optimization_barrier((other_quarter, other_parts[3]))
-    other_parts[2] = shift(other_parts[2], 2)
-    other_parts[3] = other_quarter
-    for step in (1, 3):
-        other_pairs[step] = pair(other_parts[step], "outer")
-    attention = (queries, keys_values, segment_row, segment_column)
-    attended_first, lse_first = attend_forward(*attention, 0, steps)
-    attended_second, lse_second = attend_forward(
-        *attention, steps, steps, lse_first, other_pairs[1]
-    )
-    attended_first, attended_second, upstream, other_pairs[3], other_parts[2] = (
-        lax.optimization_barrier(
-            (attended_first, attended_second, upstream, other_pairs[3], other_parts[2])
-        )
-    )
-    other_pairs[2] = pair(other_parts[2], "outer")
-    attended = jnp.concatenate((attended_first, attended_second), 0)
-    branch = tn(attended, weight_merge)
-    branch = sum_tokens(branch)
+    v["far"] = pair(keys_values, "core")
+    v["queries"] = (nt(inputs, weight_queries) + bias_queries).astype(bf16)
+    v["keys_values"] = keys_values
+    v["weights"] = (weight_keys_values, weight_queries, weight_merge)
+    v = step_of(v)
+    queries = v["queries"]
+    keys_values, far_keys_values = v["keys_values"], v["far"]
+    v["attended"], v["lse"] = attend_forward(
+        queries, keys_values, far_keys_values, segment_row, segment_column
+    )
+    v["upstream"] = to_own_tokens(v["cot"])
+    v = step_of(v)
+    attended, lse = v["attended"], v["lse"]
+    queries, keys_values, far_keys_values = v["queries"], v["keys_values"], v["far"]
+    weight_keys_values, weight_queries, weight_merge = v["weights"]
+    branch = sum_tokens(tn(attended, weight_merge))
     residual = inputs[:own].astype(f32) + (branch + vectors[0])
     scaled_one, inverse_one, normed_one = norm_forward(residual, vectors[1], vectors[2])
     normed_low = gather_tokens(normed_one.astype(bf16))
-    other_parts, other_pairs, normed_one = lax.optimization_barrier(
-        (other_parts, other_pairs, normed_one)
-    )
-
-    other_own = own_core_half(other_parts, other_pairs)
-    other_far = pair(other_own, "core")
-    hidden, slope, keep, send = hidden_forward(normed_low, other_own, other_far, bias_hidden)
+    normed_low, normed_one, hidden_all = step_of((normed_low, normed_one, hidden_all))
+    units = hidden_size // 8
+    bias_hidden = hidden_all[:, :, :, 2 * units, :units].reshape(4, 1, -1).astype(f32)
+    upstream = v["upstream"]
+
+    hidden, slope, keep, send = hidden_forward(normed_low, hidden_all, bias_hidden)
     shrunk = keep + pair(send, "row").astype(f32)
     scaled_two, inverse_two, final = norm_forward(
         normed_one + (shrunk + vectors[3]), vectors[4], vectors[5]
@@ -702,105 +715,161 @@
     )
     grad_shrunk_own = grad_sum_two.astype(bf16)
     grad_shrunk = gather_tokens(grad_shrunk_own)
-    grad_pre, sum_hidden, keep, send = hidden_backward(grad_shrunk, other_own, other_far, slope)
-    got_normed = pair(send, "row")
-    part = (grad_pre, hidden, normed_low, grad_shrunk)
-    far = hidden_weights(*part, 1, 0, 2, cols, bf16)
-    grad_normed = grad_sum_two + (keep + got_normed.astype(f32))
-    grad_res, grad_gain_one, grad_shift_one = norm_backward(
-        grad_normed, scaled_one, inverse_one, vectors[1]
-    )
-    grad_branch_own = grad_res.astype(bf16)
-    grad_branch = gather_tokens(grad_branch_own)
-    far, grad_branch_own = lax.optimization_barrier((far, grad_branch_own))
-    far = pair(far, "core")
-    mates = hidden_own_weights(*part, 1, cols, bf16, far)
-    grad_branch, mates = lax.optimization_barrier((grad_branch, mates))
-    hidden_got = collect_send(mates)
-
-    grad_attended = nt(grad_branch, weight_merge, bf16)
-    shared = (queries, keys_values, grad_attended, segment_row, segment_column)
-    dq_first, near_first, far_first = attend_backward(*shared, lse_first, 0, steps)
-    late_out, late_res, far_first = lax.optimization_barrier(
-        (final.astype(bf16), grad_res, far_first)
-    )
-    far_first = pair(far_first, "core")
-    hidden_got[2], dq_first = lax.optimization_barrier((hidden_got[2], dq_first))
-    hidden_own = hidden_own_weights(*part, 0, cols, f32, far, dq_first)
-    hidden_last = {2: collect_add(hidden_own, hidden_got, 2).astype(bf16)}
-    dq_second, near_second, far_second = attend_backward(
-        *shared, lse_second, steps, steps, hidden_last[2]
-    )
-    hidden_last[2] = shift(hidden_last[2], -2)
-    far_second = pair(far_second, "core")
-    layer_out, grad_res_columns = to_own_features(late_out), to_own_features(late_res)
-    hidden_got[1], dq_second = lax.optimization_barrier((hidden_got[1], dq_second))
-    hidden_last[1] = shift(collect_add(hidden_own, hidden_got, 1).astype(bf16), -1)
-    grad_queries = jnp.concatenate((dq_first, dq_second), 0)
-    grad_keys_values = jnp.concatenate(
-        ((near_first + far_first).astype(bf16), (near_second + far_second).astype(bf16)), 1
-    )
-
-    part = (grad_keys_values, grad_queries, attended, inputs, grad_branch)
-    far = attend_far_weights((1 - core).reshape(1), *part, cols, hidden_last[2])
-    far_got = pair(far, "core")
-    grad_entry = nn(grad_keys_values, weight_keys_values) + tn(grad_queries, weight_queries)
-    grad_tokens = sum_features(grad_entry, grad_res_columns)
-    hidden_got[3], far_got = lax.optimization_barrier((hidden_got[3], far_got))
-    hidden_last[3] = shift(collect_add(hidden_own, hidden_got, 3).astype(bf16), -3)
-    which = core.reshape(1)
-    mates = attend_weights(which, *part, 1, cols, bf16, far_got, (hidden_last[1],))
-    got = collect_send(mates)
-    attend_own_sums = attend_weights(
-        which, *part, 0, cols, f32, far_got, (hidden_got[0], hidden_last[3])
-    )
-    grad_tokens, layer_out = lax.optimization_barrier((grad_tokens, layer_out))
-    layer_out, grad_tokens = swap_sequences(layer_out), swap_sequences(grad_tokens)
-    sums = {2: collect_add(attend_own_sums, got, 2)}
-    sums[2] = shift(sums[2].astype(bf16), -2)
-    hidden_last[0] = collect_add(hidden_own, hidden_got, 0)
-    hidden_rest = collect_rest(hidden_last)
-    got[1], hidden_rest = lax.optimization_barrier((got[1], hidden_rest))
-    for step in (1, 3, 0):
-        sums[step] = collect_add(attend_own_sums, got, step)
-    for step in (1, 3):
-        sums[step] = shift(sums[step].astype(bf16), -step)
-    units = hidden_size // 8
-    both = collect_block(hidden_rest)
-    widen, narrow = both[:, :, :, :units], both[:, :, :, units:]
-    attend_rest = collect_rest(sums)
-    attend = collect_block(attend_rest)
-    grad_triple, grad_merge, grad_expand, grad_shrink = ungroup(attend, widen, narrow)
-
+    grad_pre, sum_hidden, keep, send = hidden_backward(grad_shrunk, hidden_all, slope)
+    cut = heads * HEAD // 2
+    steps = heads // 4
+    spare = sum_hidden.reshape(4, cols, units)
+    v = dict(
+        grad_pre=grad_pre, hidden=hidden, normed=normed_low, g=grad_shrunk, inputs=inputs,
+        attended=attended, queries=queries, keys_values=keys_values, lse=lse,
+        far_keys_values=far_keys_values, keep=keep, send=send, sum_two=grad_sum_two,
+        scaled_one=scaled_one, inverse_one=inverse_one, final=final, shrunk_own=grad_shrunk_own,
+        sum_two_rows=(grad_gain_two, grad_shift_two), spare=spare, vectors=vectors,
+        weight_merge=weight_merge, weight_queries=weight_queries,
+        weight_keys_values=weight_keys_values,
+    )
+
+    v = step_of(v)
+    v["got"] = pair(v["send"], "row")
+    hidden_grads = hidden_weights(
+        v["grad_pre"], v["hidden"], v["normed"], v["g"], v["spare"], hidden_all.shape
+    )
+    v["hidden_grads"] = hidden_grads
+    v = step_of(v)
+    hidden_sums = lax.psum_scatter(
+        v["hidden_grads"].reshape(-1, D), ("outer", "core", "col"), scatter_dimension=0, tiled=True
+    )
+    grad_normed = v["sum_two"] + (v["keep"] + v["got"].astype(f32))
+    res, grad_gain_one, grad_shift_one = norm_backward(
+        grad_normed, v["scaled_one"], v["inverse_one"], v["vectors"][1]
+    )
+    branch_own = res.astype(bf16)
+    branch_got = pair(branch_own, "row")
     sum_rows = jnp.stack(
         (
-            jnp.sum(grad_branch_own, axis=0, dtype=f32),
+            jnp.sum(branch_own, axis=0, dtype=f32),
             grad_gain_one,
             grad_shift_one,
-            jnp.sum(grad_shrunk_own, axis=0, dtype=f32),
-            grad_gain_two,
-            grad_shift_two,
+            jnp.sum(v["shrunk_own"], axis=0, dtype=f32),
+            *v["sum_two_rows"],
         )
     )
-    sum_queries = jnp.sum(grad_queries, axis=1, dtype=f32)
-    sum_values = jnp.sum(grad_keys_values, axis=0, dtype=f32).reshape(heads, 2, HEAD)[:, 1]
+    names = (
+        "inputs", "attended", "queries", "keys_values", "far_keys_values", "lse", "final",
+        "weight_merge", "weight_queries", "weight_keys_values",
+    )
+    v = {name: v[name] for name in names}
+    v["branch"] = jnp.concatenate((branch_own, branch_got), 0)
+    v["grad_attended"] = nt(v["branch"], v["weight_merge"], bf16)
+    v["res"], v["sum_rows"] = res, sum_rows
+    v["out"] = v["final"].astype(bf16)
+    v = step_of(v)
+    shared = (
+        v["queries"], v["keys_values"], v["far_keys_values"], v["grad_attended"], segment_row,
+        segment_column, v["lse"],
+    )
+    v["second"] = attend_backward(*shared, steps, steps)
+    v["out"] = to_own_features(v["out"])
+    v = step_of(v)
+    shared = (
+        v["queries"], v["keys_values"], v["far_keys_values"], v["grad_attended"], segment_row,
+        segment_column, v["lse"],
+    )
+    v["far"] = pair(v["second"][2], "core")
+    v["first"] = attend_backward(*shared, 0, steps)
+    middle = D // 2
+    res_low, res_high = v["res"][:, :middle], v["res"][:, middle:]
+    v["res_mine"] = jnp.where(row == 0, res_low, res_high)
+    v["res_send"] = halves(jnp.where(row == 0, res_high, res_low))
+    v["res_got"] = [pair(v["res_send"][0], "row")]
+    v = step_of(v)
+    far = pair(v["first"][2], "core")
+    dkv_second = (v["second"][1] + v["far"]).astype(bf16)
+    v["grad_queries"] = jnp.concatenate((v["first"][0], v["second"][0]), 0)
+    v["entry"] = tn(v["grad_queries"], v["weight_queries"])
+    dkv_first = (v["first"][1] + far).astype(bf16)
+    v["grad_keys_values"] = jnp.concatenate((dkv_first, dkv_second), 1)
+    v = step_of(v)
+    which = core.reshape(1)
+    part = (v["grad_keys_values"], v["grad_queries"], v["attended"], v["inputs"], v["branch"])
+    v["far"] = attend_far_weights((1 - core).reshape(1), *part, cols)
+    v["res_got"].append(pair(v["res_send"][1], "row"))
+    v = step_of(v)
+    v["far"] = pair(v["far"], "core")
+    entry = v["entry"] + nn(v["grad_keys_values"], v["weight_keys_values"])
+    v["res_columns"] = by_place(row, v["res_mine"], jnp.concatenate(v["res_got"], 0), 0)
+    v["entry_keep"] = jnp.where(row == 0, entry[:, :middle], entry[:, middle:])
+    v["entry_send"] = jnp.where(row == 0, entry[:, middle:], entry[:, :middle]).astype(bf16)
+    v = step_of(v)
+    part = (v["grad_keys_values"], v["grad_queries"], v["attended"], v["inputs"], v["branch"])
+    v["mates"] = attend_weights(which, *part, 1, cols, bf16, v["far"])
+    v = step_of(v)
+    part = (v["grad_keys_values"], v["grad_queries"], v["attended"], v["inputs"], v["branch"])
+    v["got"] = {2: pair(v["mates"][2], "outer")}
+    v["entry_got"] = pair(v["entry_send"], "row")
+    v["own"] = attend_weights(which, *part, 0, cols, f32, v["far"])
+    sum_queries = jnp.sum(v["grad_queries"], axis=1, dtype=f32)
+    sum_values = jnp.sum(v["grad_keys_values"], axis=0, dtype=f32).reshape(heads, 2, HEAD)[:, 1]
     sum_pair = jnp.stack((sum_queries, sum_values.reshape(-1))).reshape(2, 2, cols, HEAD)
     sum_pair = flip(sum_pair.transpose(2, 0, 1, 3), 2, outer).reshape(cols, -1)
-    sum_hidden = sum_hidden.reshape(2, cols // 2, 2, 2, -1).transpose(1, 3, 0, 2, 4)
-    sum_hidden = flip(flip(sum_hidden.reshape(cols, 2, 2, -1), 1, outer), 2, core).reshape(cols, -1)
-    sum_columns = jnp.concatenate((sum_pair, sum_hidden), 1)
-    length = sum_columns.shape[1]
-    sum_columns = jnp.concatenate(
+    length = sum_pair.shape[1]
+    sum_pair = jnp.concatenate(
         [
-            lax.dynamic_index_in_dim(sum_columns, (col - place_of) % cols, 0, keepdims=False)
+            lax.dynamic_index_in_dim(sum_pair, (col - place_of) % cols, 0, keepdims=False)
             for place_of in range(cols)
         ]
     )
-    total = jnp.concatenate((sum_columns, sum_rows.reshape(-1)))
-    for bit in (1, 2):
-        total = total + lax.ppermute(total, "col", [(i, i ^ bit) for i in range(cols)])
-    total = total + pair(total, "core")
-    total = total + pair(total, "outer")
+    v["total"] = jnp.concatenate((sum_pair, v["sum_rows"].reshape(-1)))
+    v = step_of(v)
+
+    def to_send(sums, got, step):
+        return (sums[step] + got.astype(f32)).astype(bf16)
+
+    got = v["got"]
+    got[1], got[3] = pair(v["mates"][1], "outer"), pair(v["mates"][3], "outer")
+    v["two"] = shift(to_send(v["own"], got[2], 2), -2)
+    total = v["total"]
+    v["total"] = total + lax.ppermute(total, "col", [(i, i ^ 1) for i in range(cols)])
+    entry = jnp.roll(v["entry_got"].astype(f32), own, axis=0)
+    v["grad_tokens"] = own_first(v["entry_keep"] + entry) + v["res_columns"]
+    v = step_of(v)
+    v["one"] = to_send(v["own"], v["got"][1], 1)
+    v["three"] = to_send(v["own"], v["got"][3], 3)
+    v["hidden_sums"] = hidden_sums
+    v = step_of(v)
+    v["one"], v["three"] = shift(v["one"], -1), shift(v["three"], -3)
+    v["got"][0] = pair(v["mates"][0], "outer")
+    total = v["total"]
+    v["total"] = total + lax.ppermute(total, "col", [(i, i ^ 2) for i in range(cols)])
+    v["block"] = collect_row(v["hidden_sums"])
+    v = step_of(v)
+    attend_rest = v["own"][0] + v["got"][0].astype(f32)
+    for name in ("one", "two", "three"):
+        attend_rest = attend_rest + v[name].astype(f32)
+    v["attend"] = collect_row(attend_rest)
+    v["block_got"] = pair(v["block"], "outer")
+    v["total"] = v["total"] + pair(v["total"], "core")
+    v["grad_tokens"] = swap_sequences(v["grad_tokens"])
+    v = step_of(v)
+    v["block"] = by_place(outer, v["block"][:, None], v["block_got"][:, None], 1)
+    v = step_of(v)
+    v["attend_got"] = pair(v["attend"], "outer")
+    v["total_got"] = pair(v["total"], "outer")
+    v["block_got"] = pair(v["block"], "core")
+    v["out"] = swap_sequences(v["out"])
+    v = step_of(v)
+    total = v["total"] + v["total_got"]
+    layer_out, grad_tokens = v["out"], v["grad_tokens"]
+    attend = by_place(outer, v["attend"][:, None], v["attend_got"][:, None], 1)
+    attend_got = pair(attend, "core")
+    hidden_block = by_place(
+        core, v["block"][:, :, None], v["block_got"][:, :, None], 2
+    ).astype(f32)
+    attend = by_place(core, attend[:, :, None], attend_got[:, :, None], 2).astype(f32)
+    grad_triple, grad_merge = ungroup(attend)
+    grad_expand = hidden_block[:, :, :, :units].reshape(-1, D // 2).T
+    grad_shrink = hidden_block[:, :, :, units : 2 * units].reshape(-1, D // 2)
+    grad_expand_bias = hidden_block[:, :, :, 2 * units, :units].reshape(-1)
     mine = lax.dynamic_slice_in_dim(total, col * length, length)
     sum_rows = total[cols * length :].reshape(6, 2, row_size)
     low, high = sum_rows[:, 0].reshape(-1), sum_rows[:, 1].reshape(-1)
@@ -811,7 +880,6 @@
     grad_pair = by_place(
         row, mine[: 2 * short].reshape(2, short), got[: 2 * short].reshape(2, short), 1
     )
-    grad_expand_bias = by_place(row, mine[2 * short :], got[2 * short :], 0)
     return (
         layer_out, grad_tokens, grad_triple, grad_pair, grad_merge, totals[0], totals[1], totals[2],
         grad_expand, grad_expand_bias, grad_shrink, totals[3], totals[4], totals[5],

time: 451 us -> 410 us (0.909)
  the two profiles are of different devices: /device:TPU:17 before, /device:TPU:0 now
where the time goes in v3:
time: 410 us; the launch traced here: 402 us
  waiting for transfers between devices  164 us (40%)
  Pallas kernels  74 us (18%)
  starting transfers between devices  58.1 us (14%)
  local copies, waits for them, and re-layouts  39.9 us (10%)
  other arithmetic  36.8 us (9%)
  between operations  15.7 us (4%)
  matrix products  13.9 us (3%)
    ppermute x39, waiting for transfers between devices, pair(): return lax.ppermute(values, axis, [(0, 1), (1, 0)])  123 us
    ppermute x39, starting transfers between devices, pair(): return lax.ppermute(values, axis, [(0, 1), (1, 0)])  37.3 us
    ppermute x6, waiting for transfers between devices, shift(): lax.ppermute(values, 'col', [(i, (i + step) % count) for i in range(count)])  34 us
    pallas_call x2, Pallas kernels, attend_backward(): pl.pallas_call(attend_backward_kernel, grid=(steps,), in_specs=[query_blo...  18.8 us
    unnamed x103, local copies, waits for them, and re-layouts  15.5 us
    ppermute x6, starting transfers between devices, shift(): lax.ppermute(values, 'col', [(i, (i + step) % count) for i in range(count)])  13.3 us
    pallas_call x1, Pallas kernels, attend_forward(): pl.pallas_call(attend_forward_kernel, grid=(steps,), in_specs=[pl.BlockSp...  11.2 us
    pallas_call x1, Pallas kernels, hidden_forward(): pl.pallas_call(hidden_forward_kernel, grid=(steps,), in_specs=[full, row,...  11.1 us
  transfers between devices with their start and end apart: 53, of which 34 were waited for; matrix products, arithmetic and copies ran while one was open for 16% of the time, Pallas kernels for 13%

profile of v3, /device:TPU:0, one launch (start us, length us, event | category | flops | bytes accessed | tf_op | source)
XLA Modules:
  0.0 402.0 jit_solution(3121379545384155926)
XLA Ops:
  13.4 3.0 collective-permute-start.2
  25.2 6.4 %collective-permute-start.5 = (bf16[136,1024]{1,0:T(8,128)(2,1)S(1)}, bf16[136,1024]{1,0:T(8,128)(2,1)}, u32[]{:S(2)}, u32[]{:S(2)}) collective-permute-start(bf16[136,1024]{1,0:T(8,128)(2,1)S(1)} %fusion.12), channel_id=1, source_target_pairs={{0,1},{1,2},{2,3},{3,0},{4,5},{5,6},{6,7},{7,4},{8,9},{9,10},{10,1... | collective-permute-start | bytes 835592 | tf_op jit(solution)/shard_map/ppermute | solution.py:41
  35.0 6.3 %collective-permute-done.5 = bf16[136,1024]{1,0:T(8,128)(2,1)} collective-permute-done((bf16[136,1024]{1,0:T(8,128)(2,1)S(1)}, bf16[136,1024]{1,0:T(8,128)(2,1)}, u32[]{:S(2)}, u32[]{:S(2)}) %collective-permute-start.5) | collective-permute-done | bytes 278560 | tf_op jit(solution)/shard_map/ppermute | solution.py:41
  41.3 4.3 %collective-permute-done.6 = bf16[136,1024]{1,0:T(8,128)(2,1)} collective-permute-done((bf16[136,1024]{1,0:T(8,128)(2,1)S(1)}, bf16[136,1024]{1,0:T(8,128)(2,1)}, u32[]{:S(2)}, u32[]{:S(2)}) %collective-permute-start.6) | collective-permute-done | bytes 278560 | tf_op jit(solution)/shard_map/ppermute | solution.py:41
  57.7 3.9 collective-permute-done.10
  65.4 6.6 %collective-permute-done.13 = bf16[136,1024]{1,0:T(8,128)(2,1)S(1)} collective-permute-done((bf16[136,1024]{1,0:T(8,128)(2,1)S(1)}, bf16[136,1024]{1,0:T(8,128)(2,1)S(1)}, u32[]{:S(2)}, u32[]{:S(2)}) %collective-permute-start.13) | collective-permute-done | bytes 278560 | tf_op jit(solution)/shard_map/ppermute | solution.py:28
  95.1 11.2 %shard_map.254 = (bf16[512,512]{1,0:T(8,128)(2,1)}, f32[4,2,512]{2,1,0:T(2,128)}) custom-call(bf16[512,512]{1,0:T(8,128)(2,1)} %fusion.1.q_ref, bf16[512,1024]{1,0:T(8,128)(2,1)} %add_convert_fusion.near_ref.kv_ref, bf16[512,1024]{1,0:T(8,128)(2,1)} %collective-permute-done.16.far_ref.far_kv_ref, s32[1,512]{1,0:T(1,128)} %get-tuple-element.667.qs_ref, ...), custom_call_target="tpu_custom_call" | custom-call | flops 4294967296 | bytes 4194304 | tf_op jit(solution)/shard_map/pallas_call | solution.py:259
  108.9 13.2 %collective-permute-done.18 = bf16[256,1024]{1,0:T(8,128)(2,1)S(1)} collective-permute-done((bf16[256,1024]{1,0:T(8,128)(2,1)S(1)}, bf16[256,1024]{1,0:T(8,128)(2,1)S(1)}, u32[]{:S(2)}, u32[]{:S(2)}) %collective-permute-start.18) | collective-permute-done | bytes 524320 | tf_op jit(solution)/shard_map/ppermute | solution.py:28
  123.3 12.4 %collective-permute-done.19 = bf16[256,1024]{1,0:T(8,128)(2,1)S(1)} collective-permute-done((bf16[256,1024]{1,0:T(8,128)(2,1)S(1)}, bf16[256,1024]{1,0:T(8,128)(2,1)S(1)}, u32[]{:S(2)}, u32[]{:S(2)}) %collective-permute-start.19) | collective-permute-done | bytes 524320 | tf_op jit(solution)/shard_map/ppermute | solution.py:28
  136.8 3.1 all-gather.3.cloned.1.call-done
  141.2 11.1 %shard_map.255 = (bf16[512,2048]{1,0:T(8,128)(2,1)}, f32[512,2048]{1,0:T(8,128)}, f32[256,1024]{1,0:T(8,128)}, bf16[256,1024]{1,0:T(8,128)(2,1)}) custom-call(bf16[512,1024]{1,0:T(8,128)(2,1)} %pad_maximum_fusion.1.x_ref, f32[4,1,512]{2,1,0:T(1,128)} %convert.10.bias_ref, bf16[2,2,4,264,1024]{4,3,2,1,0:T(8,128)(2,1)} %bitcast.221), custom_call_target="tpu_custom_call" | custom-call | flops 4294967296 | bytes 20971520 | tf_op jit(solution)/shard_map/pallas_call | solution.py:498
  153.9 12.8 %collective-permute-done.20 = bf16[256,1024]{1,0:T(8,128)(2,1)S(1)} collective-permute-done((bf16[256,1024]{1,0:T(8,128)(2,1)}, bf16[256,1024]{1,0:T(8,128)(2,1)S(1)}, u32[]{:S(2)}, u32[]{:S(2)}) %collective-permute-start.20) | collective-permute-done | bytes 524320 | tf_op jit(solution)/shard_map/ppermute | solution.py:28
  171.1 11.5 %collective-permute-done.21 = bf16[256,1024]{1,0:T(8,128)(2,1)S(1)} collective-permute-done((bf16[256,1024]{1,0:T(8,128)(2,1)S(1)}, bf16[256,1024]{1,0:T(8,128)(2,1)S(1)}, u32[]{:S(2)}, u32[]{:S(2)}) %collective-permute-start.21) | collective-permute-done | bytes 524320 | tf_op jit(solution)/shard_map/ppermute | solution.py:28
  183.7 10.4 %shard_map.256 = (bf16[512,2048]{1,0:T(8,128)(2,1)}, f32[4,1,512]{2,1,0:T(1,128)}, f32[256,1024]{1,0:T(8,128)}, bf16[256,1024]{1,0:T(8,128)(2,1)}) custom-call(bf16[512,1024]{1,0:T(8,128)(2,1)} %pad_maximum_fusion.2.g_ref, f32[512,2048]{1,0:T(8,128)} %get-tuple-element.377.slope_ref, bf16[2,2,4,264,1024]{4,3,2,1,0:T(8,128)(2,1)} %bitcast.222), custom_call_target="tpu_custom_call" | custom-call | flops 4294967296 | bytes 20971520 | tf_op jit(solution)/shard_map/pallas_call | solution.py:525
  195.7 9.4 %shard_map.257 = bf16[2,2,4,264,1024]{4,3,2,1,0:T(8,128)(2,1)} custom-call(bf16[512,2048]{1,0:T(8,128)(2,1)} %get-tuple-element.393.grad_ref, bf16[512,2048]{1,0:T(8,128)(2,1)} %get-tuple-element.394.hidden_ref, bf16[512,1024]{1,0:T(8,128)(2,1)} %pad_maximum_fusion.1.x_ref, bf16[512,1024]{1,0:T(8,128)(2,1)} %pad_maximum_fusion.2.g_ref, f32[4,4,128]{2,1,0:T(4,128)} %bitcast.223), custom_call_target="tpu_custom_call" | custom-call | flops 4294967296 | bytes 16777216 | tf_op jit(solution)/shard_map/pallas_call | solution.py:560
  211.6 10.1 %collective-permute-done.23 = bf16[256,1024]{1,0:T(8,128)(2,1)} collective-permute-done((bf16[256,1024]{1,0:T(8,128)(2,1)}, bf16[256,1024]{1,0:T(8,128)(2,1)}, u32[]{:S(2)}, u32[]{:S(2)}) %collective-permute-start.23) | collective-permute-done | bytes 524320 | tf_op jit(solution)/shard_map/ppermute | solution.py:28
  228.5 9.5 %shard_map.258 = (bf16[256,512]{1,0:T(8,128)(2,1)}, f32[512,512]{1,0:T(8,128)}, f32[512,512]{1,0:T(8,128)}) custom-call(bf16[512,512]{1,0:T(8,128)(2,1)} %fusion.1.q_ref, bf16[512,1024]{1,0:T(8,128)(2,1)} %add_convert_fusion.near_ref.kv_ref, bf16[512,1024]{1,0:T(8,128)(2,1)} %collective-permute-done.16.far_ref.far_kv_ref, ...), custom_call_target="tpu_custom_call" | custom-call | flops 5368709120 | bytes 8388608 | tf_op jit(solution)/shard_map/pallas_call | solution.py:317
  240.5 9.3 %shard_map.259 = (bf16[256,512]{1,0:T(8,128)(2,1)}, f32[512,512]{1,0:T(8,128)}, f32[512,512]{1,0:T(8,128)}) custom-call(bf16[512,512]{1,0:T(8,128)(2,1)} %fusion.1.q_ref, bf16[512,1024]{1,0:T(8,128)(2,1)} %add_convert_fusion.near_ref.kv_ref, bf16[512,1024]{1,0:T(8,128)(2,1)} %collective-permute-done.16.far_ref.far_kv_ref, ...), custom_call_target="tpu_custom_call" | custom-call | flops 5368709120 | bytes 8388608 | tf_op jit(solution)/shard_map/pallas_call | solution.py:317
  256.5 4.4 %shard_map.260 = bf16[2,4,128,1024]{3,2,1,0:T(8,128)(2,1)} custom-call(s32[1]{0:T(128)} %bitcast.61.which_ref, bf16[512,1024]{1,0:T(8,128)(2,1)} %pad_maximum_fusion.4.dkv_ref, bf16[512,512]{1,0:T(8,128)(2,1)} %copy-done.5, bf16[512,512]{1,0:T(8,128)(2,1)} %get-tuple-element.522.out_in_ref, bf16[512,1024]{1,0:T(8,128)(2,1)} %copy-done.4, ...), custom_call_target="tpu_custom_call" | custom-call | flops 1073741824 | bytes 6291456 | tf_op jit(solution)/shard_map/pallas_call | solution.py:415
  266.1 3.5 convolution_add_fusion
  272.9 4.4 %shard_map.261 = (bf16[128,1024]{1,0:T(8,128)(2,1)}, bf16[128,1024]{1,0:T(8,128)(2,1)}, bf16[128,1024]{1,0:T(8,128)(2,1)}, bf16[128,1024]{1,0:T(8,128)(2,1)}) custom-call(s32[1]{0:T(128)} %bitcast.62.which_ref, bf16[512,1024]{1,0:T(8,128)(2,1)} %pad_maximum_fusion.4.dkv_ref, bf16[512,512]{1,0:T(8,128)(2,1)} %copy-done.5, ...), custom_call_target="tpu_custom_call" | custom-call | flops 536870912 | bytes 6291456 | tf_op jit(solution)/shard_map/pallas_call | solution.py:377
  280.0 4.3 %shard_map.262 = (f32[128,1024]{1,0:T(8,128)}, f32[128,1024]{1,0:T(8,128)}, f32[128,1024]{1,0:T(8,128)}, f32[128,1024]{1,0:T(8,128)}) custom-call(s32[1]{0:T(128)} %bitcast.62.which_ref, bf16[512,1024]{1,0:T(8,128)(2,1)} %pad_maximum_fusion.4.dkv_ref, bf16[512,512]{1,0:T(8,128)(2,1)} %copy-done.5, bf16[512,512]{1,0:T(8,128)(2,1)} %get-tuple-element.522.out_in_ref, ...), custom_call_target="tpu_custom_call" | custom-call | flops 536870912 | bytes 6291456 | tf_op jit(solution)/shard_map/pallas_call | solution.py:377
  284.3 3.2 collective-permute-done.31
  287.5 4.4 %collective-permute-done.30 = bf16[512,512]{1,0:T(8,128)(2,1)S(1)} collective-permute-done((bf16[512,512]{1,0:T(8,128)(2,1)}, bf16[512,512]{1,0:T(8,128)(2,1)S(1)}, u32[]{:S(2)}, u32[]{:S(2)}) %collective-permute-start.30) | collective-permute-done | bytes 524320 | tf_op jit(solution)/shard_map/ppermute | solution.py:28
  299.4 7.2 %collective-permute-done.32 = bf16[128,1024]{1,0:T(8,128)(2,1)S(1)} collective-permute-done((bf16[128,1024]{1,0:T(8,128)(2,1)S(1)}, bf16[128,1024]{1,0:T(8,128)(2,1)S(1)}, u32[]{:S(2)}, u32[]{:S(2)}) %collective-permute-start.32) | collective-permute-done | bytes 262176 | tf_op jit(solution)/shard_map/ppermute | solution.py:28
  306.5 4.8 %collective-permute-done.33 = bf16[128,1024]{1,0:T(8,128)(2,1)S(1)} collective-permute-done((bf16[128,1024]{1,0:T(8,128)(2,1)S(1)}, bf16[128,1024]{1,0:T(8,128)(2,1)S(1)}, u32[]{:S(2)}, u32[]{:S(2)}) %collective-permute-start.33) | collective-permute-done | bytes 262176 | tf_op jit(solution)/shard_map/ppermute | solution.py:28
  311.3 12.5 %collective-permute-done.35 = bf16[128,1024]{1,0:T(8,128)(2,1)S(1)} collective-permute-done((bf16[128,1024]{1,0:T(8,128)(2,1)S(1)}, bf16[128,1024]{1,0:T(8,128)(2,1)S(1)}, u32[]{:S(2)}, u32[]{:S(2)}) %collective-permute-start.35) | collective-permute-done | bytes 262176 | tf_op jit(solution)/shard_map/ppermute | solution.py:41
  340.0 5.8 %collective-permute-done.39 = bf16[128,1024]{1,0:T(8,128)(2,1)S(1)} collective-permute-done((bf16[128,1024]{1,0:T(8,128)(2,1)S(1)}, bf16[128,1024]{1,0:T(8,128)(2,1)S(1)}, u32[]{:S(2)}, u32[]{:S(2)}) %collective-permute-start.39) | collective-permute-done | bytes 262176 | tf_op jit(solution)/shard_map/ppermute | solution.py:41
  349.3 4.1 %collective-permute-done.41 = bf16[128,512]{1,0:T(8,128)(2,1)S(1)} collective-permute-done((bf16[128,512]{1,0:T(8,128)(2,1)S(1)}, bf16[128,512]{1,0:T(8,128)(2,1)S(1)}, u32[]{:S(2)}, u32[]{:S(2)}) %collective-permute-start.41) | collective-permute-done | bytes 131104 | tf_op jit(solution)/shard_map/ppermute | solution.py:28
  353.4 8.1 %collective-permute-done.42 = bf16[2,264,512]{2,1,0:T(8,128)(2,1)S(1)} collective-permute-done((bf16[2,264,512]{2,1,0:T(8,128)(2,1)S(1)}, bf16[2,264,512]{2,1,0:T(8,128)(2,1)S(1)}, u32[]{:S(2)}, u32[]{:S(2)}) %collective-permute-start.42) | collective-permute-done | bytes 540704 | tf_op jit(solution)/shard_map/ppermute | solution.py:28
  366.5 7.6 %collective-permute-done.48 = f32[7168]{0:T(1024)S(1)} collective-permute-done((f32[7168]{0:T(1024)S(1)}, f32[7168]{0:T(1024)S(1)}, u32[]{:S(2)}, u32[]{:S(2)}) %collective-permute-start.48) | collective-permute-done | bytes 28704 | tf_op jit(solution)/shard_map/ppermute | solution.py:28
  383.3 3.1 copy.100
  (360 shorter events, 154.5 us)
Async XLA Ops:
  7.2 132.6 %all-gather.3.cloned.1.call-start = ((), (), s32[]{:S(2)}) async-start(), calls=%async_computation.2 | async-start | bytes 9191424 | tf_op jit(solution)/shard_map/all_gather | solution.py:639
  7.2 12.3 %collective-permute-start = (bf16[512,512]{1,0:T(8,128)(2,1)}, bf16[512,512]{1,0:T(8,128)(2,1)S(1)}, u32[]{:S(2)}, u32[]{:S(2)}) collective-permute-start(bf16[512,512]{1,0:T(8,128)(2,1)} %param.29), channel_id=1, source_target_pairs={{0,0},{1,8},{2,2},{3,10},{8,1},{9,9},{10,3},{11,11},{4,4},{5,12},{... | collective-permute-start | bytes 1572872 | tf_op jit(solution)/shard_map/ppermute | solution.py:82
  9.1 10.5 %collective-permute-start.1 = (bf16[512,512]{1,0:T(8,128)(2,1)}, bf16[512,512]{1,0:T(8,128)(2,1)S(1)}, u32[]{:S(2)}, u32[]{:S(2)}) collective-permute-start(bf16[512,512]{1,0:T(8,128)(2,1)} %param.15), channel_id=1, source_target_pairs={{0,0},{1,8},{2,2},{3,10},{8,1},{9,9},{10,3},{11,11},{4,4},{5,12},{... | collective-permute-start | bytes 1572872 | tf_op jit(solution)/shard_map/ppermute | solution.py:82
  19.6 26.1 %collective-permute-start.3 = (bf16[512,512]{1,0:T(8,128)(2,1)S(1)}, bf16[512,512]{1,0:T(8,128)(2,1)}, u32[]{:S(2)}, u32[]{:S(2)}) collective-permute-start(bf16[512,512]{1,0:T(8,128)(2,1)S(1)} %collective-permute-done.1), channel_id=1, source_target_pairs={{0,4},{4,0},{1,5},{5,1},{2,6},{6,2},{3,7},{7,3},{8,12},{12,8},{9,1... | collective-permute-start | bytes 1572872 | tf_op jit(solution)/shard_map/ppermute | solution.py:28
  23.6 11.3 %collective-permute-start.4 = (bf16[136,1024]{1,0:T(8,128)(2,1)S(1)}, bf16[136,1024]{1,0:T(8,128)(2,1)}, u32[]{:S(2)}, u32[]{:S(2)}) collective-permute-start(bf16[136,1024]{1,0:T(8,128)(2,1)S(1)} %fusion.12), channel_id=1, source_target_pairs={{0,16},{16,0},{1,17},{17,1},{2,18},{18,2},{3,19},{19,3},{4,20},{20... | collective-permute-start | bytes 835592 | tf_op jit(solution)/shard_map/ppermute | solution.py:28
  25.2 16.1 %collective-permute-start.5 = (bf16[136,1024]{1,0:T(8,128)(2,1)S(1)}, bf16[136,1024]{1,0:T(8,128)(2,1)}, u32[]{:S(2)}, u32[]{:S(2)}) collective-permute-start(bf16[136,1024]{1,0:T(8,128)(2,1)S(1)} %fusion.12), channel_id=1, source_target_pairs={{0,1},{1,2},{2,3},{3,0},{4,5},{5,6},{6,7},{7,4},{8,9},{9,10},{10,1... | collective-permute-start | bytes 835592 | tf_op jit(solution)/shard_map/ppermute | solution.py:41
  31.6 14.0 %collective-permute-start.6 = (bf16[136,1024]{1,0:T(8,128)(2,1)S(1)}, bf16[136,1024]{1,0:T(8,128)(2,1)}, u32[]{:S(2)}, u32[]{:S(2)}) collective-permute-start(bf16[136,1024]{1,0:T(8,128)(2,1)S(1)} %fusion.12), channel_id=1, source_target_pairs={{0,3},{1,0},{2,1},{3,2},{4,7},{5,4},{6,5},{7,6},{8,11},{9,8},{10,9... | collective-permute-start | bytes 835592 | tf_op jit(solution)/shard_map/ppermute | solution.py:41
  45.7 9.2 %collective-permute-start.7 = (bf16[256,512]{1,0:T(8,128)(2,1)S(1)}, bf16[256,512]{1,0:T(8,128)(2,1)S(1)}, u32[]{:S(2)}, u32[]{:S(2)}) collective-permute-start(bf16[256,512]{1,0:T(8,128)(2,1)S(1)} %get-tuple-element.701), channel_id=1, source_target_pairs={{0,4},{4,0},{1,5},{5,1},{2,6},{6,2},{3,7},{7,3},{8,12},{12,8},{9,1... | collective-permute-start | bytes 786440 | tf_op jit(solution)/shard_map/ppermute | solution.py:28
  47.9 9.9 %collective-permute-start.9 = (bf16[136,1024]{1,0:T(8,128)(2,1)}, bf16[136,1024]{1,0:T(8,128)(2,1)S(1)}, u32[]{:S(2)}, u32[]{:S(2)}) collective-permute-start(bf16[136,1024]{1,0:T(8,128)(2,1)} %collective-permute-done.5), channel_id=1, source_target_pairs={{0,16},{16,0},{1,17},{17,1},{2,18},{18,2},{3,19},{19,3},{4,20},{20... | collective-permute-start | bytes 835592 | tf_op jit(solution)/shard_map/ppermute | solution.py:28
  48.5 13.2 %collective-permute-start.10 = (bf16[136,1024]{1,0:T(8,128)(2,1)}, bf16[136,1024]{1,0:T(8,128)(2,1)S(1)}, u32[]{:S(2)}, u32[]{:S(2)}) collective-permute-start(bf16[136,1024]{1,0:T(8,128)(2,1)} %collective-permute-done.6), channel_id=1, source_target_pairs={{0,16},{16,0},{1,17},{17,1},{2,18},{18,2},{3,19},{19,3},{4,20},{20... | collective-permute-start | bytes 835592 | tf_op jit(solution)/shard_map/ppermute | solution.py:28
  49.9 13.9 %collective-permute-start.11 = (bf16[136,1024]{1,0:T(8,128)(2,1)S(1)}, bf16[136,1024]{1,0:T(8,128)(2,1)S(1)}, u32[]{:S(2)}, u32[]{:S(2)}) collective-permute-start(bf16[136,1024]{1,0:T(8,128)(2,1)S(1)} %fusion.12), channel_id=1, source_target_pairs={{0,2},{1,3},{2,0},{3,1},{4,6},{5,7},{6,4},{7,5},{8,10},{9,11},{10,... | collective-permute-start | bytes 835592 | tf_op jit(solution)/shard_map/ppermute | solution.py:41
  64.7 261.7 %reduce-scatter.2.cloned.1.call-start = ((), (), s32[]{:S(2)}) async-start(), calls=%async_computation.1 | async-start | bytes 9191424 | tf_op jit(solution)/shard_map/reduce_scatter | solution.py:739
  93.5 12.8 %collective-permute-start.17 = (bf16[256,512]{1,0:T(8,128)(2,1)S(1)}, bf16[256,512]{1,0:T(8,128)(2,1)S(1)}, u32[]{:S(2)}, u32[]{:S(2)}) collective-permute-start(bf16[256,512]{1,0:T(8,128)(2,1)S(1)} %get-tuple-element.697), channel_id=1, source_target_pairs={{0,4},{4,0},{1,5},{5,1},{2,6},{6,2},{3,7},{7,3},{8,12},{12,8},{9,1... | collective-permute-start | bytes 786440 | tf_op jit(solution)/shard_map/ppermute | solution.py:28
  108.3 13.8 %collective-permute-start.18 = (bf16[256,1024]{1,0:T(8,128)(2,1)S(1)}, bf16[256,1024]{1,0:T(8,128)(2,1)S(1)}, u32[]{:S(2)}, u32[]{:S(2)}) collective-permute-start(bf16[256,1024]{1,0:T(8,128)(2,1)S(1)} %slice.511), channel_id=1, source_target_pairs={{0,4},{4,0},{1,5},{5,1},{2,6},{6,2},{3,7},{7,3},{8,12},{12,8},{9,1... | collective-permute-start | bytes 1572872 | tf_op jit(solution)/shard_map/ppermute | solution.py:28
  122.7 13.0 %collective-permute-start.19 = (bf16[256,1024]{1,0:T(8,128)(2,1)S(1)}, bf16[256,1024]{1,0:T(8,128)(2,1)S(1)}, u32[]{:S(2)}, u32[]{:S(2)}) collective-permute-start(bf16[256,1024]{1,0:T(8,128)(2,1)S(1)} %get-tuple-element.663), channel_id=1, source_target_pairs={{0,4},{4,0},{1,5},{5,1},{2,6},{6,2},{3,7},{7,3},{8,12},{12,8},{9,1... | collective-permute-start | bytes 1572872 | tf_op jit(solution)/shard_map/ppermute | solution.py:28
  152.3 14.4 %collective-permute-start.20 = (bf16[256,1024]{1,0:T(8,128)(2,1)}, bf16[256,1024]{1,0:T(8,128)(2,1)S(1)}, u32[]{:S(2)}, u32[]{:S(2)}) collective-permute-start(bf16[256,1024]{1,0:T(8,128)(2,1)} %get-tuple-element.375), channel_id=1, source_target_pairs={{0,4},{4,0},{1,5},{5,1},{2,6},{6,2},{3,7},{7,3},{8,12},{12,8},{9,1... | collective-permute-start | bytes 1572872 | tf_op jit(solution)/shard_map/ppermute | solution.py:28
  169.3 13.3 %collective-permute-start.21 = (bf16[256,1024]{1,0:T(8,128)(2,1)S(1)}, bf16[256,1024]{1,0:T(8,128)(2,1)S(1)}, u32[]{:S(2)}, u32[]{:S(2)}) collective-permute-start(bf16[256,1024]{1,0:T(8,128)(2,1)S(1)} %get-tuple-element.426), channel_id=1, source_target_pairs={{0,4},{4,0},{1,5},{5,1},{2,6},{6,2},{3,7},{7,3},{8,12},{12,8},{9,1... | collective-permute-start | bytes 1572872 | tf_op jit(solution)/shard_map/ppermute | solution.py:28
  194.1 12.7 %collective-permute-start.22 = (bf16[256,1024]{1,0:T(8,128)(2,1)}, bf16[256,1024]{1,0:T(8,128)(2,1)}, u32[]{:S(2)}, u32[]{:S(2)}) collective-permute-start(bf16[256,1024]{1,0:T(8,128)(2,1)} %get-tuple-element.392), channel_id=1, source_target_pairs={{0,4},{4,0},{1,5},{5,1},{2,6},{6,2},{3,7},{7,3},{8,12},{12,8},{9,1... | collective-permute-start | bytes 1572872 | tf_op jit(solution)/shard_map/ppermute | solution.py:28
  209.9 11.7 %collective-permute-start.23 = (bf16[256,1024]{1,0:T(8,128)(2,1)}, bf16[256,1024]{1,0:T(8,128)(2,1)}, u32[]{:S(2)}, u32[]{:S(2)}) collective-permute-start(bf16[256,1024]{1,0:T(8,128)(2,1)} %get-tuple-element.657), channel_id=1, source_target_pairs={{0,4},{4,0},{1,5},{5,1},{2,6},{6,2},{3,7},{7,3},{8,12},{12,8},{9,1... | collective-permute-start | bytes 1572872 | tf_op jit(solution)/shard_map/ppermute | solution.py:28
  226.8 11.2 %collective-permute-start.24 = (bf16[256,512]{1,0:T(8,128)(2,1)S(1)}, bf16[256,512]{1,0:T(8,128)(2,1)S(1)}, u32[]{:S(2)}, u32[]{:S(2)}) collective-permute-start(bf16[256,512]{1,0:T(8,128)(2,1)S(1)} %get-tuple-element.695), channel_id=1, source_target_pairs={{0,4},{4,0},{1,5},{5,1},{2,6},{6,2},{3,7},{7,3},{8,12},{12,8},{9,1... | collective-permute-start | bytes 786440 | tf_op jit(solution)/shard_map/ppermute | solution.py:28
  239.1 10.8 %collective-permute-start.25 = (f32[512,512]{1,0:T(8,128)}, f32[512,512]{1,0:T(8,128)S(1)}, u32[]{:S(2)}, u32[]{:S(2)}) collective-permute-start(f32[512,512]{1,0:T(8,128)} %get-tuple-element.449), channel_id=1, source_target_pairs={{0,8},{8,0},{1,9},{9,1},{2,10},{10,2},{3,11},{11,3},{4,12},{12,4},... | collective-permute-start | bytes 3145736 | tf_op jit(solution)/shard_map/ppermute | solution.py:28
  240.0 9.8 %collective-permute-start.26 = (f32[128,512]{1,0:T(8,128)S(1)}, f32[128,512]{1,0:T(8,128)S(1)}, u32[]{:S(2)}, u32[]{:S(2)}) collective-permute-start(f32[128,512]{1,0:T(8,128)S(1)} %get-tuple-element.693), channel_id=1, source_target_pairs={{0,4},{4,0},{1,5},{5,1},{2,6},{6,2},{3,7},{7,3},{8,12},{12,8},{9,1... | collective-permute-start | bytes 786440 | tf_op jit(solution)/shard_map/ppermute | solution.py:28
  277.4 14.6 %collective-permute-start.30 = (bf16[512,512]{1,0:T(8,128)(2,1)}, bf16[512,512]{1,0:T(8,128)(2,1)S(1)}, u32[]{:S(2)}, u32[]{:S(2)}) collective-permute-start(bf16[512,512]{1,0:T(8,128)(2,1)} %select_convert_fusion), channel_id=1, source_target_pairs={{0,4},{4,0},{1,5},{5,1},{2,6},{6,2},{3,7},{7,3},{8,12},{12,8},{9,1... | collective-permute-start | bytes 1572872 | tf_op jit(solution)/shard_map/ppermute | solution.py:28
  291.9 14.6 %collective-permute-start.32 = (bf16[128,1024]{1,0:T(8,128)(2,1)S(1)}, bf16[128,1024]{1,0:T(8,128)(2,1)S(1)}, u32[]{:S(2)}, u32[]{:S(2)}) collective-permute-start(bf16[128,1024]{1,0:T(8,128)(2,1)S(1)} %copy-done.45), channel_id=1, source_target_pairs={{0,16},{16,0},{1,17},{17,1},{2,18},{18,2},{3,19},{19,3},{4,20},{20... | collective-permute-start | bytes 786440 | tf_op jit(solution)/shard_map/ppermute | solution.py:28
  292.6 18.7 %collective-permute-start.33 = (bf16[128,1024]{1,0:T(8,128)(2,1)S(1)}, bf16[128,1024]{1,0:T(8,128)(2,1)S(1)}, u32[]{:S(2)}, u32[]{:S(2)}) collective-permute-start(bf16[128,1024]{1,0:T(8,128)(2,1)S(1)} %copy-done.44), channel_id=1, source_target_pairs={{0,16},{16,0},{1,17},{17,1},{2,18},{18,2},{3,19},{19,3},{4,20},{20... | collective-permute-start | bytes 786440 | tf_op jit(solution)/shard_map/ppermute | solution.py:28
  295.8 28.0 %collective-permute-start.35 = (bf16[128,1024]{1,0:T(8,128)(2,1)S(1)}, bf16[128,1024]{1,0:T(8,128)(2,1)S(1)}, u32[]{:S(2)}, u32[]{:S(2)}) collective-permute-start(bf16[128,1024]{1,0:T(8,128)(2,1)S(1)} %add_convert_fusion.6), channel_id=1, source_target_pairs={{0,2},{1,3},{2,0},{3,1},{4,6},{5,7},{6,4},{7,5},{8,10},{9,11},{10,... | collective-permute-start | bytes 786440 | tf_op jit(solution)/shard_map/ppermute | solution.py:41
  333.6 12.2 %collective-permute-start.39 = (bf16[128,1024]{1,0:T(8,128)(2,1)S(1)}, bf16[128,1024]{1,0:T(8,128)(2,1)S(1)}, u32[]{:S(2)}, u32[]{:S(2)}) collective-permute-start(bf16[128,1024]{1,0:T(8,128)(2,1)S(1)} %add_convert_fusion.4), channel_id=1, source_target_pairs={{0,1},{1,2},{2,3},{3,0},{4,5},{5,6},{6,7},{7,4},{8,9},{9,10},{10,1... | collective-permute-start | bytes 786440 | tf_op jit(solution)/shard_map/ppermute | solution.py:41
  345.7 15.8 %collective-permute-start.43 = (f32[512,512]{1,0:T(8,128)S(1)}, f32[512,512]{1,0:T(8,128)S(1)}, u32[]{:S(2)}, u32[]{:S(2)}) collective-permute-start(f32[512,512]{1,0:T(8,128)S(1)} %fusion.5), channel_id=1, source_target_pairs={{0,0},{1,8},{2,2},{3,10},{8,1},{9,9},{10,3},{11,11},{4,4},{5,12},{... | collective-permute-start | bytes 3145736 | tf_op jit(solution)/shard_map/ppermute | solution.py:82
  346.5 15.1 %collective-permute-start.42 = (bf16[2,264,512]{2,1,0:T(8,128)(2,1)S(1)}, bf16[2,264,512]{2,1,0:T(8,128)(2,1)S(1)}, u32[]{:S(2)}, u32[]{:S(2)}) collective-permute-start(bf16[2,264,512]{2,1,0:T(8,128)(2,1)S(1)} %pad_maximum_fusion.5), channel_id=1, source_target_pairs={{0,16},{16,0},{1,17},{17,1},{2,18},{18,2},{3,19},{19,3},{4,20},{20... | collective-permute-start | bytes 1622024 | tf_op jit(solution)/shard_map/ppermute | solution.py:28
  362.7 11.4 %collective-permute-start.46 = (bf16[2,2,264,512]{3,2,0,1:T(8,128)(2,1)S(1)}, bf16[2,2,264,512]{3,2,0,1:T(8,128)(2,1)S(1)}, u32[]{:S(2)}, u32[]{:S(2)}) collective-permute-start(bf16[2,2,264,512]{3,2,0,1:T(8,128)(2,1)S(1)} %maximum_select_fusion.1), channel_id=1, source_target_pairs={{0,8},{8,0},{1,9},{9,1},{2,10},{10,2},{3,11},{11,3},{4,12},{12,4},... | collective-permute-start | bytes 3244040 | tf_op jit(solution)/shard_map/ppermute | solution.py:28
  362.7 11.3 %collective-permute-start.47 = (bf16[512,512]{1,0:T(8,128)(2,1)}, bf16[512,512]{1,0:T(8,128)(2,1)S(1)}, u32[]{:S(2)}, u32[]{:S(2)}) collective-permute-start(bf16[512,512]{1,0:T(8,128)(2,1)} %maximum_select_fusion.10), channel_id=1, source_target_pairs={{0,0},{1,8},{2,2},{3,10},{8,1},{9,9},{10,3},{11,11},{4,4},{5,12},{... | collective-permute-start | bytes 1572872 | tf_op jit(solution)/shard_map/ppermute | solution.py:82
  364.4 9.6 %collective-permute-start.45 = (bf16[2,128,512]{2,1,0:T(8,128)(2,1)S(1)}, bf16[2,128,512]{2,1,0:T(8,128)(2,1)S(1)}, u32[]{:S(2)}, u32[]{:S(2)}) collective-permute-start(bf16[2,128,512]{2,1,0:T(8,128)(2,1)S(1)} %pad_maximum_fusion.9), channel_id=1, source_target_pairs={{0,16},{16,0},{1,17},{17,1},{2,18},{18,2},{3,19},{19,3},{4,20},{20... | collective-permute-start | bytes 786440 | tf_op jit(solution)/shard_map/ppermute | solution.py:28
  (68 other events, 509.9 us)
Sparse Core Ops, SparseCore 0:
  64.9 74.9 all-gather.2
  207.0 119.4 reduce-scatter.1
